TPU v7x, 32 devices: a whole 2x2x4 slice. The times are simulated.
32 devices in a mesh: src: 4 (over z), xl: 8 (over y, x, core).
Axes of the slice: x: 2, y: 2, z: 4, core: 2. Of those that a mesh axis runs over, the one named last changes fastest.
Arguments:
- src_traces: float32 [64, 256, 1024], P('src', 'xl'), may hold values from -6 to 6
- rec_traces: float32 [256, 64, 1024], P('xl', 'src'), may hold values from -6 to 6
Outputs:
- multiples: float32 [64, 64, 256], P('src', 'xl')
All inputs are finite; a program needn't handle non-finite values.
Results may differ from a plain program's by a relative error of at most 0.004.
Values may be sent and summed in bfloat16 or wider, within the bound.
No kernel may reach another device: no remote copies, remote signals or barrier semaphores. Data moves between devices by JAX's collectives and lax.ppermute only.
A program may use at most 64 MiB of HBM per device.

v0:
```python
import math

import jax
import jax.numpy as jnp
from jax import lax
from jax.sharding import PartitionSpec as P

F = 128
FBASE = 4


def from_behind(value, axis, steps):
    count = lax.axis_size(axis)
    pairs = [(source, (source + steps) % count) for source in range(count)]
    return lax.ppermute(value, axis, pairs)


def fourier_table(samples):
    times = jnp.arange(samples, dtype=jnp.int32)
    freq_bins = FBASE + jnp.arange(F, dtype=jnp.int32)
    phases = times[:, None] * freq_bins[None, :] % samples
    angles = phases.astype(jnp.float32) * jnp.float32(2.0 * math.pi / samples)
    basis = jnp.concatenate([jnp.cos(angles), -jnp.sin(angles)], axis=1)
    return basis / jnp.float32(math.sqrt(samples))


def spectra(traces):
    samples = traces.shape[-1]
    flat_rows = traces.reshape(-1, samples)
    result = jnp.dot(
        flat_rows,
        fourier_table(samples),
        precision=lax.Precision.HIGHEST,
        preferred_element_type=jnp.float32,
    )
    return result.reshape(traces.shape[:-1] + (2 * F,)).astype(jnp.bfloat16)


def spectral_product(left, right, layout_kind):
    left_re = left[..., :F]
    left_im = left[..., F:]
    right_re = right[..., :F]
    right_im = right[..., F:]
    real_part = jnp.einsum(
        layout_kind, left_re, right_re, preferred_element_type=jnp.float32
    ) - jnp.einsum(layout_kind, left_im, right_im, preferred_element_type=jnp.float32)
    imag_part = jnp.einsum(
        layout_kind, left_re, right_im, preferred_element_type=jnp.float32
    ) + jnp.einsum(layout_kind, left_im, right_re, preferred_element_type=jnp.float32)
    return jnp.concatenate([real_part, imag_part], axis=-1)


def per_device(src_traces, rec_traces):
    shot_source = spectra(src_traces)
    own_panels = spectra(rec_traces)
    members = lax.axis_size("xl")
    weighting_factor = jnp.float32(1.0 / math.sqrt(shot_source.shape[1] * members))
    panels = lax.all_gather(own_panels, "src", axis=1, tiled=True)
    panel_block_width = panels.shape[1] // members
    position = lax.axis_index("xl")

    def block_term(block):
        slice_portion = lax.dynamic_slice_in_dim(
            panels, block * panel_block_width, panel_block_width, 1
        )
        return spectral_product(shot_source, slice_portion, "ltu,teu->leu") * weighting_factor

    start_offset = block_term((position + members - 1) % members)

    def advance(section, carried):
        moved = from_behind(carried, "xl", 1)
        block = (position - section + members - 1) % members
        return moved + block_term(block)

    result = lax.fori_loop(1, members, advance, start_offset)
    return result


def solution(mesh):
    return jax.shard_map(
        per_device,
        mesh=mesh,
        in_specs=(P("src", "xl", None), P("xl", "src", None)),
        out_specs=P("src", "xl", None),
        check_vma=False,
    )
```

profile of v0, /device:TPU:0, one launch (start us, length us, event | category | flops | bytes accessed | tf_op | source)
XLA Modules:
  0.0 196.6 jit_solution(6396907180168672665)
XLA Ops:
  6.5 2.1 %fusion.39 = (f32[1024,128]{1,0:T(8,128)S(1)}, f32[1024,128]{1,0:T(8,128)S(1)}) fusion(s32[128]{0:T(128)S(1)} %iota_add_fusion), kind=kLoop, calls=%fused_computation.51 | loop fusion | flops 1966080 | bytes 1049088 | tf_op jit(solution)/shard_map/cos | solution.py:23
  8.6 4.3 %fusion.19 = bf16[512,256]{0,1:T(8,128)(2,1)} fusion(f32[512,1024]{1,0:T(8,128)S(1)} %bitcast.42, f32[1024,128]{1,0:T(8,128)S(1)} %get-tuple-element.199, f32[1024,128]{1,0:T(8,128)S(1)} %get-tuple-element.198), kind=kOutput, calls=%fused_computation.26 | convolution fusion | flops 1611268096 | bytes 3407872 | tf_op jit(solution)/shard_map/dot_general | solution.py:30
  14.0 2.0 %copy.15 = bf16[32,16,256]{0,1,2:T(8,128)(2,1)} copy(bf16[32,16,256]{2,1,0:T(8,128)(2,1)S(1)} %bitcast.44) | data formatting | bytes 524288 | tf_op jit(solution)/shard_map/convert_element_type | solution.py:36
  16.1 5.2 %fusion.20 = bf16[512,256]{0,1:T(8,128)(2,1)S(1)} fusion(f32[512,1024]{1,0:T(8,128)} %bitcast.43, f32[1024,128]{1,0:T(8,128)S(1)} %get-tuple-element.199, f32[1024,128]{1,0:T(8,128)S(1)} %get-tuple-element.198), kind=kOutput, calls=%fused_computation.27 | convolution fusion | flops 1611268096 | bytes 3407872 | tf_op jit(solution)/shard_map/dot_general | solution.py:30
  21.4 1.8 copy.17
  23.3 76.2 %all-gather.2.cloned.1.call-done = bf16[32,64,256]{0,1,2:T(8,128)(2,1)} async-done(((bf16[32,16,256]{0,1,2:T(8,128)(2,1)}), bf16[32,64,256]{0,1,2:T(8,128)(2,1)}) %all-gather.2.cloned.1.call-update) | async-done | bytes 1048592 | tf_op jit(solution)/shard_map/all_gather | solution.py:58
  103.1 1.4 fusion.17
  108.5 1.4 fusion.18
  110.1 79.0 %while.17 = (s32[]{:T(128)}, f32[16,8,256]{2,1,0:T(8,128)S(1)}, s32[]{:T(128)}, bf16[32,64,256]{0,1,2:T(8,128)(2,1)}, bf16[16,32,256]{1,0,2:T(8,128)(2,1)}, /*in...) while((s32[]{:T(128)}, f32[16,8,256]{2,1,0:T(8,128)S(1)}, s32[]{:T(128)}, ...), condition=%wide.region_1.2_spmd, body=%wide.region_0.1_spmd.sunk | while | flops 4325395 | bytes 5243216 | solution.py:75
  117.4 1.4 fusion.122
  118.9 1.4 fusion.118
  120.8 1.6 collective-permute-start
  129.6 1.4 fusion.122
  131.0 1.4 fusion.118
  140.2 1.4 fusion.122
  141.7 1.4 fusion.118
  143.6 1.6 collective-permute-start
  152.4 1.4 fusion.122
  153.8 1.4 fusion.118
  163.0 1.4 fusion.122
  164.4 1.4 fusion.118
  166.3 1.6 collective-permute-start
  175.1 1.4 fusion.122
  185.8 1.4 fusion.122
  (94 shorter events, 66.2 us)
Async XLA Ops:
  6.5 2.1 %copy-start = (f32[32,16,1024]{2,1,0:T(8,128)S(1)}, f32[32,16,1024]{2,1,0:T(8,128)}, u32[]{:S(2)}) copy-start(f32[32,16,1024]{2,1,0:T(8,128)} %param.5) | copy-start | bytes 6291460
  6.5 92.9 %all-gather.2.cloned.1.call-start = ((), (), s32[]{:S(2)}) async-start(), calls=%async_computation | async-start | bytes 5242880 | tf_op jit(solution)/shard_map/all_gather | solution.py:58
  110.1 10.6 %collective-permute-start = (f32[16,8,256]{2,1,0:T(8,128)S(1)}, f32[16,8,256]{2,1,0:T(8,128)S(1)}, u32[]{:S(2)}, u32[]{:S(2)}) collective-permute-start(f32[16,8,256]{2,1,0:T(8,128)S(1)} %get-tuple-element.242), channel_id=1, source_target_pairs={{0,1},{1,2},{2,3},{3,4},{4,5},{5,6},{6,7},{7,0},{8,9},{9,10},{10,1... | collective-permute-start | bytes 393224 | tf_op jit(solution)/shard_map/while/body/eval_jaxpr/ppermute | solution.py:15
  120.8 12.1 %collective-permute-start = (f32[16,8,256]{2,1,0:T(8,128)S(1)}, f32[16,8,256]{2,1,0:T(8,128)S(1)}, u32[]{:S(2)}, u32[]{:S(2)}) collective-permute-start(f32[16,8,256]{2,1,0:T(8,128)S(1)} %get-tuple-element.242), channel_id=1, source_target_pairs={{0,1},{1,2},{2,3},{3,4},{4,5},{5,6},{6,7},{7,0},{8,9},{9,10},{10,1... | collective-permute-start | bytes 393224 | tf_op jit(solution)/shard_map/while/body/eval_jaxpr/ppermute | solution.py:15
  132.9 10.6 %collective-permute-start = (f32[16,8,256]{2,1,0:T(8,128)S(1)}, f32[16,8,256]{2,1,0:T(8,128)S(1)}, u32[]{:S(2)}, u32[]{:S(2)}) collective-permute-start(f32[16,8,256]{2,1,0:T(8,128)S(1)} %get-tuple-element.242), channel_id=1, source_target_pairs={{0,1},{1,2},{2,3},{3,4},{4,5},{5,6},{6,7},{7,0},{8,9},{9,10},{10,1... | collective-permute-start | bytes 393224 | tf_op jit(solution)/shard_map/while/body/eval_jaxpr/ppermute | solution.py:15
  143.6 12.1 %collective-permute-start = (f32[16,8,256]{2,1,0:T(8,128)S(1)}, f32[16,8,256]{2,1,0:T(8,128)S(1)}, u32[]{:S(2)}, u32[]{:S(2)}) collective-permute-start(f32[16,8,256]{2,1,0:T(8,128)S(1)} %get-tuple-element.242), channel_id=1, source_target_pairs={{0,1},{1,2},{2,3},{3,4},{4,5},{5,6},{6,7},{7,0},{8,9},{9,10},{10,1... | collective-permute-start | bytes 393224 | tf_op jit(solution)/shard_map/while/body/eval_jaxpr/ppermute | solution.py:15
  155.7 10.6 %collective-permute-start = (f32[16,8,256]{2,1,0:T(8,128)S(1)}, f32[16,8,256]{2,1,0:T(8,128)S(1)}, u32[]{:S(2)}, u32[]{:S(2)}) collective-permute-start(f32[16,8,256]{2,1,0:T(8,128)S(1)} %get-tuple-element.242), channel_id=1, source_target_pairs={{0,1},{1,2},{2,3},{3,4},{4,5},{5,6},{6,7},{7,0},{8,9},{9,10},{10,1... | collective-permute-start | bytes 393224 | tf_op jit(solution)/shard_map/while/body/eval_jaxpr/ppermute | solution.py:15
  166.3 12.1 %collective-permute-start = (f32[16,8,256]{2,1,0:T(8,128)S(1)}, f32[16,8,256]{2,1,0:T(8,128)S(1)}, u32[]{:S(2)}, u32[]{:S(2)}) collective-permute-start(f32[16,8,256]{2,1,0:T(8,128)S(1)} %get-tuple-element.242), channel_id=1, source_target_pairs={{0,1},{1,2},{2,3},{3,4},{4,5},{5,6},{6,7},{7,0},{8,9},{9,10},{10,1... | collective-permute-start | bytes 393224 | tf_op jit(solution)/shard_map/while/body/eval_jaxpr/ppermute | solution.py:15
  178.5 10.6 %collective-permute-start = (f32[16,8,256]{2,1,0:T(8,128)S(1)}, f32[16,8,256]{2,1,0:T(8,128)S(1)}, u32[]{:S(2)}, u32[]{:S(2)}) collective-permute-start(f32[16,8,256]{2,1,0:T(8,128)S(1)} %get-tuple-element.242), channel_id=1, source_target_pairs={{0,1},{1,2},{2,3},{3,4},{4,5},{5,6},{6,7},{7,0},{8,9},{9,10},{10,1... | collective-permute-start | bytes 393224 | tf_op jit(solution)/shard_map/while/body/eval_jaxpr/ppermute | solution.py:15
  189.1 0.7 copy-start.1
Sparse Core Ops, SparseCore 0:
  16.2 83.2 all-gather.1
where the time goes:
time: 200 us; the launch traced here: 197 us
  waiting for transfers between devices  76.3 us (38%)
  matrix products  55.2 us (28%)
  local copies, waits for them, and re-layouts  43.8 us (22%)
  between operations  13.5 us (7%)
  starting transfers between devices  5.13 us (3%)
  other arithmetic  2.23 us (1%)
    all_gather x1, waiting for transfers between devices, per_device(): panels = lax.all_gather(own_panels, 'src', axis=1, tiled=True)  76.2 us
    dot_general x8, matrix products, spectral_product(): jnp.einsum(layout_kind, left_im, right_im, preferred_element_type=jnp.flo...  11.5 us
    dot_general x8, matrix products, spectral_product(): jnp.einsum(layout_kind, left_im, right_re, preferred_element_type=jnp.flo...  11.4 us
    dot_general x8, matrix products, spectral_product(): jnp.einsum(layout_kind, left_re, right_im, preferred_element_type=jnp.flo...  11.4 us
    dot_general x8, matrix products, spectral_product(): jnp.einsum(layout_kind, left_re, right_re, preferred_element_type=jnp.flo...  11.4 us
    dot_general x2, matrix products, spectra(): jnp.dot(flat_rows, fourier_table(samples), precision=lax.Precision.HIGHES...  9.51 us
    dot_general x8, local copies, waits for them, and re-layouts, spectral_product(): jnp.einsum(layout_kind, left_re, right_im, preferred_element_type=jnp.flo...  8.68 us
    dot_general x8, local copies, waits for them, and re-layouts, spectral_product(): jnp.einsum(layout_kind, left_im, right_re, preferred_element_type=jnp.flo...  8.67 us
  transfers between devices with their start and end apart: 8, of which 1 were waited for; matrix products, arithmetic and copies ran while one was open for 41% of the time, Pallas kernels for 0%

commit v1 on v0

v1 whole, which is shorter than its diff:
```python
import functools
import math

import jax
import jax.numpy as jnp
import ml_dtypes
import numpy as np
from jax import lax
from jax.experimental import pallas as pl
from jax.experimental.pallas import tpu as pltpu
from jax.sharding import PartitionSpec as P

F = 128
FBASE = 4
PIECES = 2
VMEM = 40 << 20


def fourier_table(samples):
    times = np.arange(samples)[:, None]
    phases = times * (FBASE + np.arange(F))[None, :] % samples
    angles = phases * (2.0 * math.pi / samples)
    basis = np.concatenate([np.cos(angles), -np.sin(angles)], axis=1)
    basis = (basis / math.sqrt(samples)).astype(np.float32)
    high = basis.astype(ml_dtypes.bfloat16)
    low = (basis - high.astype(np.float32)).astype(ml_dtypes.bfloat16)
    return jnp.asarray(high), jnp.asarray(low)


def spectra_kernel(traces_ref, high_ref, low_ref, out_ref):
    shape = out_ref.shape
    traces = traces_ref[...].reshape(-1, traces_ref.shape[-1])
    high = traces.astype(jnp.bfloat16)
    low = (traces - high.astype(jnp.float32)).astype(jnp.bfloat16)
    dot = functools.partial(jnp.dot, preferred_element_type=jnp.float32)
    total = dot(high, high_ref[...]) + (dot(high, low_ref[...]) + dot(low, high_ref[...]))
    out_ref[...] = total.astype(jnp.bfloat16).reshape(shape)


def spectra(traces, table, axis, piece, pieces):
    samples = traces.shape[2]
    block = list(traces.shape)
    block[axis] //= pieces
    steps = 1
    while block[0] * block[1] > 256 and block[1 - axis] % 2 == 0:
        block[1 - axis] //= 2
        steps *= 2
    out_shape = list(traces.shape[:2]) + [2 * F]
    out_shape[axis] //= pieces

    def traces_at(i):
        return (piece, i, 0) if axis == 0 else (i, piece, 0)

    def out_at(i):
        return (0, i, 0) if axis == 0 else (i, 0, 0)

    whole = pl.BlockSpec((samples, 2 * F), lambda i: (0, 0))
    rows = out_shape[0] * out_shape[1]
    return pl.pallas_call(
        spectra_kernel,
        grid=(steps,),
        in_specs=[pl.BlockSpec(tuple(block), traces_at), whole, whole],
        out_specs=pl.BlockSpec((block[0], block[1], 2 * F), out_at),
        out_shape=jax.ShapeDtypeStruct(tuple(out_shape), jnp.bfloat16),
        compiler_params=pltpu.CompilerParams(vmem_limit_bytes=VMEM),
        cost_estimate=pl.CostEstimate(
            flops=6 * rows * samples * 2 * F, bytes_accessed=4 * rows * samples, transcendentals=0
        ),
    )(traces, *table)


def split_left(ref, forms, points):
    value = ref[...].astype(jnp.float32).reshape(-1, 2 * F)
    re, im = value[:, :F], value[:, F:]
    forms[0], forms[1], forms[2] = re + im, re, im


def split_right(ref, forms):
    value = ref[...].astype(jnp.float32).reshape(-1, 2 * F)
    re, im = value[:, :F], value[:, F:]
    forms[0], forms[1], forms[2] = re, im - re, re + im


def product_tile(left, right, sources, points, width, starts, emit, start_from):
    many = 4

    def some_sources(block, carry):
        def some_points(step, sums):
            sums = list(sums)
            for inner in range(8):
                point = step * 8 + inner
                rights = [
                    [right[k, pl.ds(pl.multiple_of(point * width + at, 8), 8), :] for at in starts] for k in range(3)
                ]
                for s in range(many):
                    row = (block * many + s) * points + point
                    for k in range(3):
                        one = left[k, pl.ds(row, 1), :]
                        for g in range(len(starts)):
                            i = (s * len(starts) + g) * 3 + k
                            sums[i] = sums[i] + one * rights[k][g]
            return tuple(sums)

        zero = jnp.zeros((8, F), jnp.float32)
        sums = lax.fori_loop(0, points // 8, some_points, (zero,) * (many * len(starts) * 3))
        for s in range(many):
            for g in range(len(starts)):
                first, second, third = sums[(s * len(starts) + g) * 3 :][:3]
                emit(block * many + s, g, first - third, first + second)
        return carry

    lax.fori_loop(0, sources // many, some_sources, 0)


def tiles_kernel(core_ref, *refs, lefts, rights, tiles, carried, last):
    refs = list(refs)
    left_refs = [refs.pop(0) for _ in range(lefts)]
    right_refs = [refs.pop(0) for _ in range(rights)]
    before = refs.pop(0) if carried else None
    outs = [refs.pop(0) for _ in range(2 if last else 1)]
    left_forms, right_forms = refs
    sources, points, _ = left_refs[0].shape
    width = right_refs[0].shape[1]
    for i, ref in enumerate(left_refs):
        split_left(ref, left_forms.at[i], points)
    for i, ref in enumerate(right_refs):
        split_right(ref, right_forms.at[i])
    core = core_ref[0]
    starts = [core * 8, (1 - core) * 8]
    for tile, (left, right) in enumerate(tiles):

        def emit(source, group, re, im, tile=tile):
            if before is not None:
                re = re + before[tile, group, source, :, :F]
                im = im + before[tile, group, source, :, F:]
            if last:
                out = outs[group].at[tile, source]
                out[:, :F] = re.astype(out.dtype)
                out[:, F:] = im.astype(out.dtype)
            else:
                outs[0][tile, group, source, :, :F] = re
                outs[0][tile, group, source, :, F:] = im

        product_tile(left_forms.at[left], right_forms.at[right], sources, points, width, starts, emit, None)


def tiles_of(core, lefts, rights, tiles, before=None, last=False):
    sources, points, _ = lefts[0].shape
    width = rights[0].shape[1]
    count = len(tiles)
    if last:
        out_shape = (
            jax.ShapeDtypeStruct((count, sources, 8, 2 * F), jnp.float32),
            jax.ShapeDtypeStruct((count, sources, 8, 2 * F), jnp.bfloat16),
        )
    else:
        out_shape = jax.ShapeDtypeStruct((count, 2, sources, 8, 2 * F), jnp.float32)
    operands = list(lefts) + list(rights) + ([] if before is None else [before])
    vmem = pl.BlockSpec(memory_space=pltpu.VMEM)
    return pl.pallas_call(
        functools.partial(
            tiles_kernel, lefts=len(lefts), rights=len(rights), tiles=tiles, carried=before is not None, last=last
        ),
        in_specs=[pl.BlockSpec(memory_space=pltpu.SMEM)] + [vmem] * len(operands),
        out_specs=(vmem, vmem) if last else vmem,
        out_shape=out_shape,
        scratch_shapes=[
            pltpu.VMEM((len(lefts), 3, sources * points, F), jnp.float32),
            pltpu.VMEM((len(rights), 3, points * width, F), jnp.float32),
        ],
        compiler_params=pltpu.CompilerParams(vmem_limit_bytes=VMEM),
        cost_estimate=pl.CostEstimate(
            flops=32 * count * sources * width * points * F, bytes_accessed=1 << 20, transcendentals=0
        ),
    )(core, *operands)


def slots_kernel(turn_ref, keep_a, keep_b, came_a, came_b, *refs):
    outs, sums = refs[:4], refs[4]
    sums[0:1] = (keep_a[...] + came_a[...].astype(jnp.float32)).astype(sums.dtype)
    sums[1:4] = (keep_b[...] + came_b[...].astype(jnp.float32)).astype(sums.dtype)
    for t, out in enumerate(outs):
        out[...] = sums[turn_ref[0] ^ t]


def slots_of(turn, keep_a, keep_b, came_a, came_b):
    shape = keep_a.shape[1:]
    vmem = pl.BlockSpec(memory_space=pltpu.VMEM)
    return pl.pallas_call(
        slots_kernel,
        in_specs=[pl.BlockSpec(memory_space=pltpu.SMEM)] + [vmem] * 4,
        out_specs=(vmem,) * 4,
        out_shape=(jax.ShapeDtypeStruct(shape, jnp.bfloat16),) * 4,
        scratch_shapes=[pltpu.VMEM((4,) + shape, jnp.bfloat16)],
        compiler_params=pltpu.CompilerParams(vmem_limit_bytes=VMEM),
    )(turn, keep_a, keep_b, came_a, came_b)


def block_kernel(left_ref, right_ref, out_ref, left_forms, right_forms):
    sources, points, _ = left_ref.shape

    @pl.when(pl.program_id(0) == 0)
    def _():
        split_left(left_ref, left_forms, points)

    split_right(right_ref, right_forms)

    def emit(source, group, re, im):
        out_ref[source, :, :F] = re
        out_ref[source, :, F:] = im

    product_tile(left_forms, right_forms, sources, points, 8, [0], emit, None)


def blocks_of(left, right):
    sources, points, _ = left.shape
    receivers = right.shape[1]
    return pl.pallas_call(
        block_kernel,
        grid=(receivers // 8,),
        in_specs=[
            pl.BlockSpec((sources, points, 2 * F), lambda i: (0, 0, 0)),
            pl.BlockSpec((points, 8, 2 * F), lambda i: (0, i, 0)),
        ],
        out_specs=pl.BlockSpec((sources, 8, 2 * F), lambda i: (0, i, 0)),
        out_shape=jax.ShapeDtypeStruct((sources, receivers, 2 * F), jnp.float32),
        scratch_shapes=[
            pltpu.VMEM((3, sources * points, F), jnp.float32),
            pltpu.VMEM((3, points * 8, F), jnp.float32),
        ],
        compiler_params=pltpu.CompilerParams(vmem_limit_bytes=VMEM),
    )(left, right)


def gather_and_scatter(src_traces, rec_traces, weight):
    table = fourier_table(src_traces.shape[2])
    left = spectra(src_traces, table, 1, 0, 1)
    right = lax.all_gather(spectra(rec_traces, table, 0, 0, 1), "src", axis=1, tiled=True)
    return lax.psum_scatter(blocks_of(left, right), "xl", scatter_dimension=1, tiled=True) * weight


def swap(value, axis, flip):
    count = lax.axis_size(axis)
    return lax.ppermute(value, axis, [(i, i ^ flip) for i in range(count)])


def deliver(value, t):
    members = lax.axis_size("xl")
    pairs = []
    for z in range(lax.axis_size("src")):
        for chip in range(members // 2):
            tile = z ^ chip ^ t
            for core in range(2):
                target = (z ^ (tile & 1)) * members + (z ^ (tile & 2)) * 2 + core
                pairs.append((z * members + chip * 2 + core, target))
    return lax.ppermute(value, ("src", "xl"), pairs)


def four_planes(src_traces, rec_traces, weight):
    table = fourier_table(src_traces.shape[2])
    z, member = lax.axis_index("src"), lax.axis_index("xl")
    core = (member % 2).reshape(1).astype(jnp.int32)
    turn = (z ^ (member // 2)).reshape(1).astype(jnp.int32)
    left, right, left_far, right_far = [], [], [], []
    for piece in range(PIECES):
        right.append(spectra(rec_traces, table, 0, piece, PIECES))
        right_far.append(swap(right[-1], "src", 2))
        left.append(spectra(src_traces, table, 1, piece, PIECES))
        left_far.append(swap(left[-1], "src", 1))
    sums = None
    for piece in range(PIECES):
        sums = tiles_of(core, [left[piece]], [right[piece]], [(0, 0)], sums, piece == PIECES - 1)
    keep_a, send_a = sums
    came_a = swap(send_a, "xl", 1)
    sums = None
    for piece in range(PIECES):
        sums = tiles_of(
            core,
            [left[piece], left_far[piece]],
            [right[piece], right_far[piece]],
            [(1, 0), (0, 1), (1, 1)],
            sums,
            piece == PIECES - 1,
        )
    keep_b, send_b = sums
    came_b = swap(send_b, "xl", 1)
    slots = slots_of(turn, keep_a, keep_b, came_a, came_b)
    total = None
    for t in (2, 3, 0, 1):
        part = deliver(slots[t], t).astype(jnp.float32)
        total = part if total is None else total + part
    return total * weight


def per_device(src_traces, rec_traces):
    planes, members = lax.axis_size("src"), lax.axis_size("xl")
    weight = jnp.float32(1.0 / math.sqrt(src_traces.shape[1] * members))
    if planes == 4 and members == 8 and rec_traces.shape[1] == 16:
        return four_planes(src_traces, rec_traces, weight)
    return gather_and_scatter(src_traces, rec_traces, weight)


def solution(mesh):
    return jax.shard_map(
        per_device,
        mesh=mesh,
        in_specs=(P("src", "xl", None), P("xl", "src", None)),
        out_specs=P("src", "xl", None),
        check_vma=False,
    )
```

time: 200 us -> 38.2 us (0.19)
  the two profiles are of different devices: /device:TPU:0 before, /device:TPU:22 now
where the time goes in v1:
time: 38.2 us; the launch traced here: 37.9 us
  starting transfers between devices  13.3 us (35%)
  waiting for transfers between devices  13.2 us (35%)
  Pallas kernels  6.94 us (18%)
  local copies, waits for them, and re-layouts  3.69 us (10%)
  other arithmetic  0.7 us (2%)
    ppermute x6, waiting for transfers between devices, swap(): return lax.ppermute(value, axis, [(i, i ^ flip) for i in range(count)])  8.93 us
    ppermute x4, starting transfers between devices, deliver(): return lax.ppermute(value, ('src', 'xl'), pairs)  7.43 us
    ppermute x6, starting transfers between devices, swap(): return lax.ppermute(value, axis, [(i, i ^ flip) for i in range(count)])  5.84 us
    pallas_call x4, Pallas kernels, tiles_of(): pl.pallas_call(functools.partial(tiles_kernel, lefts=len(lefts), rights=l...  4.56 us
    ppermute x4, waiting for transfers between devices, deliver(): return lax.ppermute(value, ('src', 'xl'), pairs)  4.24 us
    unnamed x12, local copies, waits for them, and re-layouts  3.69 us
    pallas_call x4, Pallas kernels, spectra(): pl.pallas_call(spectra_kernel, grid=(steps,), in_specs=[pl.BlockSpec(tupl...  2.3 us
  transfers between devices with their start and end apart: 10, of which 6 were waited for; matrix products, arithmetic and copies ran while one was open for 0% of the time, Pallas kernels for 12%

profile of v1, /device:TPU:22, one launch (start us, length us, event | category | flops | bytes accessed | tf_op | source)
XLA Modules:
  0.0 37.9 jit_solution(6160715317934395514)
XLA Ops:
  0.0 1.0 %copy-done = bf16[1024,256]{1,0:T(8,128)(2,1)S(1)} copy-done((bf16[1024,256]{1,0:T(8,128)(2,1)S(1)}, bf16[1024,256]{1,0:T(8,128)(2,1)}, u32[]{:S(2)}) %copy-start) | copy-done | bytes 524312
  1.0 1.0 %copy-done.2 = bf16[1024,256]{1,0:T(8,128)(2,1)S(1)} copy-done((bf16[1024,256]{1,0:T(8,128)(2,1)S(1)}, bf16[1024,256]{1,0:T(8,128)(2,1)}, u32[]{:S(2)}) %copy-start.2) | copy-done | bytes 524312
  2.1 1.6 %copy-done.4 = f32[32,16,1024]{2,1,0:T(8,128)S(1)} copy-done((f32[32,16,1024]{2,1,0:T(8,128)S(1)}, f32[32,16,1024]{2,1,0:T(8,128)}, u32[]{:S(2)}) %copy-start.4) | copy-done | bytes 2097176
  3.7 0.6 %shard_map.47.refs_1_.refs_2_ = bf16[16,16,256]{2,1,0:T(8,128)(2,1)S(1)} custom-call(f32[32,16,1024]{2,1,0:T(8,128)S(1)} %copy-done.4, bf16[1024,256]{1,0:T(8,128)(2,1)S(1)} %copy-done.2, bf16[1024,256]{1,0:T(8,128)(2,1)S(1)} %copy-done), custom_call_target="tpu_custom_call" | custom-call | flops 402653184 | bytes 1048576 | tf_op jit(solution)/shard_map/pallas_call | solution.py:59
  4.3 0.4 %collective-permute-start.1 = (bf16[16,16,256]{2,1,0:T(8,128)(2,1)S(1)}, bf16[16,16,256]{2,1,0:T(8,128)(2,1)S(1)}, u32[]{:S(2)}, u32[]{:S(2)}) collective-permute-start(bf16[16,16,256]{2,1,0:T(8,128)(2,1)S(1)} %shard_map.47.refs_1_.refs_2_), channel_id=1, source_target_pairs={{0,16},{8,24},{16,0},{24,8},{1,17},{9,25},{17,1},{25,9},{2,18},{10... | collective-permute-start | bytes 393224 | tf_op jit(solution)/shard_map/ppermute | solution.py:244
  4.7 0.6 %shard_map.49.refs_1_.refs_2_ = bf16[16,16,256]{2,1,0:T(8,128)(2,1)S(1)} custom-call(f32[32,16,1024]{2,1,0:T(8,128)S(1)} %copy-done.4, bf16[1024,256]{1,0:T(8,128)(2,1)S(1)} %copy-done.2, bf16[1024,256]{1,0:T(8,128)(2,1)S(1)} %copy-done), custom_call_target="tpu_custom_call" | custom-call | flops 402653184 | bytes 1048576 | tf_op jit(solution)/shard_map/pallas_call | solution.py:59
  5.3 2.7 %collective-permute-start.3 = (bf16[16,16,256]{2,1,0:T(8,128)(2,1)S(1)}, bf16[16,16,256]{2,1,0:T(8,128)(2,1)S(1)}, u32[]{:S(2)}, u32[]{:S(2)}) collective-permute-start(bf16[16,16,256]{2,1,0:T(8,128)(2,1)S(1)} %shard_map.49.refs_1_.refs_2_), channel_id=1, source_target_pairs={{0,16},{8,24},{16,0},{24,8},{1,17},{9,25},{17,1},{25,9},{2,18},{10... | collective-permute-start | bytes 393224 | tf_op jit(solution)/shard_map/ppermute | solution.py:244
  7.9 0.6 %shard_map.48.refs_0_ = bf16[16,16,256]{2,1,0:T(8,128)(2,1)S(1)} custom-call(f32[16,32,1024]{2,1,0:T(8,128)S(1)} %copy-done.5, bf16[1024,256]{1,0:T(8,128)(2,1)S(1)} %copy-done.3, bf16[1024,256]{1,0:T(8,128)(2,1)S(1)} %copy-done.1), custom_call_target="tpu_custom_call" | custom-call | flops 402653184 | bytes 1048576 | tf_op jit(solution)/shard_map/pallas_call | solution.py:59
  8.5 1.6 %collective-permute-start.2 = (bf16[16,16,256]{2,1,0:T(8,128)(2,1)S(1)}, bf16[16,16,256]{2,1,0:T(8,128)(2,1)S(1)}, u32[]{:S(2)}, u32[]{:S(2)}) collective-permute-start(bf16[16,16,256]{2,1,0:T(8,128)(2,1)S(1)} %shard_map.48.refs_0_), channel_id=1, source_target_pairs={{0,8},{8,0},{16,24},{24,16},{1,9},{9,1},{17,25},{25,17},{2,10},{10... | collective-permute-start | bytes 393224 | tf_op jit(solution)/shard_map/ppermute | solution.py:244
  10.2 0.6 %shard_map.46.refs_0_ = bf16[16,16,256]{2,1,0:T(8,128)(2,1)S(1)} custom-call(f32[16,32,1024]{2,1,0:T(8,128)S(1)} %copy-done.5, bf16[1024,256]{1,0:T(8,128)(2,1)S(1)} %copy-done.3, bf16[1024,256]{1,0:T(8,128)(2,1)S(1)} %copy-done.1), custom_call_target="tpu_custom_call" | custom-call | flops 402653184 | bytes 1048576 | tf_op jit(solution)/shard_map/pallas_call | solution.py:59
  10.7 0.5 %collective-permute-start = (bf16[16,16,256]{2,1,0:T(8,128)(2,1)S(1)}, bf16[16,16,256]{2,1,0:T(8,128)(2,1)S(1)}, u32[]{:S(2)}, u32[]{:S(2)}) collective-permute-start(bf16[16,16,256]{2,1,0:T(8,128)(2,1)S(1)} %shard_map.46.refs_0_), channel_id=1, source_target_pairs={{0,8},{8,0},{16,24},{24,16},{1,9},{9,1},{17,25},{25,17},{2,10},{10... | collective-permute-start | bytes 393224 | tf_op jit(solution)/shard_map/ppermute | solution.py:244
  11.3 4.6 %collective-permute-done.3.refs_3_ = bf16[16,16,256]{2,1,0:T(8,128)(2,1)S(1)} collective-permute-done((bf16[16,16,256]{2,1,0:T(8,128)(2,1)S(1)}, bf16[16,16,256]{2,1,0:T(8,128)(2,1)S(1)}, u32[]{:S(2)}, u32[]{:S(2)}) %collective-permute-start.3) | collective-permute-done | bytes 131104 | tf_op jit(solution)/shard_map/ppermute | solution.py:244
  15.9 3.4 %collective-permute-done.2.refs_1_ = bf16[16,16,256]{2,1,0:T(8,128)(2,1)S(1)} collective-permute-done((bf16[16,16,256]{2,1,0:T(8,128)(2,1)S(1)}, bf16[16,16,256]{2,1,0:T(8,128)(2,1)S(1)}, u32[]{:S(2)}, u32[]{:S(2)}) %collective-permute-start.2) | collective-permute-done | bytes 131104 | tf_op jit(solution)/shard_map/ppermute | solution.py:244
  19.3 1.7 %shard_map.52.refs_4_ = f32[3,2,16,8,256]{4,3,2,1,0:T(8,128)S(1)} custom-call(s32[1]{0:T(128)} %bitcast.1.core_ref, bf16[16,16,256]{2,1,0:T(8,128)(2,1)S(1)} %shard_map.48.refs_0_, bf16[16,16,256]{2,1,0:T(8,128)(2,1)S(1)} %collective-permute-done.2.refs_1_, bf16[16,16,256]{2,1,0:T(8,128)(2,1)S(1)} %shard_map.49.refs_1_.refs_2_, ...), custom_call_target="tpu_custom_call" | custom-call | flops 50331648 | bytes 1048576 | tf_op jit(solution)/shard_map/pallas_call | solution.py:160
  21.0 1.7 %shard_map.53 = (f32[3,16,8,256]{3,2,1,0:T(8,128)S(1)}, bf16[3,16,8,256]{3,2,1,0:T(8,128)(2,1)S(1)}) custom-call(s32[1]{0:T(128)} %bitcast.1.core_ref, bf16[16,16,256]{2,1,0:T(8,128)(2,1)S(1)} %shard_map.46.refs_0_, bf16[16,16,256]{2,1,0:T(8,128)(2,1)S(1)} %collective-permute-done.refs_1_, bf16[16,16,256]{2,1,0:T(8,128)(2,1)S(1)} %shard_map.47.refs_1_.refs_2_, ...), custom_call_target="tpu_custom_call" | custom-call | flops 50331648 | bytes 1048576 | tf_op jit(solution)/shard_map/pallas_call | solution.py:160
  22.8 0.6 %shard_map.50.refs_2_ = f32[1,2,16,8,256]{4,3,2,1,0:T(8,128)S(1)} custom-call(s32[1]{0:T(128)} %bitcast.1.core_ref, bf16[16,16,256]{2,1,0:T(8,128)(2,1)S(1)} %shard_map.48.refs_0_, bf16[16,16,256]{2,1,0:T(8,128)(2,1)S(1)} %shard_map.49.refs_1_.refs_2_), custom_call_target="tpu_custom_call" | custom-call | flops 16777216 | bytes 1048576 | tf_op jit(solution)/shard_map/pallas_call | solution.py:160
  23.4 0.6 %shard_map.51 = (f32[1,16,8,256]{3,2,1,0:T(8,128)S(1)}, bf16[1,16,8,256]{3,2,1,0:T(8,128)(2,1)S(1)}) custom-call(s32[1]{0:T(128)} %bitcast.1.core_ref, bf16[16,16,256]{2,1,0:T(8,128)(2,1)S(1)} %shard_map.46.refs_0_, bf16[16,16,256]{2,1,0:T(8,128)(2,1)S(1)} %shard_map.47.refs_1_.refs_2_, f32[1,2,16,8,256]{4,3,2,1,0:T(8,128)S(1)} %shard_map.50.refs_2_), custom_call_target="tpu_custom_call" | custom-call | flops 16777216 | bytes 1048576 | tf_op jit(solution)/shard_map/pallas_call | solution.py:160
  24.0 0.6 %collective-permute-start.4 = (bf16[1,16,8,256]{3,2,1,0:T(8,128)(2,1)S(1)}, bf16[1,16,8,256]{3,2,1,0:T(8,128)(2,1)S(1)}, u32[]{:S(2)}, u32[]{:S(2)}) collective-permute-start(bf16[1,16,8,256]{3,2,1,0:T(8,128)(2,1)S(1)} %get-tuple-element.15), channel_id=1, source_target_pairs={{0,1},{1,0},{2,3},{3,2},{4,5},{5,4},{6,7},{7,6},{8,9},{9,8},{10,11... | collective-permute-start | bytes 196616 | tf_op jit(solution)/shard_map/ppermute | solution.py:244
  24.5 0.9 %collective-permute-done.4.came_a = bf16[1,16,8,256]{3,2,1,0:T(8,128)(2,1)S(1)} collective-permute-done((bf16[1,16,8,256]{3,2,1,0:T(8,128)(2,1)S(1)}, bf16[1,16,8,256]{3,2,1,0:T(8,128)(2,1)S(1)}, u32[]{:S(2)}, u32[]{:S(2)}) %collective-permute-start.4) | collective-permute-done | bytes 65568 | tf_op jit(solution)/shard_map/ppermute | solution.py:244
  25.5 2.5 %collective-permute-start.6 = (bf16[16,8,256]{2,1,0:T(8,128)(2,1)S(1)}, bf16[16,8,256]{2,1,0:T(8,128)(2,1)S(1)}, u32[]{:S(2)}, u32[]{:S(2)}) collective-permute-start(bf16[16,8,256]{2,1,0:T(8,128)(2,1)S(1)} %get-tuple-element.17), channel_id=1, source_target_pairs={{0,4},{1,5},{2,12},{3,13},{4,0},{5,1},{6,8},{7,9},{8,6},{9,7},{10,... | collective-permute-start | bytes 196616 | tf_op jit(solution)/shard_map/ppermute | solution.py:256
  28.0 4.9 %collective-permute-start.8 = (bf16[16,8,256]{2,1,0:T(8,128)(2,1)S(1)}, bf16[16,8,256]{2,1,0:T(8,128)(2,1)S(1)}, u32[]{:S(2)}, u32[]{:S(2)}) collective-permute-start(bf16[16,8,256]{2,1,0:T(8,128)(2,1)S(1)} %get-tuple-element.19), channel_id=1, source_target_pairs={{0,0},{1,1},{2,8},{3,9},{4,4},{5,5},{6,12},{7,13},{8,2},{9,3},{10,... | collective-permute-start | bytes 196616 | tf_op jit(solution)/shard_map/ppermute | solution.py:256
  33.2 2.0 %collective-permute-done.8 = bf16[16,8,256]{2,1,0:T(8,128)(2,1)S(1)} collective-permute-done((bf16[16,8,256]{2,1,0:T(8,128)(2,1)S(1)}, bf16[16,8,256]{2,1,0:T(8,128)(2,1)S(1)}, u32[]{:S(2)}, u32[]{:S(2)}) %collective-permute-start.8) | collective-permute-done | bytes 65568 | tf_op jit(solution)/shard_map/ppermute | solution.py:256
  35.1 2.1 %collective-permute-done.9 = bf16[16,8,256]{2,1,0:T(8,128)(2,1)S(1)} collective-permute-done((bf16[16,8,256]{2,1,0:T(8,128)(2,1)S(1)}, bf16[16,8,256]{2,1,0:T(8,128)(2,1)S(1)}, u32[]{:S(2)}, u32[]{:S(2)}) %collective-permute-start.9) | collective-permute-done | bytes 65568 | tf_op jit(solution)/shard_map/ppermute | solution.py:256
  37.2 0.7 %add_multiply_fusion = f32[16,8,256]{2,1,0:T(8,128)} fusion(bf16[16,8,256]{2,1,0:T(8,128)(2,1)S(1)} %collective-permute-done.9, bf16[16,8,256]{2,1,0:T(8,128)(2,1)S(1)} %collective-permute-done.8, bf16[16,8,256]{2,1,0:T(8,128)(2,1)S(1)} %collective-permute-done.7, bf16[16,8,256]{2,1,0:T(8,128)(2,1)S(1)} %collective-permute-done.6), kind=kLoop, calls=%fused_computation | loop fusion | flops 262144 | bytes 393216 | tf_op jit(solution)/shard_map/mul | solution.py:292
  (18 shorter events, 0.4 us)
Async XLA Ops:
  0.0 1.0 %copy-start = (bf16[1024,256]{1,0:T(8,128)(2,1)S(1)}, bf16[1024,256]{1,0:T(8,128)(2,1)}, u32[]{:S(2)}) copy-start(bf16[1024,256]{1,0:T(8,128)(2,1)} %constant.39.clone.low_ref) | copy-start | bytes 1572868
  1.0 1.0 %copy-start.2 = (bf16[1024,256]{1,0:T(8,128)(2,1)S(1)}, bf16[1024,256]{1,0:T(8,128)(2,1)}, u32[]{:S(2)}) copy-start(bf16[1024,256]{1,0:T(8,128)(2,1)} %constant.38.clone.high_ref) | copy-start | bytes 1572868
  2.1 1.6 %copy-start.4 = (f32[32,16,1024]{2,1,0:T(8,128)S(1)}, f32[32,16,1024]{2,1,0:T(8,128)}, u32[]{:S(2)}) copy-start(f32[32,16,1024]{2,1,0:T(8,128)} %traces_ref.7) | copy-start | bytes 6291460
  4.3 3.7 %copy-start.1 = (bf16[1024,256]{1,0:T(8,128)(2,1)S(1)}, bf16[1024,256]{1,0:T(8,128)(2,1)}, u32[]{:S(2)}) copy-start(bf16[1024,256]{1,0:T(8,128)(2,1)} %constant.39.clone.low_ref) | copy-start | bytes 1572868
  4.3 3.7 %copy-start.3 = (bf16[1024,256]{1,0:T(8,128)(2,1)S(1)}, bf16[1024,256]{1,0:T(8,128)(2,1)}, u32[]{:S(2)}) copy-start(bf16[1024,256]{1,0:T(8,128)(2,1)} %constant.38.clone.high_ref) | copy-start | bytes 1572868
  4.3 3.7 %copy-start.5 = (f32[16,32,1024]{2,1,0:T(8,128)S(1)}, f32[16,32,1024]{2,1,0:T(8,128)}, u32[]{:S(2)}) copy-start(f32[16,32,1024]{2,1,0:T(8,128)} %traces_ref.6) | copy-start | bytes 6291460
  4.3 16.7 %collective-permute-start.1 = (bf16[16,16,256]{2,1,0:T(8,128)(2,1)S(1)}, bf16[16,16,256]{2,1,0:T(8,128)(2,1)S(1)}, u32[]{:S(2)}, u32[]{:S(2)}) collective-permute-start(bf16[16,16,256]{2,1,0:T(8,128)(2,1)S(1)} %shard_map.47.refs_1_.refs_2_), channel_id=1, source_target_pairs={{0,16},{8,24},{16,0},{24,8},{1,17},{9,25},{17,1},{25,9},{2,18},{10... | collective-permute-start | bytes 393224 | tf_op jit(solution)/shard_map/ppermute | solution.py:244
  5.3 10.6 %collective-permute-start.3 = (bf16[16,16,256]{2,1,0:T(8,128)(2,1)S(1)}, bf16[16,16,256]{2,1,0:T(8,128)(2,1)S(1)}, u32[]{:S(2)}, u32[]{:S(2)}) collective-permute-start(bf16[16,16,256]{2,1,0:T(8,128)(2,1)S(1)} %shard_map.49.refs_1_.refs_2_), channel_id=1, source_target_pairs={{0,16},{8,24},{16,0},{24,8},{1,17},{9,25},{17,1},{25,9},{2,18},{10... | collective-permute-start | bytes 393224 | tf_op jit(solution)/shard_map/ppermute | solution.py:244
  8.5 10.8 %collective-permute-start.2 = (bf16[16,16,256]{2,1,0:T(8,128)(2,1)S(1)}, bf16[16,16,256]{2,1,0:T(8,128)(2,1)S(1)}, u32[]{:S(2)}, u32[]{:S(2)}) collective-permute-start(bf16[16,16,256]{2,1,0:T(8,128)(2,1)S(1)} %shard_map.48.refs_0_), channel_id=1, source_target_pairs={{0,8},{8,0},{16,24},{24,16},{1,9},{9,1},{17,25},{25,17},{2,10},{10... | collective-permute-start | bytes 393224 | tf_op jit(solution)/shard_map/ppermute | solution.py:244
  10.7 10.2 %collective-permute-start = (bf16[16,16,256]{2,1,0:T(8,128)(2,1)S(1)}, bf16[16,16,256]{2,1,0:T(8,128)(2,1)S(1)}, u32[]{:S(2)}, u32[]{:S(2)}) collective-permute-start(bf16[16,16,256]{2,1,0:T(8,128)(2,1)S(1)} %shard_map.46.refs_0_), channel_id=1, source_target_pairs={{0,8},{8,0},{16,24},{24,16},{1,9},{9,1},{17,25},{25,17},{2,10},{10... | collective-permute-start | bytes 393224 | tf_op jit(solution)/shard_map/ppermute | solution.py:244
  22.7 2.7 %collective-permute-start.5 = (bf16[3,16,8,256]{3,2,1,0:T(8,128)(2,1)S(1)}, bf16[3,16,8,256]{3,2,1,0:T(8,128)(2,1)S(1)}, u32[]{:S(2)}, u32[]{:S(2)}) collective-permute-start(bf16[3,16,8,256]{3,2,1,0:T(8,128)(2,1)S(1)} %get-tuple-element.16), channel_id=1, source_target_pairs={{0,1},{1,0},{2,3},{3,2},{4,5},{5,4},{6,7},{7,6},{8,9},{9,8},{10,11... | collective-permute-start | bytes 589832 | tf_op jit(solution)/shard_map/ppermute | solution.py:244
  24.0 1.5 %collective-permute-start.4 = (bf16[1,16,8,256]{3,2,1,0:T(8,128)(2,1)S(1)}, bf16[1,16,8,256]{3,2,1,0:T(8,128)(2,1)S(1)}, u32[]{:S(2)}, u32[]{:S(2)}) collective-permute-start(bf16[1,16,8,256]{3,2,1,0:T(8,128)(2,1)S(1)} %get-tuple-element.15), channel_id=1, source_target_pairs={{0,1},{1,0},{2,3},{3,2},{4,5},{5,4},{6,7},{7,6},{8,9},{9,8},{10,11... | collective-permute-start | bytes 196616 | tf_op jit(solution)/shard_map/ppermute | solution.py:244
  25.5 7.4 %collective-permute-start.6 = (bf16[16,8,256]{2,1,0:T(8,128)(2,1)S(1)}, bf16[16,8,256]{2,1,0:T(8,128)(2,1)S(1)}, u32[]{:S(2)}, u32[]{:S(2)}) collective-permute-start(bf16[16,8,256]{2,1,0:T(8,128)(2,1)S(1)} %get-tuple-element.17), channel_id=1, source_target_pairs={{0,4},{1,5},{2,12},{3,13},{4,0},{5,1},{6,8},{7,9},{8,6},{9,7},{10,... | collective-permute-start | bytes 196616 | tf_op jit(solution)/shard_map/ppermute | solution.py:256
  28.0 5.2 %collective-permute-start.7 = (bf16[16,8,256]{2,1,0:T(8,128)(2,1)S(1)}, bf16[16,8,256]{2,1,0:T(8,128)(2,1)S(1)}, u32[]{:S(2)}, u32[]{:S(2)}) collective-permute-start(bf16[16,8,256]{2,1,0:T(8,128)(2,1)S(1)} %get-tuple-element.18), channel_id=1, source_target_pairs={{0,12},{1,13},{2,4},{3,5},{4,8},{5,9},{6,0},{7,1},{8,14},{9,15},{1... | collective-permute-start | bytes 196616 | tf_op jit(solution)/shard_map/ppermute | solution.py:256
  28.0 7.1 %collective-permute-start.8 = (bf16[16,8,256]{2,1,0:T(8,128)(2,1)S(1)}, bf16[16,8,256]{2,1,0:T(8,128)(2,1)S(1)}, u32[]{:S(2)}, u32[]{:S(2)}) collective-permute-start(bf16[16,8,256]{2,1,0:T(8,128)(2,1)S(1)} %get-tuple-element.19), channel_id=1, source_target_pairs={{0,0},{1,1},{2,8},{3,9},{4,4},{5,5},{6,12},{7,13},{8,2},{9,3},{10,... | collective-permute-start | bytes 196616 | tf_op jit(solution)/shard_map/ppermute | solution.py:256
  32.9 4.3 %collective-permute-start.9 = (bf16[16,8,256]{2,1,0:T(8,128)(2,1)S(1)}, bf16[16,8,256]{2,1,0:T(8,128)(2,1)S(1)}, u32[]{:S(2)}, u32[]{:S(2)}) collective-permute-start(bf16[16,8,256]{2,1,0:T(8,128)(2,1)S(1)} %get-tuple-element.20), channel_id=1, source_target_pairs={{0,8},{1,9},{2,0},{3,1},{4,12},{5,13},{6,4},{7,5},{8,10},{9,11},{1... | collective-permute-start | bytes 196616 | tf_op jit(solution)/shard_map/ppermute | solution.py:256

commit v2 on v1

v2 whole, which is shorter than its diff:
```python
import functools
import math

import jax
import jax.numpy as jnp
import ml_dtypes
import numpy as np
from jax import lax
from jax.experimental import pallas as pl
from jax.experimental.pallas import tpu as pltpu
from jax.sharding import PartitionSpec as P

F = 128
FBASE = 4
LEFTS = (16, 16)
RIGHTS = (16, 16)
VMEM = 40 << 20


def fourier_table(samples):
    times = np.arange(samples)[:, None]
    phases = times * (FBASE + np.arange(F))[None, :] % samples
    angles = phases * (2.0 * math.pi / samples)
    basis = np.concatenate([np.cos(angles), -np.sin(angles)], axis=1)
    basis = (basis / math.sqrt(samples)).astype(np.float32)
    high = basis.astype(ml_dtypes.bfloat16)
    low = (basis - high.astype(np.float32)).astype(ml_dtypes.bfloat16)
    return jnp.asarray(high), jnp.asarray(low)


def transform(traces, high_table, low_table):
    high = traces.astype(jnp.bfloat16)
    low = (traces - high.astype(jnp.float32)).astype(jnp.bfloat16)
    dot = functools.partial(jnp.dot, preferred_element_type=jnp.float32)
    return dot(high, high_table) + (dot(high, low_table) + dot(low, high_table))


def spectra_kernel(traces_ref, high_ref, low_ref, *refs):
    out_ref = refs[-1]
    traces = traces_ref[...].reshape(-1, traces_ref.shape[-1])
    total = transform(traces, high_ref[...], low_ref[...])
    out_ref[...] = total.astype(jnp.bfloat16).reshape(out_ref.shape)


def spectra(traces, table, axis, first, count, after=()):
    samples = traces.shape[2]
    points = 16 if first % 16 == 0 and count % 16 == 0 else 8
    block = list(traces.shape)
    block[axis] = points
    out_shape = list(traces.shape[:2]) + [2 * F]
    out_shape[axis] = count

    def at(start):
        return lambda i: (start + i, 0, 0) if axis == 0 else (0, start + i, 0)

    whole = pl.BlockSpec((samples, 2 * F), lambda i: (0, 0))
    rows = out_shape[0] * out_shape[1]
    return pl.pallas_call(
        spectra_kernel,
        grid=(count // points,),
        in_specs=[pl.BlockSpec(tuple(block), at(first // points)), whole, whole]
        + [pl.BlockSpec(memory_space=pl.ANY)] * len(after),
        out_specs=pl.BlockSpec((block[0], block[1], 2 * F), at(0)),
        out_shape=jax.ShapeDtypeStruct(tuple(out_shape), jnp.bfloat16),
        compiler_params=pltpu.CompilerParams(vmem_limit_bytes=VMEM),
        cost_estimate=pl.CostEstimate(
            flops=6 * rows * samples * 2 * F, bytes_accessed=4 * rows * samples, transcendentals=0
        ),
    )(traces, *table, *after)


def first_spectra_kernel(traces_ref, high_ref, low_ref, out_ref, traces, high, low, sems, *, steps):
    count = out_ref.shape[0]
    depth = traces.shape[2] // steps
    copies = []
    for step in range(steps):
        part = pl.ds(step * depth, depth)
        copies.append(
            [
                pltpu.make_async_copy(
                    traces_ref.at[pl.ds(0, count), :, part], traces.at[:, :, part], sems.at[step, 0]
                ),
                pltpu.make_async_copy(high_ref.at[part], high.at[part], sems.at[step, 1]),
                pltpu.make_async_copy(low_ref.at[part], low.at[part], sems.at[step, 2]),
            ]
        )
    for group in copies:
        for copy in group:
            copy.start()
    total = None
    for step, group in enumerate(copies):
        for copy in group:
            copy.wait()
        part = pl.ds(step * depth, depth)
        value = traces[:, :, part].reshape(-1, depth)
        term = transform(value, high[part], low[part])
        total = term if total is None else total + term
    out_ref[...] = total.astype(jnp.bfloat16).reshape(out_ref.shape)


def first_spectra(traces, table, count, steps=1):
    samples = traces.shape[2]
    operands = [pltpu.with_memory_space_constraint(one, pltpu.HBM) for one in (traces, *table)]
    return pl.pallas_call(
        functools.partial(first_spectra_kernel, steps=steps),
        in_specs=[pl.BlockSpec(memory_space=pltpu.HBM)] * 3,
        out_specs=pl.BlockSpec(memory_space=pltpu.VMEM),
        out_shape=jax.ShapeDtypeStruct((count, traces.shape[1], 2 * F), jnp.bfloat16),
        scratch_shapes=[
            pltpu.VMEM((count,) + traces.shape[1:], jnp.float32),
            pltpu.VMEM((samples, 2 * F), jnp.bfloat16),
            pltpu.VMEM((samples, 2 * F), jnp.bfloat16),
            pltpu.SemaphoreType.DMA((steps, 3)),
        ],
        compiler_params=pltpu.CompilerParams(vmem_limit_bytes=VMEM),
    )(*operands)


def split_left(ref, forms, first=0, count=None):
    value = ref[...] if count is None else ref[:, first : first + count]
    value = value.astype(jnp.float32).reshape(-1, 2 * F)
    re, im = value[:, :F], value[:, F:]
    forms[0], forms[1], forms[2] = re + im, re, im


def split_right(ref, forms):
    value = ref[...].astype(jnp.float32).reshape(-1, 2 * F)
    re, im = value[:, :F], value[:, F:]
    forms[0], forms[1], forms[2] = re, im - re, re + im


def product_tile(terms, sources, width, starts, emit):
    many = 4

    def some_sources(block, carry):
        zero = jnp.zeros((8, F), jnp.float32)
        sums = (zero,) * (many * len(starts) * 3)
        for left, length, first, right, points in terms:

            def some_points(step, sums, left=left, length=length, first=first, right=right):
                sums = list(sums)
                for inner in range(8):
                    point = step * 8 + inner
                    rights = [
                        [right[k, pl.ds(pl.multiple_of(point * width + at, 8), 8), :] for at in starts]
                        for k in range(3)
                    ]
                    for s in range(many):
                        row = (block * many + s) * length + first + point
                        for k in range(3):
                            one = left[k, pl.ds(row, 1), :]
                            for g in range(len(starts)):
                                i = (s * len(starts) + g) * 3 + k
                                sums[i] = sums[i] + one * rights[k][g]
                return tuple(sums)

            sums = lax.fori_loop(0, points // 8, some_points, sums)
        for s in range(many):
            for g in range(len(starts)):
                first, second, third = sums[(s * len(starts) + g) * 3 :][:3]
                emit(block * many + s, g, first - third, first + second)
        return carry

    lax.fori_loop(0, sources // many, some_sources, 0)


def tiles_kernel(core_ref, *refs, lefts, rights, tiles, ranges, carried, spare, last):
    refs = list(refs)
    left_refs = [refs.pop(0) for _ in range(lefts)]
    right_refs = [refs.pop(0) for _ in range(rights)]
    before = refs.pop(0) if carried else None
    del refs[:spare]
    outs = [refs.pop(0) for _ in range(2 if last else 1)]
    left_forms, right_forms = refs[:lefts], refs[lefts:]
    sources = left_refs[0].shape[0]
    width = right_refs[0].shape[1]
    for ref, forms, (origin, total) in zip(left_refs, left_forms, ranges):
        split_left(ref, forms, origin, total)
    for ref, forms in zip(right_refs, right_forms):
        split_right(ref, forms)
    core = core_ref[0]
    starts = [core * 8, (1 - core) * 8]
    for tile, pairs in enumerate(tiles):

        def emit(source, group, re, im, tile=tile):
            if before is not None:
                re = re + before[tile, group, source, :, :F]
                im = im + before[tile, group, source, :, F:]
            if last:
                out = outs[group].at[tile, source]
                out[:, :F] = re.astype(out.dtype)
                out[:, F:] = im.astype(out.dtype)
            else:
                outs[0][tile, group, source, :, :F] = re
                outs[0][tile, group, source, :, F:] = im

        terms = [
            (left_forms[i], ranges[i][1], first - ranges[i][0], right_forms[j], right_refs[j].shape[0])
            for i, j, first in pairs
        ]
        product_tile(terms, sources, width, starts, emit)


def tiles_of(core, lefts, rights, tiles, before=None, last=False, after=()):
    sources = lefts[0].shape[0]
    width = rights[0].shape[1]
    count = len(tiles)
    if last:
        out_shape = (
            jax.ShapeDtypeStruct((count, sources, 8, 2 * F), jnp.float32),
            jax.ShapeDtypeStruct((count, sources, 8, 2 * F), jnp.bfloat16),
        )
    else:
        out_shape = jax.ShapeDtypeStruct((count, 2, sources, 8, 2 * F), jnp.float32)
    operands = list(lefts) + list(rights) + ([] if before is None else [before])
    vmem = pl.BlockSpec(memory_space=pltpu.VMEM)
    points = sum(rights[j].shape[0] for terms in tiles for _, j, _ in terms)
    ranges = []
    for one in range(len(lefts)):
        used = [(first, first + rights[j].shape[0]) for terms in tiles for i, j, first in terms if i == one]
        origin = min(first for first, _ in used)
        ranges.append((origin, max(end for _, end in used) - origin))
    return pl.pallas_call(
        functools.partial(
            tiles_kernel,
            lefts=len(lefts),
            rights=len(rights),
            tiles=tiles,
            ranges=ranges,
            carried=before is not None,
            spare=len(after),
            last=last,
        ),
        in_specs=[pl.BlockSpec(memory_space=pltpu.SMEM)]
        + [vmem] * len(operands)
        + [pl.BlockSpec(memory_space=pl.ANY)] * len(after),
        out_specs=(vmem, vmem) if last else vmem,
        out_shape=out_shape,
        scratch_shapes=[pltpu.VMEM((3, sources * total, F), jnp.float32) for _, total in ranges]
        + [pltpu.VMEM((3, right.shape[0] * width, F), jnp.float32) for right in rights],
        compiler_params=pltpu.CompilerParams(vmem_limit_bytes=VMEM),
        cost_estimate=pl.CostEstimate(
            flops=32 * sources * width * points * F, bytes_accessed=1 << 20, transcendentals=0
        ),
    )(core, *operands, *after)


def slots_kernel(turn_ref, *refs):
    parts = (len(refs) - 5) // 2
    keep, came, outs, sums = refs[:parts], refs[parts : 2 * parts], refs[-5:-1], refs[-1]
    first = 0
    for own, other in zip(keep, came):
        count = own.shape[0]
        sums[first : first + count] = (own[...] + other[...].astype(jnp.float32)).astype(sums.dtype)
        first += count
    for t, out in enumerate(outs):
        out[...] = sums[turn_ref[0] ^ t]


def slots_of(turn, keep, came):
    shape = keep[0].shape[1:]
    vmem = pl.BlockSpec(memory_space=pltpu.VMEM)
    return pl.pallas_call(
        slots_kernel,
        in_specs=[pl.BlockSpec(memory_space=pltpu.SMEM)] + [vmem] * (2 * len(keep)),
        out_specs=(vmem,) * 4,
        out_shape=(jax.ShapeDtypeStruct(shape, jnp.bfloat16),) * 4,
        scratch_shapes=[pltpu.VMEM((4,) + shape, jnp.bfloat16)],
        compiler_params=pltpu.CompilerParams(vmem_limit_bytes=VMEM),
    )(turn, *keep, *came)


def block_kernel(left_ref, right_ref, out_ref, left_forms, right_forms):
    sources, points, _ = left_ref.shape

    @pl.when(pl.program_id(0) == 0)
    def _():
        split_left(left_ref, left_forms)

    split_right(right_ref, right_forms)

    def emit(source, group, re, im):
        out_ref[source, :, :F] = re
        out_ref[source, :, F:] = im

    product_tile([(left_forms, points, 0, right_forms, points)], sources, 8, [0], emit)


def blocks_of(left, right):
    sources, points, _ = left.shape
    receivers = right.shape[1]
    return pl.pallas_call(
        block_kernel,
        grid=(receivers // 8,),
        in_specs=[
            pl.BlockSpec((sources, points, 2 * F), lambda i: (0, 0, 0)),
            pl.BlockSpec((points, 8, 2 * F), lambda i: (0, i, 0)),
        ],
        out_specs=pl.BlockSpec((sources, 8, 2 * F), lambda i: (0, i, 0)),
        out_shape=jax.ShapeDtypeStruct((sources, receivers, 2 * F), jnp.float32),
        scratch_shapes=[
            pltpu.VMEM((3, sources * points, F), jnp.float32),
            pltpu.VMEM((3, points * 8, F), jnp.float32),
        ],
        compiler_params=pltpu.CompilerParams(vmem_limit_bytes=VMEM),
    )(left, right)


def gather_and_scatter(src_traces, rec_traces, weight):
    table = fourier_table(src_traces.shape[2])
    left = spectra(src_traces, table, 1, 0, src_traces.shape[1])
    right = lax.all_gather(spectra(rec_traces, table, 0, 0, rec_traces.shape[0]), "src", axis=1, tiled=True)
    return lax.psum_scatter(blocks_of(left, right), "xl", scatter_dimension=1, tiled=True) * weight


def swap(value, axis, flip):
    count = lax.axis_size(axis)
    return lax.ppermute(value, axis, [(i, i ^ flip) for i in range(count)])


def deliver(value, t):
    members = lax.axis_size("xl")
    pairs = []
    for z in range(lax.axis_size("src")):
        for chip in range(members // 2):
            tile = z ^ chip ^ t
            for core in range(2):
                target = (z ^ (tile & 1)) * members + (z ^ (tile & 2)) * 2 + core
                pairs.append((z * members + chip * 2 + core, target))
    return lax.ppermute(value, ("src", "xl"), pairs)


def four_planes(src_traces, rec_traces, weight):
    table = fourier_table(src_traces.shape[2])
    z, member = lax.axis_index("src"), lax.axis_index("xl")
    core = (member % 2).reshape(1).astype(jnp.int32)
    turn = (z ^ (member // 2)).reshape(1).astype(jnp.int32)
    right = [first_spectra(rec_traces, table, RIGHTS[0])]
    right_far = [swap(right[0], "src", 2)]
    left, left_far = [], []
    token = right[0]
    jobs = [("left", i, count) for i, count in enumerate(LEFTS)]
    jobs[1:1] = [("right", i, count) for i, count in enumerate(RIGHTS) if i]
    for side, i, count in jobs:
        sizes = LEFTS if side == "left" else RIGHTS
        token = spectra(
            src_traces if side == "left" else rec_traces,
            table,
            1 if side == "left" else 0,
            sum(sizes[:i]),
            count,
            (token,),
        )
        if side == "left":
            left.append(token)
            left_far.append(swap(token, "src", 1))
        else:
            right.append(token)
            right_far.append(swap(token, "src", 2))
    keep, send, came = [None] * 3, [None] * 3, [None] * 3
    others = range(1, len(RIGHTS))
    offsets = [sum(RIGHTS[:i]) - LEFTS[0] for i in range(len(RIGHTS))]
    all_here = [(0, 0, 0)] + [(1, i, offsets[i]) for i in others]
    keep[0], send[0] = tiles_of(core, left, right, [all_here], last=True, after=(token,))
    came[0] = swap(send[0], "xl", 1)
    part = tiles_of(core, left_far[:1], right[:1], [[(0, 0, 0)]], after=(keep[0],))
    sums = tiles_of(core, [left[0], left_far[0]], right_far[:1], [[(0, 0, 0)], [(1, 0, 0)]], after=(part, came[0]))
    keep[1], send[1] = tiles_of(core, left_far[1:], right[1:], [[(0, i - 1, offsets[i]) for i in others]], part, last=True, after=(sums,))
    came[1] = swap(send[1], "xl", 1)
    after = keep[1]
    for i in others:
        done = i == len(RIGHTS) - 1
        there = [[(side, 0, offsets[i])] for side in range(2)]
        sums = tiles_of(core, [left[1], left_far[1]], right_far[i : i + 1], there, sums, done, (after,))
        after = came[1]
    keep[2], send[2] = sums
    came[2] = swap(send[2], "xl", 1)
    slots = slots_of(turn, keep, came)
    total = None
    for t in (2, 3, 0, 1):
        part = deliver(slots[t], t).astype(jnp.float32)
        total = part if total is None else total + part
    return total * weight


def per_device(src_traces, rec_traces):
    planes, members = lax.axis_size("src"), lax.axis_size("xl")
    weight = jnp.float32(1.0 / math.sqrt(src_traces.shape[1] * members))
    if planes == 4 and members == 8 and rec_traces.shape[:2] == (sum(RIGHTS), 16):
        return four_planes(src_traces, rec_traces, weight)
    return gather_and_scatter(src_traces, rec_traces, weight)


def solution(mesh):
    return jax.shard_map(
        per_device,
        mesh=mesh,
        in_specs=(P("src", "xl", None), P("xl", "src", None)),
        out_specs=P("src", "xl", None),
        check_vma=False,
    )
```

time: 38.2 us -> 32.7 us (0.86)
  the two profiles are of different devices: /device:TPU:22 before, /device:TPU:12 now
where the time goes in v2:
time: 32.7 us; the launch traced here: 32.5 us
  starting transfers between devices  12.8 us (39%)
  waiting for transfers between devices  10.3 us (31%)
  Pallas kernels  8.63 us (26%)
  other arithmetic  0.69 us (2%)
    ppermute x4, starting transfers between devices, deliver(): return lax.ppermute(value, ('src', 'xl'), pairs)  7 us
    ppermute x7, starting transfers between devices, swap(): return lax.ppermute(value, axis, [(i, i ^ flip) for i in range(count)])  5.79 us
    ppermute x7, waiting for transfers between devices, swap(): return lax.ppermute(value, axis, [(i, i ^ flip) for i in range(count)])  5.17 us
    ppermute x4, waiting for transfers between devices, deliver(): return lax.ppermute(value, ('src', 'xl'), pairs)  5.09 us
    pallas_call x5, Pallas kernels, tiles_of(): pl.pallas_call(functools.partial(tiles_kernel, lefts=len(lefts), rights=l...  4.55 us
    pallas_call x1, Pallas kernels, first_spectra(): pl.pallas_call(functools.partial(first_spectra_kernel, steps=steps), in_s...  2.28 us
    pallas_call x3, Pallas kernels, spectra(): pl.pallas_call(spectra_kernel, grid=(count // points,), in_specs=[pl.Bloc...  1.72 us
    mul x1, other arithmetic, four_planes(): return total * weight  0.69 us
  transfers between devices with their start and end apart: 11, of which 6 were waited for; matrix products, arithmetic and copies ran while one was open for 0% of the time, Pallas kernels for 16%

profile of v2, /device:TPU:12, one launch (start us, length us, event | category | flops | bytes accessed | tf_op | source)
XLA Modules:
  0.0 32.5 jit_solution(12872275808609091275)
XLA Ops:
  0.0 2.3 %shard_map.46.refs_0_.refs_2_.refs_1_ = bf16[16,16,256]{2,1,0:T(8,128)(2,1)S(1)} custom-call(f32[32,16,1024]{2,1,0:T(8,128)} %traces_ref.6, bf16[1024,256]{1,0:T(8,128)(2,1)} %constant.38.clone.high_ref, bf16[1024,256]{1,0:T(8,128)(2,1)} %constant.39.clone.low_ref), custom_call_target="tpu_custom_call" | custom-call | tf_op jit(solution)/shard_map/pallas_call | solution.py:104
  2.3 2.7 %collective-permute-start.2 = (bf16[16,16,256]{2,1,0:T(8,128)(2,1)S(1)}, bf16[16,16,256]{2,1,0:T(8,128)(2,1)S(1)}, u32[]{:S(2)}, u32[]{:S(2)}) collective-permute-start(bf16[16,16,256]{2,1,0:T(8,128)(2,1)S(1)} %shard_map.46.refs_0_.refs_2_.refs_1_), channel_id=1, source_target_pairs={{0,16},{8,24},{16,0},{24,8},{1,17},{9,25},{17,1},{25,9},{2,18},{10... | collective-permute-start | bytes 393224 | tf_op jit(solution)/shard_map/ppermute | solution.py:318
  5.0 0.6 %shard_map.47.refs_0_ = bf16[16,16,256]{2,1,0:T(8,128)(2,1)S(1)} custom-call(f32[16,32,1024]{2,1,0:T(8,128)S(1)} %copy-done.1, bf16[1024,256]{1,0:T(8,128)(2,1)S(1)} %copy-done.2, bf16[1024,256]{1,0:T(8,128)(2,1)S(1)} %copy-done.3, bf16[16,16,256]{2,1,0:T(8,128)(2,1)S(1)} %shard_map.46.refs_0_.refs_2_.refs_1_), custom_call_target="tpu_custom_call" | custom-call | flops 402653184 | bytes 1048576 | tf_op jit(solution)/shard_map/pallas_call | solution.py:58
  5.5 0.5 %collective-permute-start.1 = (bf16[16,16,256]{2,1,0:T(8,128)(2,1)S(1)}, bf16[16,16,256]{2,1,0:T(8,128)(2,1)S(1)}, u32[]{:S(2)}, u32[]{:S(2)}) collective-permute-start(bf16[16,16,256]{2,1,0:T(8,128)(2,1)S(1)} %shard_map.47.refs_0_), channel_id=1, source_target_pairs={{0,8},{8,0},{16,24},{24,16},{1,9},{9,1},{17,25},{25,17},{2,10},{10... | collective-permute-start | bytes 393224 | tf_op jit(solution)/shard_map/ppermute | solution.py:318
  6.1 0.6 %shard_map.48.refs_0_.refs_3_.refs_1_ = bf16[16,16,256]{2,1,0:T(8,128)(2,1)S(1)} custom-call(f32[32,16,1024]{2,1,0:T(8,128)S(1)} %copy-done, bf16[1024,256]{1,0:T(8,128)(2,1)S(1)} %copy-done.2, bf16[1024,256]{1,0:T(8,128)(2,1)S(1)} %copy-done.3, bf16[16,16,256]{2,1,0:T(8,128)(2,1)S(1)} %shard_map.47.refs_0_), custom_call_target="tpu_custom_call" | custom-call | flops 402653184 | bytes 1048576 | tf_op jit(solution)/shard_map/pallas_call | solution.py:58
  6.6 0.6 %shard_map.49.refs_1_.refs_4_.refs_0_ = bf16[16,16,256]{2,1,0:T(8,128)(2,1)S(1)} custom-call(f32[16,32,1024]{2,1,0:T(8,128)S(1)} %copy-done.1, bf16[1024,256]{1,0:T(8,128)(2,1)S(1)} %copy-done.2, bf16[1024,256]{1,0:T(8,128)(2,1)S(1)} %copy-done.3, bf16[16,16,256]{2,1,0:T(8,128)(2,1)S(1)} %shard_map.48.refs_0_.refs_3_.refs_1_), custom_call_target="tpu_custom_call" | custom-call | flops 402653184 | bytes 1048576 | tf_op jit(solution)/shard_map/pallas_call | solution.py:58
  7.2 1.6 %collective-permute-start = (bf16[16,16,256]{2,1,0:T(8,128)(2,1)S(1)}, bf16[16,16,256]{2,1,0:T(8,128)(2,1)S(1)}, u32[]{:S(2)}, u32[]{:S(2)}) collective-permute-start(bf16[16,16,256]{2,1,0:T(8,128)(2,1)S(1)} %shard_map.49.refs_1_.refs_4_.refs_0_), channel_id=1, source_target_pairs={{0,8},{8,0},{16,24},{24,16},{1,9},{9,1},{17,25},{25,17},{2,10},{10... | collective-permute-start | bytes 393224 | tf_op jit(solution)/shard_map/ppermute | solution.py:318
  9.2 1.1 %shard_map.50 = (f32[1,16,8,256]{3,2,1,0:T(8,128)S(1)}, bf16[1,16,8,256]{3,2,1,0:T(8,128)(2,1)S(1)}) custom-call(s32[1]{0:T(128)} %bitcast.1.core_ref, bf16[16,16,256]{2,1,0:T(8,128)(2,1)S(1)} %shard_map.47.refs_0_, bf16[16,16,256]{2,1,0:T(8,128)(2,1)S(1)} %shard_map.49.refs_1_.refs_4_.refs_0_, bf16[16,16,256]{2,1,0:T(8,128)(2,1)S(1)} %shard_map.46.refs_0_.refs_2_.refs_1_, ...), custom_call_target="tpu_custom_call" | custom-call | flops 33554432 | bytes 1048576 | tf_op jit(solution)/shard_map/pallas_call | solution.py:223
  10.4 3.8 %collective-permute-done.1.refs_0_.refs_1_ = bf16[16,16,256]{2,1,0:T(8,128)(2,1)S(1)} collective-permute-done((bf16[16,16,256]{2,1,0:T(8,128)(2,1)S(1)}, bf16[16,16,256]{2,1,0:T(8,128)(2,1)S(1)}, u32[]{:S(2)}, u32[]{:S(2)}) %collective-permute-start.1) | collective-permute-done | bytes 131104 | tf_op jit(solution)/shard_map/ppermute | solution.py:318
  14.2 0.6 %shard_map.51.refs_3_.refs_2_ = f32[1,2,16,8,256]{4,3,2,1,0:T(8,128)S(1)} custom-call(s32[1]{0:T(128)} %bitcast.1.core_ref, bf16[16,16,256]{2,1,0:T(8,128)(2,1)S(1)} %collective-permute-done.1.refs_0_.refs_1_, bf16[16,16,256]{2,1,0:T(8,128)(2,1)S(1)} %shard_map.46.refs_0_.refs_2_.refs_1_, f32[1,16,8,256]{3,2,1,0:T(8,128)S(1)} %get-tuple-element.15.refs_2_.refs_0_), custom_call_target="tpu_custom_call" | custom-call | flops 16777216 | bytes 1048576 | tf_op jit(solution)/shard_map/pallas_call | solution.py:223
  14.8 1.1 %shard_map.52.refs_3_ = f32[2,2,16,8,256]{4,3,2,1,0:T(8,128)S(1)} custom-call(s32[1]{0:T(128)} %bitcast.1.core_ref, bf16[16,16,256]{2,1,0:T(8,128)(2,1)S(1)} %shard_map.47.refs_0_, bf16[16,16,256]{2,1,0:T(8,128)(2,1)S(1)} %collective-permute-done.1.refs_0_.refs_1_, bf16[16,16,256]{2,1,0:T(8,128)(2,1)S(1)} %collective-permute-done.2.refs_2_, ...), custom_call_target="tpu_custom_call" | custom-call | flops 33554432 | bytes 1048576 | tf_op jit(solution)/shard_map/pallas_call | solution.py:223
  15.9 0.6 %shard_map.53 = (f32[1,16,8,256]{3,2,1,0:T(8,128)S(1)}, bf16[1,16,8,256]{3,2,1,0:T(8,128)(2,1)S(1)}) custom-call(s32[1]{0:T(128)} %bitcast.1.core_ref, bf16[16,16,256]{2,1,0:T(8,128)(2,1)S(1)} %collective-permute-done.refs_0_.refs_1_, bf16[16,16,256]{2,1,0:T(8,128)(2,1)S(1)} %shard_map.48.refs_0_.refs_3_.refs_1_, ...), custom_call_target="tpu_custom_call" | custom-call | flops 16777216 | bytes 1048576 | tf_op jit(solution)/shard_map/pallas_call | solution.py:223
  16.5 0.4 %collective-permute-done.4.refs_2_ = bf16[16,16,256]{2,1,0:T(8,128)(2,1)S(1)} collective-permute-done((bf16[16,16,256]{2,1,0:T(8,128)(2,1)S(1)}, bf16[16,16,256]{2,1,0:T(8,128)(2,1)S(1)}, u32[]{:S(2)}, u32[]{:S(2)}) %collective-permute-start.4) | collective-permute-done | bytes 131104 | tf_op jit(solution)/shard_map/ppermute | solution.py:318
  17.0 1.1 %shard_map.54 = (f32[2,16,8,256]{3,2,1,0:T(8,128)S(1)}, bf16[2,16,8,256]{3,2,1,0:T(8,128)(2,1)S(1)}) custom-call(s32[1]{0:T(128)} %bitcast.1.core_ref, bf16[16,16,256]{2,1,0:T(8,128)(2,1)S(1)} %shard_map.49.refs_1_.refs_4_.refs_0_, bf16[16,16,256]{2,1,0:T(8,128)(2,1)S(1)} %collective-permute-done.refs_0_.refs_1_, ...), custom_call_target="tpu_custom_call" | custom-call | flops 33554432 | bytes 1048576 | tf_op jit(solution)/shard_map/pallas_call | solution.py:223
  18.2 0.5 %collective-permute-start.5 = (bf16[1,16,8,256]{3,2,1,0:T(8,128)(2,1)S(1)}, bf16[1,16,8,256]{3,2,1,0:T(8,128)(2,1)S(1)}, u32[]{:S(2)}, u32[]{:S(2)}) collective-permute-start(bf16[1,16,8,256]{3,2,1,0:T(8,128)(2,1)S(1)} %get-tuple-element.19), channel_id=1, source_target_pairs={{0,1},{1,0},{2,3},{3,2},{4,5},{5,4},{6,7},{7,6},{8,9},{9,8},{10,11... | collective-permute-start | bytes 196616 | tf_op jit(solution)/shard_map/ppermute | solution.py:318
  18.7 0.9 %collective-permute-done.5.refs_4_ = bf16[1,16,8,256]{3,2,1,0:T(8,128)(2,1)S(1)} collective-permute-done((bf16[1,16,8,256]{3,2,1,0:T(8,128)(2,1)S(1)}, bf16[1,16,8,256]{3,2,1,0:T(8,128)(2,1)S(1)}, u32[]{:S(2)}, u32[]{:S(2)}) %collective-permute-start.5) | collective-permute-done | bytes 65568 | tf_op jit(solution)/shard_map/ppermute | solution.py:318
  19.7 1.5 %collective-permute-start.10 = (bf16[16,8,256]{2,1,0:T(8,128)(2,1)S(1)}, bf16[16,8,256]{2,1,0:T(8,128)(2,1)S(1)}, u32[]{:S(2)}, u32[]{:S(2)}) collective-permute-start(bf16[16,8,256]{2,1,0:T(8,128)(2,1)S(1)} %get-tuple-element.24), channel_id=1, source_target_pairs={{0,8},{1,9},{2,0},{3,1},{4,12},{5,13},{6,4},{7,5},{8,10},{9,11},{1... | collective-permute-start | bytes 196616 | tf_op jit(solution)/shard_map/ppermute | solution.py:330
  21.3 1.9 %collective-permute-start.7 = (bf16[16,8,256]{2,1,0:T(8,128)(2,1)S(1)}, bf16[16,8,256]{2,1,0:T(8,128)(2,1)S(1)}, u32[]{:S(2)}, u32[]{:S(2)}) collective-permute-start(bf16[16,8,256]{2,1,0:T(8,128)(2,1)S(1)} %get-tuple-element.21), channel_id=1, source_target_pairs={{0,4},{1,5},{2,12},{3,13},{4,0},{5,1},{6,8},{7,9},{8,6},{9,7},{10,... | collective-permute-start | bytes 196616 | tf_op jit(solution)/shard_map/ppermute | solution.py:330
  23.2 1.6 %collective-permute-start.8 = (bf16[16,8,256]{2,1,0:T(8,128)(2,1)S(1)}, bf16[16,8,256]{2,1,0:T(8,128)(2,1)S(1)}, u32[]{:S(2)}, u32[]{:S(2)}) collective-permute-start(bf16[16,8,256]{2,1,0:T(8,128)(2,1)S(1)} %get-tuple-element.22), channel_id=1, source_target_pairs={{0,12},{1,13},{2,4},{3,5},{4,8},{5,9},{6,0},{7,1},{8,14},{9,15},{1... | collective-permute-start | bytes 196616 | tf_op jit(solution)/shard_map/ppermute | solution.py:330
  24.8 1.9 %collective-permute-start.9 = (bf16[16,8,256]{2,1,0:T(8,128)(2,1)S(1)}, bf16[16,8,256]{2,1,0:T(8,128)(2,1)S(1)}, u32[]{:S(2)}, u32[]{:S(2)}) collective-permute-start(bf16[16,8,256]{2,1,0:T(8,128)(2,1)S(1)} %get-tuple-element.23), channel_id=1, source_target_pairs={{0,0},{1,1},{2,8},{3,9},{4,4},{5,5},{6,12},{7,13},{8,2},{9,3},{10,... | collective-permute-start | bytes 196616 | tf_op jit(solution)/shard_map/ppermute | solution.py:330
  26.7 1.1 %collective-permute-done.7 = bf16[16,8,256]{2,1,0:T(8,128)(2,1)S(1)} collective-permute-done((bf16[16,8,256]{2,1,0:T(8,128)(2,1)S(1)}, bf16[16,8,256]{2,1,0:T(8,128)(2,1)S(1)}, u32[]{:S(2)}, u32[]{:S(2)}) %collective-permute-start.7) | collective-permute-done | bytes 65568 | tf_op jit(solution)/shard_map/ppermute | solution.py:330
  27.8 0.7 %collective-permute-done.8 = bf16[16,8,256]{2,1,0:T(8,128)(2,1)S(1)} collective-permute-done((bf16[16,8,256]{2,1,0:T(8,128)(2,1)S(1)}, bf16[16,8,256]{2,1,0:T(8,128)(2,1)S(1)}, u32[]{:S(2)}, u32[]{:S(2)}) %collective-permute-start.8) | collective-permute-done | bytes 65568 | tf_op jit(solution)/shard_map/ppermute | solution.py:330
  28.6 3.3 %collective-permute-done.9 = bf16[16,8,256]{2,1,0:T(8,128)(2,1)S(1)} collective-permute-done((bf16[16,8,256]{2,1,0:T(8,128)(2,1)S(1)}, bf16[16,8,256]{2,1,0:T(8,128)(2,1)S(1)}, u32[]{:S(2)}, u32[]{:S(2)}) %collective-permute-start.9) | collective-permute-done | bytes 65568 | tf_op jit(solution)/shard_map/ppermute | solution.py:330
  31.8 0.7 %add_multiply_fusion = f32[16,8,256]{2,1,0:T(8,128)} fusion(bf16[16,8,256]{2,1,0:T(8,128)(2,1)S(1)} %collective-permute-done.10, bf16[16,8,256]{2,1,0:T(8,128)(2,1)S(1)} %collective-permute-done.9, bf16[16,8,256]{2,1,0:T(8,128)(2,1)S(1)} %collective-permute-done.8, bf16[16,8,256]{2,1,0:T(8,128)(2,1)S(1)} %collective-permute-done.7), kind=kLoop, calls=%fused_computation | loop fusion | flops 262144 | bytes 393216 | tf_op jit(solution)/shard_map/mul | solution.py:383
  (17 shorter events, 0.6 us)
Async XLA Ops:
  0.0 5.0 %copy-start.2 = (bf16[1024,256]{1,0:T(8,128)(2,1)S(1)}, bf16[1024,256]{1,0:T(8,128)(2,1)}, u32[]{:S(2)}) copy-start(bf16[1024,256]{1,0:T(8,128)(2,1)} %constant.38.clone.high_ref) | copy-start | bytes 1572868
  0.0 5.0 %copy-start.3 = (bf16[1024,256]{1,0:T(8,128)(2,1)S(1)}, bf16[1024,256]{1,0:T(8,128)(2,1)}, u32[]{:S(2)}) copy-start(bf16[1024,256]{1,0:T(8,128)(2,1)} %constant.39.clone.low_ref) | copy-start | bytes 1572868
  0.0 5.0 %copy-start.1 = (f32[16,32,1024]{2,1,0:T(8,128)S(1)}, f32[16,32,1024]{2,1,0:T(8,128)}, u32[]{:S(2)}) copy-start(f32[16,32,1024]{2,1,0:T(8,128)} %traces_ref.7) | copy-start | bytes 6291460
  2.3 3.8 %copy-start = (f32[32,16,1024]{2,1,0:T(8,128)S(1)}, f32[32,16,1024]{2,1,0:T(8,128)}, u32[]{:S(2)}) copy-start(f32[32,16,1024]{2,1,0:T(8,128)} %traces_ref.6) | copy-start | bytes 6291460
  2.3 12.5 %collective-permute-start.2 = (bf16[16,16,256]{2,1,0:T(8,128)(2,1)S(1)}, bf16[16,16,256]{2,1,0:T(8,128)(2,1)S(1)}, u32[]{:S(2)}, u32[]{:S(2)}) collective-permute-start(bf16[16,16,256]{2,1,0:T(8,128)(2,1)S(1)} %shard_map.46.refs_0_.refs_2_.refs_1_), channel_id=1, source_target_pairs={{0,16},{8,24},{16,0},{24,8},{1,17},{9,25},{17,1},{25,9},{2,18},{10... | collective-permute-start | bytes 393224 | tf_op jit(solution)/shard_map/ppermute | solution.py:318
  5.5 8.6 %collective-permute-start.1 = (bf16[16,16,256]{2,1,0:T(8,128)(2,1)S(1)}, bf16[16,16,256]{2,1,0:T(8,128)(2,1)S(1)}, u32[]{:S(2)}, u32[]{:S(2)}) collective-permute-start(bf16[16,16,256]{2,1,0:T(8,128)(2,1)S(1)} %shard_map.47.refs_0_), channel_id=1, source_target_pairs={{0,8},{8,0},{16,24},{24,16},{1,9},{9,1},{17,25},{25,17},{2,10},{10... | collective-permute-start | bytes 393224 | tf_op jit(solution)/shard_map/ppermute | solution.py:318
  7.2 8.7 %collective-permute-start = (bf16[16,16,256]{2,1,0:T(8,128)(2,1)S(1)}, bf16[16,16,256]{2,1,0:T(8,128)(2,1)S(1)}, u32[]{:S(2)}, u32[]{:S(2)}) collective-permute-start(bf16[16,16,256]{2,1,0:T(8,128)(2,1)S(1)} %shard_map.49.refs_1_.refs_4_.refs_0_), channel_id=1, source_target_pairs={{0,8},{8,0},{16,24},{24,16},{1,9},{9,1},{17,25},{25,17},{2,10},{10... | collective-permute-start | bytes 393224 | tf_op jit(solution)/shard_map/ppermute | solution.py:318
  8.9 8.1 %collective-permute-start.4 = (bf16[16,16,256]{2,1,0:T(8,128)(2,1)S(1)}, bf16[16,16,256]{2,1,0:T(8,128)(2,1)S(1)}, u32[]{:S(2)}, u32[]{:S(2)}) collective-permute-start(bf16[16,16,256]{2,1,0:T(8,128)(2,1)S(1)} %shard_map.48.refs_0_.refs_3_.refs_1_), channel_id=1, source_target_pairs={{0,16},{8,24},{16,0},{24,8},{1,17},{9,25},{17,1},{25,9},{2,18},{10... | collective-permute-start | bytes 393224 | tf_op jit(solution)/shard_map/ppermute | solution.py:318
  10.3 4.4 %collective-permute-start.3 = (bf16[1,16,8,256]{3,2,1,0:T(8,128)(2,1)S(1)}, bf16[1,16,8,256]{3,2,1,0:T(8,128)(2,1)S(1)}, u32[]{:S(2)}, u32[]{:S(2)}) collective-permute-start(bf16[1,16,8,256]{3,2,1,0:T(8,128)(2,1)S(1)} %get-tuple-element.16), channel_id=1, source_target_pairs={{0,1},{1,0},{2,3},{3,2},{4,5},{5,4},{6,7},{7,6},{8,9},{9,8},{10,11... | collective-permute-start | bytes 196616 | tf_op jit(solution)/shard_map/ppermute | solution.py:318
  18.1 1.5 %collective-permute-start.6 = (bf16[2,16,8,256]{3,2,1,0:T(8,128)(2,1)S(1)}, bf16[2,16,8,256]{3,2,1,0:T(8,128)(2,1)S(1)}, u32[]{:S(2)}, u32[]{:S(2)}) collective-permute-start(bf16[2,16,8,256]{3,2,1,0:T(8,128)(2,1)S(1)} %get-tuple-element.20), channel_id=1, source_target_pairs={{0,1},{1,0},{2,3},{3,2},{4,5},{5,4},{6,7},{7,6},{8,9},{9,8},{10,11... | collective-permute-start | bytes 393224 | tf_op jit(solution)/shard_map/ppermute | solution.py:318
  18.2 1.4 %collective-permute-start.5 = (bf16[1,16,8,256]{3,2,1,0:T(8,128)(2,1)S(1)}, bf16[1,16,8,256]{3,2,1,0:T(8,128)(2,1)S(1)}, u32[]{:S(2)}, u32[]{:S(2)}) collective-permute-start(bf16[1,16,8,256]{3,2,1,0:T(8,128)(2,1)S(1)} %get-tuple-element.19), channel_id=1, source_target_pairs={{0,1},{1,0},{2,3},{3,2},{4,5},{5,4},{6,7},{7,6},{8,9},{9,8},{10,11... | collective-permute-start | bytes 196616 | tf_op jit(solution)/shard_map/ppermute | solution.py:318
  19.7 7.0 %collective-permute-start.10 = (bf16[16,8,256]{2,1,0:T(8,128)(2,1)S(1)}, bf16[16,8,256]{2,1,0:T(8,128)(2,1)S(1)}, u32[]{:S(2)}, u32[]{:S(2)}) collective-permute-start(bf16[16,8,256]{2,1,0:T(8,128)(2,1)S(1)} %get-tuple-element.24), channel_id=1, source_target_pairs={{0,8},{1,9},{2,0},{3,1},{4,12},{5,13},{6,4},{7,5},{8,10},{9,11},{1... | collective-permute-start | bytes 196616 | tf_op jit(solution)/shard_map/ppermute | solution.py:330
  21.3 6.6 %collective-permute-start.7 = (bf16[16,8,256]{2,1,0:T(8,128)(2,1)S(1)}, bf16[16,8,256]{2,1,0:T(8,128)(2,1)S(1)}, u32[]{:S(2)}, u32[]{:S(2)}) collective-permute-start(bf16[16,8,256]{2,1,0:T(8,128)(2,1)S(1)} %get-tuple-element.21), channel_id=1, source_target_pairs={{0,4},{1,5},{2,12},{3,13},{4,0},{5,1},{6,8},{7,9},{8,6},{9,7},{10,... | collective-permute-start | bytes 196616 | tf_op jit(solution)/shard_map/ppermute | solution.py:330
  23.2 5.4 %collective-permute-start.8 = (bf16[16,8,256]{2,1,0:T(8,128)(2,1)S(1)}, bf16[16,8,256]{2,1,0:T(8,128)(2,1)S(1)}, u32[]{:S(2)}, u32[]{:S(2)}) collective-permute-start(bf16[16,8,256]{2,1,0:T(8,128)(2,1)S(1)} %get-tuple-element.22), channel_id=1, source_target_pairs={{0,12},{1,13},{2,4},{3,5},{4,8},{5,9},{6,0},{7,1},{8,14},{9,15},{1... | collective-permute-start | bytes 196616 | tf_op jit(solution)/shard_map/ppermute | solution.py:330
  24.8 7.0 %collective-permute-start.9 = (bf16[16,8,256]{2,1,0:T(8,128)(2,1)S(1)}, bf16[16,8,256]{2,1,0:T(8,128)(2,1)S(1)}, u32[]{:S(2)}, u32[]{:S(2)}) collective-permute-start(bf16[16,8,256]{2,1,0:T(8,128)(2,1)S(1)} %get-tuple-element.23), channel_id=1, source_target_pairs={{0,0},{1,1},{2,8},{3,9},{4,4},{5,5},{6,12},{7,13},{8,2},{9,3},{10,... | collective-permute-start | bytes 196616 | tf_op jit(solution)/shard_map/ppermute | solution.py:330

commit v3 on v0

v3 whole, which is shorter than its diff:
```python
import functools
import math

import jax
import jax.numpy as jnp
import ml_dtypes
import numpy as np
from jax import lax
from jax.experimental import pallas as pl
from jax.experimental.pallas import tpu as pltpu
from jax.sharding import PartitionSpec as P

F = 128
FBASE = 4
VMEM = 40 << 20
POINTS = 8
ROWS = 16 * POINTS
ONES = ((0, 2), (2, 2))
OTHERS = ((0, 2), (2, 1), (3, 1))


def fourier_table(samples):
    times = np.arange(samples // 2)[:, None]
    bins = FBASE + np.arange(F)
    angles = times * bins[None, :] % samples * (2.0 * math.pi / samples)
    basis = np.concatenate([np.cos(angles), -np.sin(angles)], axis=1)
    basis = (basis / math.sqrt(samples)).astype(np.float32)
    high = basis.astype(ml_dtypes.bfloat16)
    low = (basis - high.astype(np.float32)).astype(ml_dtypes.bfloat16)
    return jnp.asarray(high), jnp.asarray(low)


def transform(traces, high_table, low_table):
    rows, samples = traces.shape
    half = samples // 2
    halves = jnp.concatenate([traces[:, :half], traces[:, half:]], axis=0)
    high = halves.astype(jnp.bfloat16)
    low = (halves - high.astype(jnp.float32)).astype(jnp.bfloat16)
    dot = functools.partial(jnp.dot, preferred_element_type=jnp.float32)
    total = dot(high, high_table) + (dot(high, low_table) + dot(low, high_table))
    odd = (FBASE + lax.broadcasted_iota(jnp.int32, (1, 2 * F), 1)) % 2
    return total[:rows] + total[rows:] * (1 - 2 * odd).astype(jnp.float32)


def spectra_kernel(traces_ref, high_ref, low_ref, out_ref):
    traces = traces_ref[...].reshape(-1, traces_ref.shape[-1])
    total = transform(traces, high_ref[...], low_ref[...])
    out_ref[...] = total.astype(jnp.bfloat16).reshape(out_ref.shape)


def spectra(traces, table):
    rows, width, samples = traces.shape
    block = 8 if rows % 8 == 0 else rows
    whole = pl.BlockSpec((samples // 2, 2 * F), lambda i: (0, 0))
    return pl.pallas_call(
        spectra_kernel,
        grid=(rows // block,),
        in_specs=[pl.BlockSpec((block, width, samples), lambda i: (i, 0, 0)), whole, whole],
        out_specs=pl.BlockSpec((block, width, 2 * F), lambda i: (i, 0, 0)),
        out_shape=jax.ShapeDtypeStruct((rows, width, 2 * F), jnp.bfloat16),
        compiler_params=pltpu.CompilerParams(vmem_limit_bytes=VMEM),
    )(traces, *table)


def first_kernel(side_ref, src_ref, rec_ref, high_ref, low_ref, out_ref, traces, high, low, sems, *, blocks):
    tables = [
        pltpu.make_async_copy(high_ref, high, sems.at[0]),
        pltpu.make_async_copy(low_ref, low, sems.at[1]),
    ]
    choices = [
        [pltpu.make_async_copy(rec_ref.at[i], traces.at[i], sems.at[2 + i]) for i in range(blocks)],
        [pltpu.make_async_copy(src_ref.at[:, i], traces.at[i], sems.at[2 + i]) for i in range(blocks)],
    ]
    for side, copies in enumerate(choices):

        @pl.when(side_ref[0] == side)
        def _(copies=copies):
            for copy in copies:
                copy.start()

    for copy in tables:
        copy.start()
    for side, copies in enumerate(choices):

        @pl.when(side_ref[0] == side)
        def _(copies=copies):
            for copy in copies:
                copy.wait()

    for copy in tables:
        copy.wait()
    total = transform(traces[...].reshape(-1, traces.shape[-1]), high[...], low[...])
    out_ref[...] = total.astype(jnp.bfloat16)


def first_spectra(side, blocks, src_blocks, rec_blocks, table):
    samples = src_blocks.shape[3]
    operands = [pltpu.with_memory_space_constraint(one, pltpu.HBM) for one in (src_blocks, rec_blocks, *table)]
    return pl.pallas_call(
        functools.partial(first_kernel, blocks=blocks),
        in_specs=[pl.BlockSpec(memory_space=pltpu.SMEM)] + [pl.BlockSpec(memory_space=pltpu.HBM)] * 4,
        out_specs=pl.BlockSpec(memory_space=pltpu.VMEM),
        out_shape=jax.ShapeDtypeStruct((blocks * ROWS, 2 * F), jnp.bfloat16),
        scratch_shapes=[
            pltpu.VMEM((blocks, 16, POINTS, samples), jnp.float32),
            pltpu.VMEM((samples // 2, 2 * F), jnp.bfloat16),
            pltpu.VMEM((samples // 2, 2 * F), jnp.bfloat16),
            pltpu.SemaphoreType.DMA((2 + blocks,)),
        ],
        compiler_params=pltpu.CompilerParams(vmem_limit_bytes=VMEM),
    )(side, *operands)


def either_kernel(side_ref, src_ref, rec_ref, high_ref, low_ref, *refs, other, first, blocks):
    out_ref = refs[-1]
    samples = src_ref.shape[-1]
    from_src = (side_ref[0] ^ other) == 1
    parts = []
    for i in range(first, first + blocks):
        src, rec = src_ref[:, i].reshape(ROWS, samples), rec_ref[i].reshape(ROWS, samples)
        parts.append(jnp.where(from_src, src, rec))
    total = transform(jnp.concatenate(parts, axis=0), high_ref[...], low_ref[...])
    out_ref[...] = total.astype(jnp.bfloat16)


def either_spectra(side, other, first, blocks, src_blocks, rec_blocks, table, after):
    samples = src_blocks.shape[3]
    rows = blocks * ROWS
    vmem = pl.BlockSpec(memory_space=pltpu.VMEM)
    return pl.pallas_call(
        functools.partial(either_kernel, other=other, first=first, blocks=blocks),
        in_specs=[pl.BlockSpec(memory_space=pltpu.SMEM)] + [vmem] * 4 + [pl.BlockSpec(memory_space=pl.ANY)],
        out_specs=vmem,
        out_shape=jax.ShapeDtypeStruct((rows, 2 * F), jnp.bfloat16),
        compiler_params=pltpu.CompilerParams(vmem_limit_bytes=VMEM),
        cost_estimate=pl.CostEstimate(
            flops=rows, bytes_accessed=rows, transcendentals=0
        ),
    )(side, src_blocks, rec_blocks, *table, after)


def products(left, right, points, starts, emit):
    many, groups = 4, len(starts)

    def some_sources(block, carry):
        def some_points(step, sums):
            sums = list(sums)
            for inner in range(POINTS):
                point = step * POINTS + inner
                rights = [
                    [right[k, pl.ds(pl.multiple_of(point * 16 + at, 8), 8), :] for at in starts] for k in range(3)
                ]
                for s in range(many):
                    row = (block * many + s) * points + point
                    for k in range(3):
                        one = left[k, pl.ds(row, 1), :]
                        for g in range(groups):
                            i = (s * groups + g) * 3 + k
                            sums[i] = sums[i] + one * rights[k][g]
            return tuple(sums)

        zero = jnp.zeros((8, F), jnp.float32)
        sums = lax.fori_loop(0, points // POINTS, some_points, (zero,) * (many * groups * 3))
        for s in range(many):
            for g in range(groups):
                first, second, third = sums[(s * groups + g) * 3 :][:3]
                emit(block * many + s, g, first - third, first + second)
        return carry

    lax.fori_loop(0, 16 // many, some_sources, 0)


def split(ref, block, forms, at, points, side):
    left = side.astype(jnp.float32)
    right = 1.0 - left

    def some_rows(step, carry):
        value = ref[pl.ds(pl.multiple_of(block * ROWS + step * 16, 16), 16)].astype(jnp.float32)
        for half in range(2):
            re, im = value[half * 8 : half * 8 + 8, :F], value[half * 8 : half * 8 + 8, F:]
            row = step * 2 + half
            start = jnp.where(side == 1, row * points + at * POINTS, at * ROWS + row * 8)
            here = pl.ds(pl.multiple_of(start, 8), 8)
            forms[0, here] = re + im * left
            forms[1, here] = im * right + re * (left - right)
            forms[2, here] = im + re * right
        return carry

    lax.fori_loop(0, ROWS // 16, some_rows, 0, unroll=2)


def tiles_kernel(side_ref, *refs, arrays, ones, others, carried, spare):
    operands, out, forms = refs[:arrays], refs[-2], refs[-1]
    before = refs[arrays] if carried else None
    side = side_ref[0]
    points = len(ones) * POINTS
    for at, (array, block) in enumerate(ones):
        split(operands[array], block, forms.at[0], at, points, side)
    for tile, blocks in enumerate(others):
        for at, (array, block) in enumerate(blocks):
            split(operands[array], block, forms.at[1 + tile], at, points, 1 - side)

    def tile_of(tile, carry):
        left = forms.at[jnp.where(side == 1, 0, 1 + tile)]
        right = forms.at[jnp.where(side == 1, 1 + tile, 0)]

        def emit(source, group, re, im):
            if carried:
                re = re + before[tile, group, source, :, :F]
                im = im + before[tile, group, source, :, F:]
            out[tile, group, source, :, :F] = re
            out[tile, group, source, :, F:] = im

        products(left, right, points, (0, 8), emit)
        return carry

    lax.fori_loop(0, len(others), tile_of, 0)


def tile_at(place, core, op):
    side, _, turn = place
    tile = turn ^ jnp.where(core == 0, 1 - op, 2 + op)
    middle = jnp.logical_or(tile == 1, tile == 2)
    return jnp.where(jnp.logical_and(middle, side == 1), 3 - tile, tile)


def with_tile(place, kept, use):
    first = 0
    for array in kept:
        count = array.shape[0]

        @pl.when(jnp.logical_and(place >= first, place < first + count))
        def _(array=array, first=first):
            use(array.at[place - first])

        first += count


def last_tiles_kernel(side_ref, core_ref, turn_ref, *refs, kept, **options):
    place = side_ref[0], core_ref[0], turn_ref[0]
    earlier, send = refs[:kept], refs[-2]
    refs = refs[kept:-2] + refs[-1:]
    tiles_kernel(side_ref, *refs, **options)
    for op in range(2):

        def use(tile, op=op):
            send[op] = tile[...].astype(send.dtype)

        with_tile(tile_at(place, 1 - place[1], op), [*earlier, refs[-2]], use)


def tiles_of(place, ones, others, before=None, after=(), kept=()):
    arrays = []

    def placed(blocks):
        result = []
        for array, block in blocks:
            if not any(array is one for one in arrays):
                arrays.append(array)
            result.append(([array is one for one in arrays].index(True), block))
        return result

    ones, others = placed(ones), [placed(blocks) for blocks in others]
    count = len(others)
    out_shape = [jax.ShapeDtypeStruct((count, 2, 16, 8, 2 * F), jnp.float32)]
    if kept:
        out_shape.append(jax.ShapeDtypeStruct((2, 2, 16, 8, 2 * F), jnp.bfloat16))
    operands = [*kept, *arrays] + ([] if before is None else [before])
    vmem = pl.BlockSpec(memory_space=pltpu.VMEM)
    options = dict(arrays=len(arrays), ones=ones, others=others, carried=before is not None, spare=len(after))
    kernel = functools.partial(tiles_kernel, **options)
    scalars = place if kept else place[:1]
    if kept:
        kernel = functools.partial(last_tiles_kernel, kept=len(kept), **options)
    result = pl.pallas_call(
        kernel,
        in_specs=[pl.BlockSpec(memory_space=pltpu.SMEM)] * len(scalars)
        + [vmem] * len(operands)
        + [pl.BlockSpec(memory_space=pl.ANY)] * len(after),
        out_specs=[vmem] * len(out_shape),
        out_shape=out_shape,
        scratch_shapes=[pltpu.VMEM((1 + count, 3, len(ones) * ROWS, F), jnp.float32)],
        compiler_params=pltpu.CompilerParams(vmem_limit_bytes=VMEM),
        cost_estimate=pl.CostEstimate(flops=count, bytes_accessed=count, transcendentals=0),
    )(*scalars, *operands, *after)
    return result if kept else result[0]


def pairs_kernel(side_ref, core_ref, turn_ref, *refs, kept):
    place = side_ref[0], core_ref[0], turn_ref[0]
    came, outs = refs[kept], refs[kept + 1 :]
    for op, out in enumerate(outs):

        def use(tile, op=op, out=out):
            out[...] = (tile[...] + came[op].astype(jnp.float32)).astype(out.dtype)

        with_tile(tile_at(place, place[1], op), refs[:kept], use)


def pairs_of(place, kept, came):
    vmem = pl.BlockSpec(memory_space=pltpu.VMEM)
    return pl.pallas_call(
        functools.partial(pairs_kernel, kept=len(kept)),
        in_specs=[pl.BlockSpec(memory_space=pltpu.SMEM)] * 3 + [vmem] * (len(kept) + 1),
        out_specs=(vmem, vmem),
        out_shape=(jax.ShapeDtypeStruct(came.shape[1:], jnp.bfloat16),) * 2,
        compiler_params=pltpu.CompilerParams(vmem_limit_bytes=VMEM),
    )(*place, *kept, came)


def halves_kernel(core_ref, first, second, keep, send):
    own = core_ref[0]
    keep[...] = first[own].astype(jnp.float32) + second[own].astype(jnp.float32)
    send[...] = (first[1 - own].astype(jnp.float32) + second[1 - own].astype(jnp.float32)).astype(send.dtype)


def halves_of(place, first, second):
    vmem = pl.BlockSpec(memory_space=pltpu.VMEM)
    return pl.pallas_call(
        halves_kernel,
        in_specs=[pl.BlockSpec(memory_space=pltpu.SMEM), vmem, vmem],
        out_specs=(vmem, vmem),
        out_shape=(
            jax.ShapeDtypeStruct(first.shape[1:], jnp.float32),
            jax.ShapeDtypeStruct(first.shape[1:], jnp.bfloat16),
        ),
        compiler_params=pltpu.CompilerParams(vmem_limit_bytes=VMEM),
    )(place[1], first, second)


def block_kernel(left_ref, right_ref, out_ref, left_forms, right_forms):
    @pl.when(pl.program_id(0) == 0)
    def _():
        value = left_ref[...].astype(jnp.float32).reshape(-1, 2 * F)
        re, im = value[:, :F], value[:, F:]
        left_forms[0], left_forms[1], left_forms[2] = re + im, re, im

    value = right_ref[...].astype(jnp.float32).reshape(-1, 2 * F)
    re, im = value[:, :F], value[:, F:]
    right_forms[0], right_forms[1], right_forms[2] = re, im - re, re + im
    sources, points, _ = left_ref.shape

    def one_source(source, carry):
        def one_point(point, sums):
            row = source * points + point
            here = pl.ds(pl.multiple_of(point * 8, 8), 8)
            return tuple(total + left_forms[k, pl.ds(row, 1), :] * right_forms[k, here, :] for k, total in enumerate(sums))

        zero = jnp.zeros((8, F), jnp.float32)
        first, second, third = lax.fori_loop(0, points, one_point, (zero,) * 3)
        out_ref[source, :, :F] = first - third
        out_ref[source, :, F:] = first + second
        return carry

    lax.fori_loop(0, sources, one_source, 0)


def blocks_of(left, right):
    sources, points, _ = left.shape
    receivers = right.shape[1]
    return pl.pallas_call(
        block_kernel,
        grid=(receivers // 8,),
        in_specs=[
            pl.BlockSpec((sources, points, 2 * F), lambda i: (0, 0, 0)),
            pl.BlockSpec((points, 8, 2 * F), lambda i: (0, i, 0)),
        ],
        out_specs=pl.BlockSpec((sources, 8, 2 * F), lambda i: (0, i, 0)),
        out_shape=jax.ShapeDtypeStruct((sources, receivers, 2 * F), jnp.float32),
        scratch_shapes=[
            pltpu.VMEM((3, sources * points, F), jnp.float32),
            pltpu.VMEM((3, points * 8, F), jnp.float32),
        ],
        compiler_params=pltpu.CompilerParams(vmem_limit_bytes=VMEM),
    )(left, right)


def gather_and_scatter(src_traces, rec_traces, weight):
    table = fourier_table(src_traces.shape[2])
    left = spectra(src_traces, table)
    right = lax.all_gather(spectra(rec_traces, table), "src", axis=1, tiled=True)
    return lax.psum_scatter(blocks_of(left, right), "xl", scatter_dimension=1, tiled=True) * weight


def swap(value, axis, flip):
    count = lax.axis_size(axis)
    return lax.ppermute(value, axis, [(i, i ^ flip) for i in range(count)])


def side_of(z):
    return (z + 1) // 2 % 2


def cross(value, other):
    return lax.ppermute(value, "src", [(z, z ^ (1 if side_of(z) ^ other else 2)) for z in range(4)])


def deliver(value, op):
    members = lax.axis_size("xl")
    pairs = []
    for z in range(lax.axis_size("src")):
        for chip in range(members // 2):
            for core in range(2):
                tile = z ^ chip ^ ((2 + op) if core else (1 - op))
                target = (z ^ (tile & 1)) * members + (z ^ (tile & 2)) * 2 + core
                pairs.append((z * members + chip * 2 + core, target))
    return lax.ppermute(value, ("src", "xl"), pairs)


def four_planes(src_traces, rec_traces, weight):
    table = fourier_table(src_traces.shape[2])
    z, member = lax.axis_index("src"), lax.axis_index("xl")
    place = [one.reshape(1).astype(jnp.int32) for one in (side_of(z), member % 2, z ^ (member // 2))]
    samples = src_traces.shape[2]
    blocks = src_traces.shape[1] // POINTS
    src_blocks = src_traces.reshape(16, blocks, POINTS, samples)
    rec_blocks = rec_traces.reshape(blocks, 16, POINTS, samples)
    one, far_one, other, far_other = [], [], [], []
    token = None
    for first, count in ONES:
        if token is None:
            token = first_spectra(place[0], count, src_blocks, rec_blocks, table)
        else:
            token = either_spectra(place[0], 0, first, count, src_blocks, rec_blocks, table, token)
        far = cross(token, 0)
        one += [(token, i) for i in range(count)]
        far_one += [(far, i) for i in range(count)]
    for first, count in OTHERS:
        token = either_spectra(place[0], 1, first, count, src_blocks, rec_blocks, table, token)
        far = cross(token, 1)
        other += [(token, i) for i in range(count)]
        far_other += [(far, i) for i in range(count)]
    early = [tiles_of(place, one, [other], after=(token,))]
    sums, after = None, (early[0],)
    for first, count in ONES:
        here = slice(first, first + count)
        sums = tiles_of(place, one[here], [far_one[here]], sums, after)
        after = ()
    early.append(sums)
    sums = None
    for first, count in OTHERS:
        here = slice(first, first + count)
        kept = early if first + count == blocks else ()
        sums = tiles_of(place, far_other[here], [other[here], far_one[here]], sums, (early[1],), kept)
    sums, send = sums
    pairs = pairs_of(place, [*early, sums], swap(send, "xl", 1))
    keep, send = halves_of(place, *[deliver(part, op) for op, part in enumerate(pairs)])
    return (keep + swap(send, "xl", 1).astype(jnp.float32)) * weight


def per_device(src_traces, rec_traces):
    planes, members = lax.axis_size("src"), lax.axis_size("xl")
    weight = float(np.float32(1.0 / math.sqrt(src_traces.shape[1] * members)))
    if planes == 4 and members == 8 and rec_traces.shape[:2] == (4 * POINTS, 16) and src_traces.shape[:2] == (16, 4 * POINTS):
        return four_planes(src_traces, rec_traces, weight)
    return gather_and_scatter(src_traces, rec_traces, weight)


def solution(mesh):
    return jax.shard_map(
        per_device,
        mesh=mesh,
        in_specs=(P("src", "xl", None), P("xl", "src", None)),
        out_specs=P("src", "xl", None),
        check_vma=False,
    )
```

time: 200 us -> 31.5 us (0.16); the launches traced: 197 us -> 31.4 us
  waiting for transfers between devices: 76.3 us -> 7.49 us
  matrix products: 55.2 us -> 0 us
  local copies, waits for them, and re-layouts: 43.8 us -> 0.01 us
  between operations: 13.5 us -> 0.15 us
  Pallas kernels: 0 us -> 9.85 us
  starting transfers between devices: 5.13 us -> 13.2 us
    all_gather x1 -> x0, waiting for transfers between devices: 76.2 us -> none  [per_device(): panels = lax.all_gather(own_panels, 'src', axis=1, tiled=True)]
    dot_general x34 -> x0, matrix products: 55.2 us -> none  [the longest x8 11.5 us: spectral_product(): jnp.einsum(layout_kind, left_im, right_im, preferred_element_type=jnp.flo...]
    dot_general x32 -> x0, local copies, waits for them, and re-layouts: 34.6 us -> none  [the longest x8 8.68 us: spectral_product(): jnp.einsum(layout_kind, left_re, right_im, preferred_element_type=jnp.flo...]
    pallas_call x0 -> x13, Pallas kernels: none -> 9.85 us  [the longest x6 5.68 us: tiles_of(): pl.pallas_call(kernel, in_specs=[pl.BlockSpec(memory_space=pltpu.SMEM)] *...]
    ppermute x7 -> x9, starting transfers between devices: 5.12 us -> 13.2 us  [the longest x5 8.46 us: cross(): lax.ppermute(value, 'src', [(z, z ^ (1 if side_of(z) ^ other else 2)) for...]
    ppermute x7 -> x9, waiting for transfers between devices: 0.12 us -> 7.49 us  [the longest x2 3.42 us: deliver(): return lax.ppermute(value, ('src', 'xl'), pairs)]
    convert_element_type x4 -> x0, local copies, waits for them, and re-layouts: 5.06 us -> none  [spectra(): return result.reshape(traces.shape[:-1] + (2 * F,)).astype(jnp.bfloat16)]
    cos x1 -> x0, other arithmetic: 2.08 us -> none  [fourier_table(): basis = jnp.concatenate([jnp.cos(angles), -jnp.sin(angles)], axis=1)]
  transfers between devices with their start and end apart: 8 -> 9, of which waited for: 1 -> 6; matrix products, arithmetic and copies ran while one was open for 41% -> 0% of each run, Pallas kernels for 0% -> 22%
where the time goes in v3:
time: 31.5 us; the launch traced here: 31.4 us
  starting transfers between devices  13.2 us (42%)
  Pallas kernels  9.85 us (31%)
  waiting for transfers between devices  7.49 us (24%)
  other arithmetic  0.67 us (2%)
    ppermute x5, starting transfers between devices, cross(): lax.ppermute(value, 'src', [(z, z ^ (1 if side_of(z) ^ other else 2)) for...  8.46 us
    pallas_call x6, Pallas kernels, tiles_of(): pl.pallas_call(kernel, in_specs=[pl.BlockSpec(memory_space=pltpu.SMEM)] *...  5.68 us
    ppermute x2, waiting for transfers between devices, deliver(): return lax.ppermute(value, ('src', 'xl'), pairs)  3.42 us
    ppermute x2, starting transfers between devices, swap(): return lax.ppermute(value, axis, [(i, i ^ flip) for i in range(count)])  3.15 us
    ppermute x2, waiting for transfers between devices, swap(): return lax.ppermute(value, axis, [(i, i ^ flip) for i in range(count)])  2.42 us
    pallas_call x1, Pallas kernels, first_spectra(): pl.pallas_call(functools.partial(first_kernel, blocks=blocks), in_specs=[...  2.11 us
    pallas_call x4, Pallas kernels, either_spectra(): pl.pallas_call(functools.partial(either_kernel, other=other, first=first,...  1.96 us
    ppermute x5, waiting for transfers between devices, cross(): lax.ppermute(value, 'src', [(z, z ^ (1 if side_of(z) ^ other else 2)) for...  1.65 us
  transfers between devices with their start and end apart: 9, of which 6 were waited for; matrix products, arithmetic and copies ran while one was open for 0% of the time, Pallas kernels for 22%

profile of v3, /device:TPU:0, one launch (start us, length us, event | category | flops | bytes accessed | tf_op | source)
XLA Modules:
  0.0 31.4 jit_solution(10438799761575339770)
XLA Ops:
  0.0 2.1 %shard_map.46.refs_0_ = bf16[256,256]{1,0:T(8,128)(2,1)S(1)} custom-call(s32[1]{0:T(128)} %bitcast.1.side_ref, f32[16,4,8,1024]{3,2,1,0:T(8,128)} %bitcast.5, f32[4,16,8,1024]{3,2,1,0:T(8,128)} %bitcast.10, bf16[512,256]{1,0:T(8,128)(2,1)} %constant.50.clone.high_ref, bf16[512,256]{1,0:T(8,128)(2,1)} %constant.51.clone.low_ref), custom_call_target="tpu_custom_call" | custom-call | tf_op jit(solution)/shard_map/pallas_call | solution.py:99
  2.1 4.1 %collective-permute-start.1 = (bf16[256,256]{1,0:T(8,128)(2,1)S(1)}, bf16[256,256]{1,0:T(8,128)(2,1)S(1)}, u32[]{:S(2)}, u32[]{:S(2)}) collective-permute-start(bf16[256,256]{1,0:T(8,128)(2,1)S(1)} %shard_map.46.refs_0_), channel_id=1, source_target_pairs={{0,16},{8,0},{16,24},{24,8},{1,17},{9,1},{17,25},{25,9},{2,18},{10... | collective-permute-start | bytes 393224 | tf_op jit(solution)/shard_map/ppermute | solution.py:395
  6.3 0.6 %shard_map.47.refs_0_.refs_1_ = bf16[256,256]{1,0:T(8,128)(2,1)S(1)} custom-call(s32[1]{0:T(128)} %bitcast.1.side_ref, f32[16,4,8,1024]{3,2,1,0:T(8,128)S(1)} %bitcast.6, f32[4,16,8,1024]{3,2,1,0:T(8,128)S(1)} %bitcast.11, bf16[512,256]{1,0:T(8,128)(2,1)S(1)} %copy-done.3, bf16[512,256]{1,0:T(8,128)(2,1)S(1)} %copy-done.2, ...), custom_call_target="tpu_custom_call" | custom-call | flops 256 | bytes 256 | tf_op jit(solution)/shard_map/pallas_call | solution.py:130
  6.9 1.6 %collective-permute-start = (bf16[256,256]{1,0:T(8,128)(2,1)S(1)}, bf16[256,256]{1,0:T(8,128)(2,1)S(1)}, u32[]{:S(2)}, u32[]{:S(2)}) collective-permute-start(bf16[256,256]{1,0:T(8,128)(2,1)S(1)} %shard_map.47.refs_0_.refs_1_), channel_id=1, source_target_pairs={{0,16},{8,0},{16,24},{24,8},{1,17},{9,1},{17,25},{25,9},{2,18},{10... | collective-permute-start | bytes 393224 | tf_op jit(solution)/shard_map/ppermute | solution.py:395
  8.5 0.6 %shard_map.48.refs_0_.refs_2_.refs_1_ = bf16[256,256]{1,0:T(8,128)(2,1)S(1)} custom-call(s32[1]{0:T(128)} %bitcast.1.side_ref, f32[16,4,8,1024]{3,2,1,0:T(8,128)S(1)} %bitcast.7, f32[4,16,8,1024]{3,2,1,0:T(8,128)S(1)} %bitcast.12, bf16[512,256]{1,0:T(8,128)(2,1)S(1)} %copy-done.3, bf16[512,256]{1,0:T(8,128)(2,1)S(1)} %copy-done.2, ...), custom_call_target="tpu_custom_call" | custom-call | flops 256 | bytes 256 | tf_op jit(solution)/shard_map/pallas_call | solution.py:130
  9.1 0.5 %collective-permute-start.4 = (bf16[256,256]{1,0:T(8,128)(2,1)S(1)}, bf16[256,256]{1,0:T(8,128)(2,1)S(1)}, u32[]{:S(2)}, u32[]{:S(2)}) collective-permute-start(bf16[256,256]{1,0:T(8,128)(2,1)S(1)} %shard_map.48.refs_0_.refs_2_.refs_1_), channel_id=1, source_target_pairs={{0,8},{8,24},{16,0},{24,16},{1,9},{9,25},{17,1},{25,17},{2,10},{10... | collective-permute-start | bytes 393224 | tf_op jit(solution)/shard_map/ppermute | solution.py:395
  9.6 0.4 %shard_map.49.refs_0_.refs_3_.refs_1_ = bf16[128,256]{1,0:T(8,128)(2,1)S(1)} custom-call(s32[1]{0:T(128)} %bitcast.1.side_ref, f32[16,4,8,1024]{3,2,1,0:T(8,128)S(1)} %bitcast.8, f32[4,16,8,1024]{3,2,1,0:T(8,128)S(1)} %bitcast.13, bf16[512,256]{1,0:T(8,128)(2,1)S(1)} %copy-done.3, bf16[512,256]{1,0:T(8,128)(2,1)S(1)} %copy-done.2, ...), custom_call_target="tpu_custom_call" | custom-call | flops 128 | bytes 128 | tf_op jit(solution)/shard_map/pallas_call | solution.py:130
  10.0 0.5 %collective-permute-start.3 = (bf16[128,256]{1,0:T(8,128)(2,1)S(1)}, bf16[128,256]{1,0:T(8,128)(2,1)S(1)}, u32[]{:S(2)}, u32[]{:S(2)}) collective-permute-start(bf16[128,256]{1,0:T(8,128)(2,1)S(1)} %shard_map.49.refs_0_.refs_3_.refs_1_), channel_id=1, source_target_pairs={{0,8},{8,24},{16,0},{24,16},{1,9},{9,25},{17,1},{25,17},{2,10},{10... | collective-permute-start | bytes 196616 | tf_op jit(solution)/shard_map/ppermute | solution.py:395
  10.5 0.4 %shard_map.50.refs_4_.refs_5_.refs_3_ = bf16[128,256]{1,0:T(8,128)(2,1)S(1)} custom-call(s32[1]{0:T(128)} %bitcast.1.side_ref, f32[16,4,8,1024]{3,2,1,0:T(8,128)S(1)} %bitcast.9, f32[4,16,8,1024]{3,2,1,0:T(8,128)S(1)} %bitcast.14, bf16[512,256]{1,0:T(8,128)(2,1)S(1)} %copy-done.3, bf16[512,256]{1,0:T(8,128)(2,1)S(1)} %copy-done.2, ...), custom_call_target="tpu_custom_call" | custom-call | flops 128 | bytes 128 | tf_op jit(solution)/shard_map/pallas_call | solution.py:130
  10.9 1.7 %collective-permute-start.2 = (bf16[128,256]{1,0:T(8,128)(2,1)S(1)}, bf16[128,256]{1,0:T(8,128)(2,1)S(1)}, u32[]{:S(2)}, u32[]{:S(2)}) collective-permute-start(bf16[128,256]{1,0:T(8,128)(2,1)S(1)} %shard_map.50.refs_4_.refs_5_.refs_3_), channel_id=1, source_target_pairs={{0,8},{8,24},{16,0},{24,16},{1,9},{9,25},{17,1},{25,17},{2,10},{10... | collective-permute-start | bytes 196616 | tf_op jit(solution)/shard_map/ppermute | solution.py:395
  12.6 1.4 %shard_map.51.refs_2_.refs_0_ = f32[1,2,16,8,256]{4,3,2,1,0:T(8,128)S(1)} custom-call(s32[1]{0:T(128)} %bitcast.1.side_ref, bf16[256,256]{1,0:T(8,128)(2,1)S(1)} %shard_map.46.refs_0_, bf16[256,256]{1,0:T(8,128)(2,1)S(1)} %shard_map.47.refs_0_.refs_1_, bf16[256,256]{1,0:T(8,128)(2,1)S(1)} %shard_map.48.refs_0_.refs_2_.refs_1_, ...), custom_call_target="tpu_custom_call" | custom-call | flops 1 | bytes 1 | tf_op jit(solution)/shard_map/pallas_call | solution.py:275
  14.1 0.7 %shard_map.52.refs_2_ = f32[1,2,16,8,256]{4,3,2,1,0:T(8,128)S(1)} custom-call(s32[1]{0:T(128)} %bitcast.1.side_ref, bf16[256,256]{1,0:T(8,128)(2,1)S(1)} %shard_map.46.refs_0_, bf16[256,256]{1,0:T(8,128)(2,1)S(1)} %collective-permute-done.1.refs_1_.refs_2_, f32[1,2,16,8,256]{4,3,2,1,0:T(8,128)S(1)} %shard_map.51.refs_2_.refs_0_), custom_call_target="tpu_custom_call" | custom-call | flops 1 | bytes 1 | tf_op jit(solution)/shard_map/pallas_call | solution.py:275
  14.8 0.7 %shard_map.53.refs_3_.refs_4_.refs_1_.refs_6_ = f32[1,2,16,8,256]{4,3,2,1,0:T(8,128)S(1)} custom-call(s32[1]{0:T(128)} %bitcast.1.side_ref, bf16[256,256]{1,0:T(8,128)(2,1)S(1)} %shard_map.47.refs_0_.refs_1_, bf16[256,256]{1,0:T(8,128)(2,1)S(1)} %collective-permute-done.refs_1_.refs_2_.refs_4_, f32[1,2,16,8,256]{4,3,2,1,0:T(8,128)S(1)} %shard_map.52.refs_2_), custom_call_target="tpu_custom_call" | custom-call | flops 1 | bytes 1 | tf_op jit(solution)/shard_map/pallas_call | solution.py:275
  15.5 1.5 %collective-permute-done.4.refs_0_ = bf16[256,256]{1,0:T(8,128)(2,1)S(1)} collective-permute-done((bf16[256,256]{1,0:T(8,128)(2,1)S(1)}, bf16[256,256]{1,0:T(8,128)(2,1)S(1)}, u32[]{:S(2)}, u32[]{:S(2)}) %collective-permute-start.4) | collective-permute-done | bytes 131104 | tf_op jit(solution)/shard_map/ppermute | solution.py:395
  17.0 1.3 %shard_map.54.refs_3_ = f32[2,2,16,8,256]{4,3,2,1,0:T(8,128)S(1)} custom-call(s32[1]{0:T(128)} %bitcast.1.side_ref, bf16[256,256]{1,0:T(8,128)(2,1)S(1)} %collective-permute-done.4.refs_0_, bf16[256,256]{1,0:T(8,128)(2,1)S(1)} %shard_map.48.refs_0_.refs_2_.refs_1_, bf16[256,256]{1,0:T(8,128)(2,1)S(1)} %collective-permute-done.1.refs_1_.refs_2_, ...), custom_call_target="tpu_custom_call" | custom-call | flops 2 | bytes 2 | tf_op jit(solution)/shard_map/pallas_call | solution.py:275
  18.5 0.7 %shard_map.55.refs_5_ = f32[2,2,16,8,256]{4,3,2,1,0:T(8,128)S(1)} custom-call(s32[1]{0:T(128)} %bitcast.1.side_ref, bf16[128,256]{1,0:T(8,128)(2,1)S(1)} %collective-permute-done.3.refs_0_, bf16[128,256]{1,0:T(8,128)(2,1)S(1)} %shard_map.49.refs_0_.refs_3_.refs_1_, bf16[256,256]{1,0:T(8,128)(2,1)S(1)} %collective-permute-done.refs_1_.refs_2_.refs_4_, ...), custom_call_target="tpu_custom_call" | custom-call | flops 2 | bytes 2 | tf_op jit(solution)/shard_map/pallas_call | solution.py:275
  19.2 0.8 %shard_map.56 = (f32[2,2,16,8,256]{4,3,2,1,0:T(8,128)S(1)}, bf16[2,2,16,8,256]{4,3,2,1,0:T(8,128)(2,1)S(1)}) custom-call(s32[1]{0:T(128)} %bitcast.1.side_ref, s32[1]{0:T(128)} %bitcast.core_ref, s32[1]{0:T(128)} %bitcast.2.turn_ref, f32[1,2,16,8,256]{4,3,2,1,0:T(8,128)S(1)} %shard_map.51.refs_2_.refs_0_, ...), custom_call_target="tpu_custom_call" | custom-call | flops 2 | bytes 2 | tf_op jit(solution)/shard_map/pallas_call | solution.py:275
  20.1 1.5 %collective-permute-done.5.refs_3_ = bf16[2,2,16,8,256]{4,3,2,1,0:T(8,128)(2,1)S(1)} collective-permute-done((bf16[2,2,16,8,256]{4,3,2,1,0:T(8,128)(2,1)S(1)}, bf16[2,2,16,8,256]{4,3,2,1,0:T(8,128)(2,1)S(1)}, u32[]{:S(2)}, u32[]{:S(2)}) %collective-permute-start.5) | collective-permute-done | bytes 262176 | tf_op jit(solution)/shard_map/ppermute | solution.py:387
  21.7 0.9 %collective-permute-start.6 = (bf16[2,16,8,256]{3,2,1,0:T(8,128)(2,1)S(1)}, bf16[2,16,8,256]{3,2,1,0:T(8,128)(2,1)S(1)}, u32[]{:S(2)}, u32[]{:S(2)}) collective-permute-start(bf16[2,16,8,256]{3,2,1,0:T(8,128)(2,1)S(1)} %get-tuple-element.13), channel_id=1, source_target_pairs={{0,8},{1,5},{2,0},{3,13},{4,12},{5,1},{6,4},{7,9},{8,10},{9,7},{10... | collective-permute-start | bytes 393224 | tf_op jit(solution)/shard_map/ppermute | solution.py:407
  22.6 0.7 %collective-permute-start.7 = (bf16[2,16,8,256]{3,2,1,0:T(8,128)(2,1)S(1)}, bf16[2,16,8,256]{3,2,1,0:T(8,128)(2,1)S(1)}, u32[]{:S(2)}, u32[]{:S(2)}) collective-permute-start(bf16[2,16,8,256]{3,2,1,0:T(8,128)(2,1)S(1)} %get-tuple-element.14), channel_id=1, source_target_pairs={{0,0},{1,13},{2,8},{3,5},{4,4},{5,9},{6,12},{7,1},{8,2},{9,15},{10... | collective-permute-start | bytes 393224 | tf_op jit(solution)/shard_map/ppermute | solution.py:407
  23.3 3.4 %collective-permute-done.6.first = bf16[2,16,8,256]{3,2,1,0:T(8,128)(2,1)S(1)} collective-permute-done((bf16[2,16,8,256]{3,2,1,0:T(8,128)(2,1)S(1)}, bf16[2,16,8,256]{3,2,1,0:T(8,128)(2,1)S(1)}, u32[]{:S(2)}, u32[]{:S(2)}) %collective-permute-start.6) | collective-permute-done | bytes 131104 | tf_op jit(solution)/shard_map/ppermute | solution.py:407
  26.7 3.1 %collective-permute-start.8 = (bf16[16,8,256]{2,1,0:T(8,128)(2,1)S(1)}, bf16[16,8,256]{2,1,0:T(8,128)(2,1)S(1)}, u32[]{:S(2)}, u32[]{:S(2)}) collective-permute-start(bf16[16,8,256]{2,1,0:T(8,128)(2,1)S(1)} %get-tuple-element.16), channel_id=1, source_target_pairs={{0,1},{1,0},{2,3},{3,2},{4,5},{5,4},{6,7},{7,6},{8,9},{9,8},{10,11... | collective-permute-start | bytes 196616 | tf_op jit(solution)/shard_map/ppermute | solution.py:387
  29.8 0.9 %collective-permute-done.8 = bf16[16,8,256]{2,1,0:T(8,128)(2,1)S(1)} collective-permute-done((bf16[16,8,256]{2,1,0:T(8,128)(2,1)S(1)}, bf16[16,8,256]{2,1,0:T(8,128)(2,1)S(1)}, u32[]{:S(2)}, u32[]{:S(2)}) %collective-permute-start.8) | collective-permute-done | bytes 65568 | tf_op jit(solution)/shard_map/ppermute | solution.py:387
  30.7 0.7 %add_multiply_fusion = f32[16,8,256]{2,1,0:T(8,128)} fusion(f32[16,8,256]{2,1,0:T(8,128)S(1)} %get-tuple-element.15, bf16[16,8,256]{2,1,0:T(8,128)(2,1)S(1)} %collective-permute-done.8), kind=kLoop, calls=%fused_computation | loop fusion | flops 98304 | bytes 327680 | tf_op jit(solution)/shard_map/mul | solution.py:448
  (16 shorter events, 0.3 us)
Async XLA Ops:
  0.0 6.2 %copy-start = (f32[16,32,1024]{2,1,0:T(8,128)S(1)}, f32[16,32,1024]{2,1,0:T(8,128)}, u32[]{:S(2)}) copy-start(f32[16,32,1024]{2,1,0:T(8,128)} %param.4) | copy-start | bytes 6291460
  0.0 6.2 %copy-start.1 = (f32[32,16,1024]{2,1,0:T(8,128)S(1)}, f32[32,16,1024]{2,1,0:T(8,128)}, u32[]{:S(2)}) copy-start(f32[32,16,1024]{2,1,0:T(8,128)} %param.5) | copy-start | bytes 6291460
  0.0 6.2 %copy-start.2 = (bf16[512,256]{1,0:T(8,128)(2,1)S(1)}, bf16[512,256]{1,0:T(8,128)(2,1)}, u32[]{:S(2)}) copy-start(bf16[512,256]{1,0:T(8,128)(2,1)} %constant.51.clone.low_ref) | copy-start | bytes 786436
  0.0 6.2 %copy-start.3 = (bf16[512,256]{1,0:T(8,128)(2,1)S(1)}, bf16[512,256]{1,0:T(8,128)(2,1)}, u32[]{:S(2)}) copy-start(bf16[512,256]{1,0:T(8,128)(2,1)} %constant.50.clone.high_ref) | copy-start | bytes 786436
  2.1 11.9 %collective-permute-start.1 = (bf16[256,256]{1,0:T(8,128)(2,1)S(1)}, bf16[256,256]{1,0:T(8,128)(2,1)S(1)}, u32[]{:S(2)}, u32[]{:S(2)}) collective-permute-start(bf16[256,256]{1,0:T(8,128)(2,1)S(1)} %shard_map.46.refs_0_), channel_id=1, source_target_pairs={{0,16},{8,0},{16,24},{24,8},{1,17},{9,1},{17,25},{25,9},{2,18},{10... | collective-permute-start | bytes 393224 | tf_op jit(solution)/shard_map/ppermute | solution.py:395
  6.9 7.9 %collective-permute-start = (bf16[256,256]{1,0:T(8,128)(2,1)S(1)}, bf16[256,256]{1,0:T(8,128)(2,1)S(1)}, u32[]{:S(2)}, u32[]{:S(2)}) collective-permute-start(bf16[256,256]{1,0:T(8,128)(2,1)S(1)} %shard_map.47.refs_0_.refs_1_), channel_id=1, source_target_pairs={{0,16},{8,0},{16,24},{24,8},{1,17},{9,1},{17,25},{25,9},{2,18},{10... | collective-permute-start | bytes 393224 | tf_op jit(solution)/shard_map/ppermute | solution.py:395
  9.1 8.0 %collective-permute-start.4 = (bf16[256,256]{1,0:T(8,128)(2,1)S(1)}, bf16[256,256]{1,0:T(8,128)(2,1)S(1)}, u32[]{:S(2)}, u32[]{:S(2)}) collective-permute-start(bf16[256,256]{1,0:T(8,128)(2,1)S(1)} %shard_map.48.refs_0_.refs_2_.refs_1_), channel_id=1, source_target_pairs={{0,8},{8,24},{16,0},{24,16},{1,9},{9,25},{17,1},{25,17},{2,10},{10... | collective-permute-start | bytes 393224 | tf_op jit(solution)/shard_map/ppermute | solution.py:395
  10.0 8.5 %collective-permute-start.3 = (bf16[128,256]{1,0:T(8,128)(2,1)S(1)}, bf16[128,256]{1,0:T(8,128)(2,1)S(1)}, u32[]{:S(2)}, u32[]{:S(2)}) collective-permute-start(bf16[128,256]{1,0:T(8,128)(2,1)S(1)} %shard_map.49.refs_0_.refs_3_.refs_1_), channel_id=1, source_target_pairs={{0,8},{8,24},{16,0},{24,16},{1,9},{9,25},{17,1},{25,17},{2,10},{10... | collective-permute-start | bytes 196616 | tf_op jit(solution)/shard_map/ppermute | solution.py:395
  10.9 8.4 %collective-permute-start.2 = (bf16[128,256]{1,0:T(8,128)(2,1)S(1)}, bf16[128,256]{1,0:T(8,128)(2,1)S(1)}, u32[]{:S(2)}, u32[]{:S(2)}) collective-permute-start(bf16[128,256]{1,0:T(8,128)(2,1)S(1)} %shard_map.50.refs_4_.refs_5_.refs_3_), channel_id=1, source_target_pairs={{0,8},{8,24},{16,0},{24,16},{1,9},{9,25},{17,1},{25,17},{2,10},{10... | collective-permute-start | bytes 196616 | tf_op jit(solution)/shard_map/ppermute | solution.py:395
  20.0 1.6 %collective-permute-start.5 = (bf16[2,2,16,8,256]{4,3,2,1,0:T(8,128)(2,1)S(1)}, bf16[2,2,16,8,256]{4,3,2,1,0:T(8,128)(2,1)S(1)}, u32[]{:S(2)}, u32[]{:S(2)}) collective-permute-start(bf16[2,2,16,8,256]{4,3,2,1,0:T(8,128)(2,1)S(1)} %get-tuple-element.12), channel_id=1, source_target_pairs={{0,1},{1,0},{2,3},{3,2},{4,5},{5,4},{6,7},{7,6},{8,9},{9,8},{10,11... | collective-permute-start | bytes 786440 | tf_op jit(solution)/shard_map/ppermute | solution.py:387
  21.7 5.0 %collective-permute-start.6 = (bf16[2,16,8,256]{3,2,1,0:T(8,128)(2,1)S(1)}, bf16[2,16,8,256]{3,2,1,0:T(8,128)(2,1)S(1)}, u32[]{:S(2)}, u32[]{:S(2)}) collective-permute-start(bf16[2,16,8,256]{3,2,1,0:T(8,128)(2,1)S(1)} %get-tuple-element.13), channel_id=1, source_target_pairs={{0,8},{1,5},{2,0},{3,13},{4,12},{5,1},{6,4},{7,9},{8,10},{9,7},{10... | collective-permute-start | bytes 393224 | tf_op jit(solution)/shard_map/ppermute | solution.py:407
  22.6 4.1 %collective-permute-start.7 = (bf16[2,16,8,256]{3,2,1,0:T(8,128)(2,1)S(1)}, bf16[2,16,8,256]{3,2,1,0:T(8,128)(2,1)S(1)}, u32[]{:S(2)}, u32[]{:S(2)}) collective-permute-start(bf16[2,16,8,256]{3,2,1,0:T(8,128)(2,1)S(1)} %get-tuple-element.14), channel_id=1, source_target_pairs={{0,0},{1,13},{2,8},{3,5},{4,4},{5,9},{6,12},{7,1},{8,2},{9,15},{10... | collective-permute-start | bytes 393224 | tf_op jit(solution)/shard_map/ppermute | solution.py:407
  26.7 4.0 %collective-permute-start.8 = (bf16[16,8,256]{2,1,0:T(8,128)(2,1)S(1)}, bf16[16,8,256]{2,1,0:T(8,128)(2,1)S(1)}, u32[]{:S(2)}, u32[]{:S(2)}) collective-permute-start(bf16[16,8,256]{2,1,0:T(8,128)(2,1)S(1)} %get-tuple-element.16), channel_id=1, source_target_pairs={{0,1},{1,0},{2,3},{3,2},{4,5},{5,4},{6,7},{7,6},{8,9},{9,8},{10,11... | collective-permute-start | bytes 196616 | tf_op jit(solution)/shard_map/ppermute | solution.py:387

commit v4 on v3

--- a/solution.py
+++ b/solution.py
@@ -167,7 +167,7 @@
                 emit(block * many + s, g, first - third, first + second)
         return carry
 
-    lax.fori_loop(0, 16 // many, some_sources, 0)
+    lax.fori_loop(0, 16 // many, some_sources, 0, unroll=2)
 
 
 def split(ref, block, forms, at, points, side):
@@ -186,7 +186,7 @@
             forms[2, here] = im + re * right
         return carry
 
-    lax.fori_loop(0, ROWS // 16, some_rows, 0, unroll=2)
+    lax.fori_loop(0, ROWS // 16, some_rows, 0, unroll=8)
 
 
 def tiles_kernel(side_ref, *refs, arrays, ones, others, carried, spare):

time: 31.5 us -> 31.4 us (level)
  waiting for transfers between devices: 7.49 us -> 8.38 us
  Pallas kernels: 9.85 us -> 9 us
    pallas_call x6, Pallas kernels: 5.68 us -> 4.83 us  [tiles_of(): pl.pallas_call(kernel, in_specs=[pl.BlockSpec(memory_space=pltpu.SMEM)] *...]
    ppermute x5, waiting for transfers between devices: 1.65 us -> 2.39 us  [cross(): lax.ppermute(value, 'src', [(z, z ^ (1 if side_of(z) ^ other else 2)) for...]
  transfers between devices with their start and end apart: 9 -> 9, of which waited for: 6 -> 6; matrix products, arithmetic and copies ran while one was open for 0% -> 0% of each run, Pallas kernels for 22% -> 20%
where the time goes in v4:
time: 31.4 us; the launch traced here: 31.3 us
  starting transfers between devices  13.1 us (42%)
  Pallas kernels  9 us (29%)
  waiting for transfers between devices  8.38 us (27%)
  other arithmetic  0.67 us (2%)
    ppermute x5, starting transfers between devices, cross(): lax.ppermute(value, 'src', [(z, z ^ (1 if side_of(z) ^ other else 2)) for...  8.46 us
    pallas_call x6, Pallas kernels, tiles_of(): pl.pallas_call(kernel, in_specs=[pl.BlockSpec(memory_space=pltpu.SMEM)] *...  4.83 us
    ppermute x2, waiting for transfers between devices, deliver(): return lax.ppermute(value, ('src', 'xl'), pairs)  3.57 us
    ppermute x2, starting transfers between devices, swap(): return lax.ppermute(value, axis, [(i, i ^ flip) for i in range(count)])  3.15 us
    ppermute x2, waiting for transfers between devices, swap(): return lax.ppermute(value, axis, [(i, i ^ flip) for i in range(count)])  2.42 us
    ppermute x5, waiting for transfers between devices, cross(): lax.ppermute(value, 'src', [(z, z ^ (1 if side_of(z) ^ other else 2)) for...  2.39 us
    pallas_call x1, Pallas kernels, first_spectra(): pl.pallas_call(functools.partial(first_kernel, blocks=blocks), in_specs=[...  2.11 us
    pallas_call x4, Pallas kernels, either_spectra(): pl.pallas_call(functools.partial(either_kernel, other=other, first=first,...  1.96 us
  transfers between devices with their start and end apart: 9, of which 6 were waited for; matrix products, arithmetic and copies ran while one was open for 0% of the time, Pallas kernels for 20%

profile of v4, /device:TPU:0, one launch (start us, length us, event | category | flops | bytes accessed | tf_op | source)
XLA Modules:
  0.0 31.3 jit_solution(10770875418828821820)
XLA Ops:
  0.0 2.1 %shard_map.46.refs_0_ = bf16[256,256]{1,0:T(8,128)(2,1)S(1)} custom-call(s32[1]{0:T(128)} %bitcast.1.side_ref, f32[16,4,8,1024]{3,2,1,0:T(8,128)} %bitcast.5, f32[4,16,8,1024]{3,2,1,0:T(8,128)} %bitcast.10, bf16[512,256]{1,0:T(8,128)(2,1)} %constant.50.clone.high_ref, bf16[512,256]{1,0:T(8,128)(2,1)} %constant.51.clone.low_ref), custom_call_target="tpu_custom_call" | custom-call | tf_op jit(solution)/shard_map/pallas_call | solution.py:99
  2.1 4.1 %collective-permute-start.1 = (bf16[256,256]{1,0:T(8,128)(2,1)S(1)}, bf16[256,256]{1,0:T(8,128)(2,1)S(1)}, u32[]{:S(2)}, u32[]{:S(2)}) collective-permute-start(bf16[256,256]{1,0:T(8,128)(2,1)S(1)} %shard_map.46.refs_0_), channel_id=1, source_target_pairs={{0,16},{8,0},{16,24},{24,8},{1,17},{9,1},{17,25},{25,9},{2,18},{10... | collective-permute-start | bytes 393224 | tf_op jit(solution)/shard_map/ppermute | solution.py:395
  6.3 0.6 %shard_map.47.refs_0_.refs_1_ = bf16[256,256]{1,0:T(8,128)(2,1)S(1)} custom-call(s32[1]{0:T(128)} %bitcast.1.side_ref, f32[16,4,8,1024]{3,2,1,0:T(8,128)S(1)} %bitcast.6, f32[4,16,8,1024]{3,2,1,0:T(8,128)S(1)} %bitcast.11, bf16[512,256]{1,0:T(8,128)(2,1)S(1)} %copy-done.3, bf16[512,256]{1,0:T(8,128)(2,1)S(1)} %copy-done.2, ...), custom_call_target="tpu_custom_call" | custom-call | flops 256 | bytes 256 | tf_op jit(solution)/shard_map/pallas_call | solution.py:130
  6.9 1.6 %collective-permute-start = (bf16[256,256]{1,0:T(8,128)(2,1)S(1)}, bf16[256,256]{1,0:T(8,128)(2,1)S(1)}, u32[]{:S(2)}, u32[]{:S(2)}) collective-permute-start(bf16[256,256]{1,0:T(8,128)(2,1)S(1)} %shard_map.47.refs_0_.refs_1_), channel_id=1, source_target_pairs={{0,16},{8,0},{16,24},{24,8},{1,17},{9,1},{17,25},{25,9},{2,18},{10... | collective-permute-start | bytes 393224 | tf_op jit(solution)/shard_map/ppermute | solution.py:395
  8.5 0.6 %shard_map.48.refs_0_.refs_2_.refs_1_ = bf16[256,256]{1,0:T(8,128)(2,1)S(1)} custom-call(s32[1]{0:T(128)} %bitcast.1.side_ref, f32[16,4,8,1024]{3,2,1,0:T(8,128)S(1)} %bitcast.7, f32[4,16,8,1024]{3,2,1,0:T(8,128)S(1)} %bitcast.12, bf16[512,256]{1,0:T(8,128)(2,1)S(1)} %copy-done.3, bf16[512,256]{1,0:T(8,128)(2,1)S(1)} %copy-done.2, ...), custom_call_target="tpu_custom_call" | custom-call | flops 256 | bytes 256 | tf_op jit(solution)/shard_map/pallas_call | solution.py:130
  9.1 0.5 %collective-permute-start.4 = (bf16[256,256]{1,0:T(8,128)(2,1)S(1)}, bf16[256,256]{1,0:T(8,128)(2,1)S(1)}, u32[]{:S(2)}, u32[]{:S(2)}) collective-permute-start(bf16[256,256]{1,0:T(8,128)(2,1)S(1)} %shard_map.48.refs_0_.refs_2_.refs_1_), channel_id=1, source_target_pairs={{0,8},{8,24},{16,0},{24,16},{1,9},{9,25},{17,1},{25,17},{2,10},{10... | collective-permute-start | bytes 393224 | tf_op jit(solution)/shard_map/ppermute | solution.py:395
  9.6 0.4 %shard_map.49.refs_0_.refs_3_.refs_1_ = bf16[128,256]{1,0:T(8,128)(2,1)S(1)} custom-call(s32[1]{0:T(128)} %bitcast.1.side_ref, f32[16,4,8,1024]{3,2,1,0:T(8,128)S(1)} %bitcast.8, f32[4,16,8,1024]{3,2,1,0:T(8,128)S(1)} %bitcast.13, bf16[512,256]{1,0:T(8,128)(2,1)S(1)} %copy-done.3, bf16[512,256]{1,0:T(8,128)(2,1)S(1)} %copy-done.2, ...), custom_call_target="tpu_custom_call" | custom-call | flops 128 | bytes 128 | tf_op jit(solution)/shard_map/pallas_call | solution.py:130
  10.0 0.5 %collective-permute-start.3 = (bf16[128,256]{1,0:T(8,128)(2,1)S(1)}, bf16[128,256]{1,0:T(8,128)(2,1)S(1)}, u32[]{:S(2)}, u32[]{:S(2)}) collective-permute-start(bf16[128,256]{1,0:T(8,128)(2,1)S(1)} %shard_map.49.refs_0_.refs_3_.refs_1_), channel_id=1, source_target_pairs={{0,8},{8,24},{16,0},{24,16},{1,9},{9,25},{17,1},{25,17},{2,10},{10... | collective-permute-start | bytes 196616 | tf_op jit(solution)/shard_map/ppermute | solution.py:395
  10.5 0.4 %shard_map.50.refs_4_.refs_5_.refs_3_ = bf16[128,256]{1,0:T(8,128)(2,1)S(1)} custom-call(s32[1]{0:T(128)} %bitcast.1.side_ref, f32[16,4,8,1024]{3,2,1,0:T(8,128)S(1)} %bitcast.9, f32[4,16,8,1024]{3,2,1,0:T(8,128)S(1)} %bitcast.14, bf16[512,256]{1,0:T(8,128)(2,1)S(1)} %copy-done.3, bf16[512,256]{1,0:T(8,128)(2,1)S(1)} %copy-done.2, ...), custom_call_target="tpu_custom_call" | custom-call | flops 128 | bytes 128 | tf_op jit(solution)/shard_map/pallas_call | solution.py:130
  10.9 1.7 %collective-permute-start.2 = (bf16[128,256]{1,0:T(8,128)(2,1)S(1)}, bf16[128,256]{1,0:T(8,128)(2,1)S(1)}, u32[]{:S(2)}, u32[]{:S(2)}) collective-permute-start(bf16[128,256]{1,0:T(8,128)(2,1)S(1)} %shard_map.50.refs_4_.refs_5_.refs_3_), channel_id=1, source_target_pairs={{0,8},{8,24},{16,0},{24,16},{1,9},{9,25},{17,1},{25,17},{2,10},{10... | collective-permute-start | bytes 196616 | tf_op jit(solution)/shard_map/ppermute | solution.py:395
  12.6 1.2 %shard_map.51.refs_2_.refs_0_ = f32[1,2,16,8,256]{4,3,2,1,0:T(8,128)S(1)} custom-call(s32[1]{0:T(128)} %bitcast.1.side_ref, bf16[256,256]{1,0:T(8,128)(2,1)S(1)} %shard_map.46.refs_0_, bf16[256,256]{1,0:T(8,128)(2,1)S(1)} %shard_map.47.refs_0_.refs_1_, bf16[256,256]{1,0:T(8,128)(2,1)S(1)} %shard_map.48.refs_0_.refs_2_.refs_1_, ...), custom_call_target="tpu_custom_call" | custom-call | flops 1 | bytes 1 | tf_op jit(solution)/shard_map/pallas_call | solution.py:275
  13.8 0.6 %shard_map.52.refs_2_ = f32[1,2,16,8,256]{4,3,2,1,0:T(8,128)S(1)} custom-call(s32[1]{0:T(128)} %bitcast.1.side_ref, bf16[256,256]{1,0:T(8,128)(2,1)S(1)} %shard_map.46.refs_0_, bf16[256,256]{1,0:T(8,128)(2,1)S(1)} %collective-permute-done.1.refs_1_.refs_2_, f32[1,2,16,8,256]{4,3,2,1,0:T(8,128)S(1)} %shard_map.51.refs_2_.refs_0_), custom_call_target="tpu_custom_call" | custom-call | flops 1 | bytes 1 | tf_op jit(solution)/shard_map/pallas_call | solution.py:275
  14.5 0.6 %shard_map.53.refs_3_.refs_4_.refs_1_.refs_6_ = f32[1,2,16,8,256]{4,3,2,1,0:T(8,128)S(1)} custom-call(s32[1]{0:T(128)} %bitcast.1.side_ref, bf16[256,256]{1,0:T(8,128)(2,1)S(1)} %shard_map.47.refs_0_.refs_1_, bf16[256,256]{1,0:T(8,128)(2,1)S(1)} %collective-permute-done.refs_1_.refs_2_.refs_4_, f32[1,2,16,8,256]{4,3,2,1,0:T(8,128)S(1)} %shard_map.52.refs_2_), custom_call_target="tpu_custom_call" | custom-call | flops 1 | bytes 1 | tf_op jit(solution)/shard_map/pallas_call | solution.py:275
  15.1 2.0 %collective-permute-done.4.refs_0_ = bf16[256,256]{1,0:T(8,128)(2,1)S(1)} collective-permute-done((bf16[256,256]{1,0:T(8,128)(2,1)S(1)}, bf16[256,256]{1,0:T(8,128)(2,1)S(1)}, u32[]{:S(2)}, u32[]{:S(2)}) %collective-permute-start.4) | collective-permute-done | bytes 131104 | tf_op jit(solution)/shard_map/ppermute | solution.py:395
  17.0 1.2 %shard_map.54.refs_3_ = f32[2,2,16,8,256]{4,3,2,1,0:T(8,128)S(1)} custom-call(s32[1]{0:T(128)} %bitcast.1.side_ref, bf16[256,256]{1,0:T(8,128)(2,1)S(1)} %collective-permute-done.4.refs_0_, bf16[256,256]{1,0:T(8,128)(2,1)S(1)} %shard_map.48.refs_0_.refs_2_.refs_1_, bf16[256,256]{1,0:T(8,128)(2,1)S(1)} %collective-permute-done.1.refs_1_.refs_2_, ...), custom_call_target="tpu_custom_call" | custom-call | flops 2 | bytes 2 | tf_op jit(solution)/shard_map/pallas_call | solution.py:275
  18.5 0.6 %shard_map.55.refs_5_ = f32[2,2,16,8,256]{4,3,2,1,0:T(8,128)S(1)} custom-call(s32[1]{0:T(128)} %bitcast.1.side_ref, bf16[128,256]{1,0:T(8,128)(2,1)S(1)} %collective-permute-done.3.refs_0_, bf16[128,256]{1,0:T(8,128)(2,1)S(1)} %shard_map.49.refs_0_.refs_3_.refs_1_, bf16[256,256]{1,0:T(8,128)(2,1)S(1)} %collective-permute-done.refs_1_.refs_2_.refs_4_, ...), custom_call_target="tpu_custom_call" | custom-call | flops 2 | bytes 2 | tf_op jit(solution)/shard_map/pallas_call | solution.py:275
  19.2 0.7 %shard_map.56 = (f32[2,2,16,8,256]{4,3,2,1,0:T(8,128)S(1)}, bf16[2,2,16,8,256]{4,3,2,1,0:T(8,128)(2,1)S(1)}) custom-call(s32[1]{0:T(128)} %bitcast.1.side_ref, s32[1]{0:T(128)} %bitcast.core_ref, s32[1]{0:T(128)} %bitcast.2.turn_ref, f32[1,2,16,8,256]{4,3,2,1,0:T(8,128)S(1)} %shard_map.51.refs_2_.refs_0_, ...), custom_call_target="tpu_custom_call" | custom-call | flops 2 | bytes 2 | tf_op jit(solution)/shard_map/pallas_call | solution.py:275
  20.0 1.5 %collective-permute-done.5.refs_3_ = bf16[2,2,16,8,256]{4,3,2,1,0:T(8,128)(2,1)S(1)} collective-permute-done((bf16[2,2,16,8,256]{4,3,2,1,0:T(8,128)(2,1)S(1)}, bf16[2,2,16,8,256]{4,3,2,1,0:T(8,128)(2,1)S(1)}, u32[]{:S(2)}, u32[]{:S(2)}) %collective-permute-start.5) | collective-permute-done | bytes 262176 | tf_op jit(solution)/shard_map/ppermute | solution.py:387
  21.6 0.8 %collective-permute-start.6 = (bf16[2,16,8,256]{3,2,1,0:T(8,128)(2,1)S(1)}, bf16[2,16,8,256]{3,2,1,0:T(8,128)(2,1)S(1)}, u32[]{:S(2)}, u32[]{:S(2)}) collective-permute-start(bf16[2,16,8,256]{3,2,1,0:T(8,128)(2,1)S(1)} %get-tuple-element.13), channel_id=1, source_target_pairs={{0,8},{1,5},{2,0},{3,13},{4,12},{5,1},{6,4},{7,9},{8,10},{9,7},{10... | collective-permute-start | bytes 393224 | tf_op jit(solution)/shard_map/ppermute | solution.py:407
  22.4 0.7 %collective-permute-start.7 = (bf16[2,16,8,256]{3,2,1,0:T(8,128)(2,1)S(1)}, bf16[2,16,8,256]{3,2,1,0:T(8,128)(2,1)S(1)}, u32[]{:S(2)}, u32[]{:S(2)}) collective-permute-start(bf16[2,16,8,256]{3,2,1,0:T(8,128)(2,1)S(1)} %get-tuple-element.14), channel_id=1, source_target_pairs={{0,0},{1,13},{2,8},{3,5},{4,4},{5,9},{6,12},{7,1},{8,2},{9,15},{10... | collective-permute-start | bytes 393224 | tf_op jit(solution)/shard_map/ppermute | solution.py:407
  23.0 3.6 %collective-permute-done.6.first = bf16[2,16,8,256]{3,2,1,0:T(8,128)(2,1)S(1)} collective-permute-done((bf16[2,16,8,256]{3,2,1,0:T(8,128)(2,1)S(1)}, bf16[2,16,8,256]{3,2,1,0:T(8,128)(2,1)S(1)}, u32[]{:S(2)}, u32[]{:S(2)}) %collective-permute-start.6) | collective-permute-done | bytes 131104 | tf_op jit(solution)/shard_map/ppermute | solution.py:407
  26.6 3.1 %collective-permute-start.8 = (bf16[16,8,256]{2,1,0:T(8,128)(2,1)S(1)}, bf16[16,8,256]{2,1,0:T(8,128)(2,1)S(1)}, u32[]{:S(2)}, u32[]{:S(2)}) collective-permute-start(bf16[16,8,256]{2,1,0:T(8,128)(2,1)S(1)} %get-tuple-element.16), channel_id=1, source_target_pairs={{0,1},{1,0},{2,3},{3,2},{4,5},{5,4},{6,7},{7,6},{8,9},{9,8},{10,11... | collective-permute-start | bytes 196616 | tf_op jit(solution)/shard_map/ppermute | solution.py:387
  29.7 0.9 %collective-permute-done.8 = bf16[16,8,256]{2,1,0:T(8,128)(2,1)S(1)} collective-permute-done((bf16[16,8,256]{2,1,0:T(8,128)(2,1)S(1)}, bf16[16,8,256]{2,1,0:T(8,128)(2,1)S(1)}, u32[]{:S(2)}, u32[]{:S(2)}) %collective-permute-start.8) | collective-permute-done | bytes 65568 | tf_op jit(solution)/shard_map/ppermute | solution.py:387
  30.6 0.7 %add_multiply_fusion = f32[16,8,256]{2,1,0:T(8,128)} fusion(f32[16,8,256]{2,1,0:T(8,128)S(1)} %get-tuple-element.15, bf16[16,8,256]{2,1,0:T(8,128)(2,1)S(1)} %collective-permute-done.8), kind=kLoop, calls=%fused_computation | loop fusion | flops 98304 | bytes 327680 | tf_op jit(solution)/shard_map/mul | solution.py:448
  (16 shorter events, 0.6 us)
Async XLA Ops:
  0.0 6.2 %copy-start = (f32[16,32,1024]{2,1,0:T(8,128)S(1)}, f32[16,32,1024]{2,1,0:T(8,128)}, u32[]{:S(2)}) copy-start(f32[16,32,1024]{2,1,0:T(8,128)} %param.4) | copy-start | bytes 6291460
  0.0 6.2 %copy-start.1 = (f32[32,16,1024]{2,1,0:T(8,128)S(1)}, f32[32,16,1024]{2,1,0:T(8,128)}, u32[]{:S(2)}) copy-start(f32[32,16,1024]{2,1,0:T(8,128)} %param.5) | copy-start | bytes 6291460
  0.0 6.2 %copy-start.2 = (bf16[512,256]{1,0:T(8,128)(2,1)S(1)}, bf16[512,256]{1,0:T(8,128)(2,1)}, u32[]{:S(2)}) copy-start(bf16[512,256]{1,0:T(8,128)(2,1)} %constant.51.clone.low_ref) | copy-start | bytes 786436
  0.0 6.2 %copy-start.3 = (bf16[512,256]{1,0:T(8,128)(2,1)S(1)}, bf16[512,256]{1,0:T(8,128)(2,1)}, u32[]{:S(2)}) copy-start(bf16[512,256]{1,0:T(8,128)(2,1)} %constant.50.clone.high_ref) | copy-start | bytes 786436
  2.1 11.7 %collective-permute-start.1 = (bf16[256,256]{1,0:T(8,128)(2,1)S(1)}, bf16[256,256]{1,0:T(8,128)(2,1)S(1)}, u32[]{:S(2)}, u32[]{:S(2)}) collective-permute-start(bf16[256,256]{1,0:T(8,128)(2,1)S(1)} %shard_map.46.refs_0_), channel_id=1, source_target_pairs={{0,16},{8,0},{16,24},{24,8},{1,17},{9,1},{17,25},{25,9},{2,18},{10... | collective-permute-start | bytes 393224 | tf_op jit(solution)/shard_map/ppermute | solution.py:395
  6.9 7.6 %collective-permute-start = (bf16[256,256]{1,0:T(8,128)(2,1)S(1)}, bf16[256,256]{1,0:T(8,128)(2,1)S(1)}, u32[]{:S(2)}, u32[]{:S(2)}) collective-permute-start(bf16[256,256]{1,0:T(8,128)(2,1)S(1)} %shard_map.47.refs_0_.refs_1_), channel_id=1, source_target_pairs={{0,16},{8,0},{16,24},{24,8},{1,17},{9,1},{17,25},{25,9},{2,18},{10... | collective-permute-start | bytes 393224 | tf_op jit(solution)/shard_map/ppermute | solution.py:395
  9.1 8.0 %collective-permute-start.4 = (bf16[256,256]{1,0:T(8,128)(2,1)S(1)}, bf16[256,256]{1,0:T(8,128)(2,1)S(1)}, u32[]{:S(2)}, u32[]{:S(2)}) collective-permute-start(bf16[256,256]{1,0:T(8,128)(2,1)S(1)} %shard_map.48.refs_0_.refs_2_.refs_1_), channel_id=1, source_target_pairs={{0,8},{8,24},{16,0},{24,16},{1,9},{9,25},{17,1},{25,17},{2,10},{10... | collective-permute-start | bytes 393224 | tf_op jit(solution)/shard_map/ppermute | solution.py:395
  10.0 8.5 %collective-permute-start.3 = (bf16[128,256]{1,0:T(8,128)(2,1)S(1)}, bf16[128,256]{1,0:T(8,128)(2,1)S(1)}, u32[]{:S(2)}, u32[]{:S(2)}) collective-permute-start(bf16[128,256]{1,0:T(8,128)(2,1)S(1)} %shard_map.49.refs_0_.refs_3_.refs_1_), channel_id=1, source_target_pairs={{0,8},{8,24},{16,0},{24,16},{1,9},{9,25},{17,1},{25,17},{2,10},{10... | collective-permute-start | bytes 196616 | tf_op jit(solution)/shard_map/ppermute | solution.py:395
  10.9 8.4 %collective-permute-start.2 = (bf16[128,256]{1,0:T(8,128)(2,1)S(1)}, bf16[128,256]{1,0:T(8,128)(2,1)S(1)}, u32[]{:S(2)}, u32[]{:S(2)}) collective-permute-start(bf16[128,256]{1,0:T(8,128)(2,1)S(1)} %shard_map.50.refs_4_.refs_5_.refs_3_), channel_id=1, source_target_pairs={{0,8},{8,24},{16,0},{24,16},{1,9},{9,25},{17,1},{25,17},{2,10},{10... | collective-permute-start | bytes 196616 | tf_op jit(solution)/shard_map/ppermute | solution.py:395
  19.9 1.6 %collective-permute-start.5 = (bf16[2,2,16,8,256]{4,3,2,1,0:T(8,128)(2,1)S(1)}, bf16[2,2,16,8,256]{4,3,2,1,0:T(8,128)(2,1)S(1)}, u32[]{:S(2)}, u32[]{:S(2)}) collective-permute-start(bf16[2,2,16,8,256]{4,3,2,1,0:T(8,128)(2,1)S(1)} %get-tuple-element.12), channel_id=1, source_target_pairs={{0,1},{1,0},{2,3},{3,2},{4,5},{5,4},{6,7},{7,6},{8,9},{9,8},{10,11... | collective-permute-start | bytes 786440 | tf_op jit(solution)/shard_map/ppermute | solution.py:387
  21.6 5.0 %collective-permute-start.6 = (bf16[2,16,8,256]{3,2,1,0:T(8,128)(2,1)S(1)}, bf16[2,16,8,256]{3,2,1,0:T(8,128)(2,1)S(1)}, u32[]{:S(2)}, u32[]{:S(2)}) collective-permute-start(bf16[2,16,8,256]{3,2,1,0:T(8,128)(2,1)S(1)} %get-tuple-element.13), channel_id=1, source_target_pairs={{0,8},{1,5},{2,0},{3,13},{4,12},{5,1},{6,4},{7,9},{8,10},{9,7},{10... | collective-permute-start | bytes 393224 | tf_op jit(solution)/shard_map/ppermute | solution.py:407
  22.4 4.2 %collective-permute-start.7 = (bf16[2,16,8,256]{3,2,1,0:T(8,128)(2,1)S(1)}, bf16[2,16,8,256]{3,2,1,0:T(8,128)(2,1)S(1)}, u32[]{:S(2)}, u32[]{:S(2)}) collective-permute-start(bf16[2,16,8,256]{3,2,1,0:T(8,128)(2,1)S(1)} %get-tuple-element.14), channel_id=1, source_target_pairs={{0,0},{1,13},{2,8},{3,5},{4,4},{5,9},{6,12},{7,1},{8,2},{9,15},{10... | collective-permute-start | bytes 393224 | tf_op jit(solution)/shard_map/ppermute | solution.py:407
  26.6 4.0 %collective-permute-start.8 = (bf16[16,8,256]{2,1,0:T(8,128)(2,1)S(1)}, bf16[16,8,256]{2,1,0:T(8,128)(2,1)S(1)}, u32[]{:S(2)}, u32[]{:S(2)}) collective-permute-start(bf16[16,8,256]{2,1,0:T(8,128)(2,1)S(1)} %get-tuple-element.16), channel_id=1, source_target_pairs={{0,1},{1,0},{2,3},{3,2},{4,5},{5,4},{6,7},{7,6},{8,9},{9,8},{10,11... | collective-permute-start | bytes 196616 | tf_op jit(solution)/shard_map/ppermute | solution.py:387

commit v5 on v4

--- a/solution.py
+++ b/solution.py
@@ -288,44 +288,46 @@
 
 def pairs_kernel(side_ref, core_ref, turn_ref, *refs, kept):
     place = side_ref[0], core_ref[0], turn_ref[0]
-    came, outs = refs[kept], refs[kept + 1 :]
-    for op, out in enumerate(outs):
-
-        def use(tile, op=op, out=out):
-            out[...] = (tile[...] + came[op].astype(jnp.float32)).astype(out.dtype)
-
+    came, first, second, third = refs[kept:]
+
+    def use_first(tile):
+        first[...] = (tile[...] + came[0].astype(jnp.float32)).astype(first.dtype)
+
+    def use_second(tile):
+        for out, half in ((second, place[1]), (third, 1 - place[1])):
+            out[...] = (tile[half] + came[1, half].astype(jnp.float32)).astype(out.dtype)
+
+    for op, use in enumerate((use_first, use_second)):
         with_tile(tile_at(place, place[1], op), refs[:kept], use)
 
 
 def pairs_of(place, kept, came):
     vmem = pl.BlockSpec(memory_space=pltpu.VMEM)
+    shape = came.shape[1:]
     return pl.pallas_call(
         functools.partial(pairs_kernel, kept=len(kept)),
         in_specs=[pl.BlockSpec(memory_space=pltpu.SMEM)] * 3 + [vmem] * (len(kept) + 1),
+        out_specs=(vmem,) * 3,
+        out_shape=[jax.ShapeDtypeStruct(one, jnp.bfloat16) for one in (shape, shape[1:], shape[1:])],
+        compiler_params=pltpu.CompilerParams(vmem_limit_bytes=VMEM),
+    )(*place, *kept, came)
+
+
+def halves_kernel(core_ref, whole, keep, send):
+    own = core_ref[0]
+    keep[...] = whole[own]
+    send[...] = whole[1 - own]
+
+
+def halves_of(place, whole):
+    vmem = pl.BlockSpec(memory_space=pltpu.VMEM)
+    return pl.pallas_call(
+        halves_kernel,
+        in_specs=[pl.BlockSpec(memory_space=pltpu.SMEM), vmem],
         out_specs=(vmem, vmem),
-        out_shape=(jax.ShapeDtypeStruct(came.shape[1:], jnp.bfloat16),) * 2,
-        compiler_params=pltpu.CompilerParams(vmem_limit_bytes=VMEM),
-    )(*place, *kept, came)
-
-
-def halves_kernel(core_ref, first, second, keep, send):
-    own = core_ref[0]
-    keep[...] = first[own].astype(jnp.float32) + second[own].astype(jnp.float32)
-    send[...] = (first[1 - own].astype(jnp.float32) + second[1 - own].astype(jnp.float32)).astype(send.dtype)
-
-
-def halves_of(place, first, second):
-    vmem = pl.BlockSpec(memory_space=pltpu.VMEM)
-    return pl.pallas_call(
-        halves_kernel,
-        in_specs=[pl.BlockSpec(memory_space=pltpu.SMEM), vmem, vmem],
-        out_specs=(vmem, vmem),
-        out_shape=(
-            jax.ShapeDtypeStruct(first.shape[1:], jnp.float32),
-            jax.ShapeDtypeStruct(first.shape[1:], jnp.bfloat16),
-        ),
-        compiler_params=pltpu.CompilerParams(vmem_limit_bytes=VMEM),
-    )(place[1], first, second)
+        out_shape=(jax.ShapeDtypeStruct(whole.shape[1:], jnp.bfloat16),) * 2,
+        compiler_params=pltpu.CompilerParams(vmem_limit_bytes=VMEM),
+    )(place[1], whole)
 
 
 def block_kernel(left_ref, right_ref, out_ref, left_forms, right_forms):
@@ -395,14 +397,14 @@
     return lax.ppermute(value, "src", [(z, z ^ (1 if side_of(z) ^ other else 2)) for z in range(4)])
 
 
-def deliver(value, op):
+def deliver(value, op, flip):
     members = lax.axis_size("xl")
     pairs = []
     for z in range(lax.axis_size("src")):
         for chip in range(members // 2):
             for core in range(2):
                 tile = z ^ chip ^ ((2 + op) if core else (1 - op))
-                target = (z ^ (tile & 1)) * members + (z ^ (tile & 2)) * 2 + core
+                target = (z ^ (tile & 1)) * members + (z ^ (tile & 2)) * 2 + (core ^ flip)
                 pairs.append((z * members + chip * 2 + core, target))
     return lax.ppermute(value, ("src", "xl"), pairs)
 
@@ -443,9 +445,10 @@
         kept = early if first + count == blocks else ()
         sums = tiles_of(place, far_other[here], [other[here], far_one[here]], sums, (early[1],), kept)
     sums, send = sums
-    pairs = pairs_of(place, [*early, sums], swap(send, "xl", 1))
-    keep, send = halves_of(place, *[deliver(part, op) for op, part in enumerate(pairs)])
-    return (keep + swap(send, "xl", 1).astype(jnp.float32)) * weight
+    first, second, third = pairs_of(place, [*early, sums], swap(send, "xl", 1))
+    keep, send = halves_of(place, deliver(first, 0, 0))
+    parts = [keep, swap(send, "xl", 1), deliver(second, 1, 0), deliver(third, 1, 1)]
+    return sum(part.astype(jnp.float32) for part in parts) * weight
 
 
 def per_device(src_traces, rec_traces):

time: 31.4 us -> 30.6 us (0.975)
  waiting for transfers between devices: 8.38 us -> 5.48 us
  starting transfers between devices: 13.1 us -> 15.2 us
    ppermute x2 -> x3, starting transfers between devices: 1.44 us -> 5.43 us  [deliver(): return lax.ppermute(value, ('src', 'xl'), pairs)]
    ppermute x2 -> x3, waiting for transfers between devices: 3.57 us -> 1.56 us  [deliver(): return lax.ppermute(value, ('src', 'xl'), pairs)]
    ppermute x2, starting transfers between devices: 3.15 us -> 1.27 us  [swap(): return lax.ppermute(value, axis, [(i, i ^ flip) for i in range(count)])]
    ppermute x2, waiting for transfers between devices: 2.42 us -> 1.52 us  [swap(): return lax.ppermute(value, axis, [(i, i ^ flip) for i in range(count)])]
  transfers between devices with their start and end apart: 9 -> 10, of which waited for: 6 -> 5; matrix products, arithmetic and copies ran while one was open for 0% -> 0% of each run, Pallas kernels for 20% -> 20%
where the time goes in v5:
time: 30.6 us; the launch traced here: 30.5 us
  starting transfers between devices  15.2 us (50%)
  Pallas kernels  8.99 us (29%)
  waiting for transfers between devices  5.48 us (18%)
  other arithmetic  0.69 us (2%)
    ppermute x5, starting transfers between devices, cross(): lax.ppermute(value, 'src', [(z, z ^ (1 if side_of(z) ^ other else 2)) for...  8.46 us
    ppermute x3, starting transfers between devices, deliver(): return lax.ppermute(value, ('src', 'xl'), pairs)  5.43 us
    pallas_call x6, Pallas kernels, tiles_of(): pl.pallas_call(kernel, in_specs=[pl.BlockSpec(memory_space=pltpu.SMEM)] *...  4.83 us
    ppermute x5, waiting for transfers between devices, cross(): lax.ppermute(value, 'src', [(z, z ^ (1 if side_of(z) ^ other else 2)) for...  2.39 us
    pallas_call x1, Pallas kernels, first_spectra(): pl.pallas_call(functools.partial(first_kernel, blocks=blocks), in_specs=[...  2.11 us
    pallas_call x4, Pallas kernels, either_spectra(): pl.pallas_call(functools.partial(either_kernel, other=other, first=first,...  1.96 us
    ppermute x3, waiting for transfers between devices, deliver(): return lax.ppermute(value, ('src', 'xl'), pairs)  1.56 us
    ppermute x2, waiting for transfers between devices, swap(): return lax.ppermute(value, axis, [(i, i ^ flip) for i in range(count)])  1.52 us
  transfers between devices with their start and end apart: 10, of which 5 were waited for; matrix products, arithmetic and copies ran while one was open for 0% of the time, Pallas kernels for 20%

profile of v5, /device:TPU:0, one launch (start us, length us, event | category | flops | bytes accessed | tf_op | source)
XLA Modules:
  0.0 30.5 jit_solution(17060843316500185967)
XLA Ops:
  0.0 2.1 %shard_map.46.refs_0_ = bf16[256,256]{1,0:T(8,128)(2,1)S(1)} custom-call(s32[1]{0:T(128)} %bitcast.1.side_ref, f32[16,4,8,1024]{3,2,1,0:T(8,128)} %bitcast.5, f32[4,16,8,1024]{3,2,1,0:T(8,128)} %bitcast.10, bf16[512,256]{1,0:T(8,128)(2,1)} %constant.50.clone.high_ref, bf16[512,256]{1,0:T(8,128)(2,1)} %constant.51.clone.low_ref), custom_call_target="tpu_custom_call" | custom-call | tf_op jit(solution)/shard_map/pallas_call | solution.py:99
  2.1 4.1 %collective-permute-start.1 = (bf16[256,256]{1,0:T(8,128)(2,1)S(1)}, bf16[256,256]{1,0:T(8,128)(2,1)S(1)}, u32[]{:S(2)}, u32[]{:S(2)}) collective-permute-start(bf16[256,256]{1,0:T(8,128)(2,1)S(1)} %shard_map.46.refs_0_), channel_id=1, source_target_pairs={{0,16},{8,0},{16,24},{24,8},{1,17},{9,1},{17,25},{25,9},{2,18},{10... | collective-permute-start | bytes 393224 | tf_op jit(solution)/shard_map/ppermute | solution.py:397
  6.3 0.6 %shard_map.47.refs_0_.refs_1_ = bf16[256,256]{1,0:T(8,128)(2,1)S(1)} custom-call(s32[1]{0:T(128)} %bitcast.1.side_ref, f32[16,4,8,1024]{3,2,1,0:T(8,128)S(1)} %bitcast.6, f32[4,16,8,1024]{3,2,1,0:T(8,128)S(1)} %bitcast.11, bf16[512,256]{1,0:T(8,128)(2,1)S(1)} %copy-done.3, bf16[512,256]{1,0:T(8,128)(2,1)S(1)} %copy-done.2, ...), custom_call_target="tpu_custom_call" | custom-call | flops 256 | bytes 256 | tf_op jit(solution)/shard_map/pallas_call | solution.py:130
  6.9 1.6 %collective-permute-start = (bf16[256,256]{1,0:T(8,128)(2,1)S(1)}, bf16[256,256]{1,0:T(8,128)(2,1)S(1)}, u32[]{:S(2)}, u32[]{:S(2)}) collective-permute-start(bf16[256,256]{1,0:T(8,128)(2,1)S(1)} %shard_map.47.refs_0_.refs_1_), channel_id=1, source_target_pairs={{0,16},{8,0},{16,24},{24,8},{1,17},{9,1},{17,25},{25,9},{2,18},{10... | collective-permute-start | bytes 393224 | tf_op jit(solution)/shard_map/ppermute | solution.py:397
  8.5 0.6 %shard_map.48.refs_0_.refs_2_.refs_1_ = bf16[256,256]{1,0:T(8,128)(2,1)S(1)} custom-call(s32[1]{0:T(128)} %bitcast.1.side_ref, f32[16,4,8,1024]{3,2,1,0:T(8,128)S(1)} %bitcast.7, f32[4,16,8,1024]{3,2,1,0:T(8,128)S(1)} %bitcast.12, bf16[512,256]{1,0:T(8,128)(2,1)S(1)} %copy-done.3, bf16[512,256]{1,0:T(8,128)(2,1)S(1)} %copy-done.2, ...), custom_call_target="tpu_custom_call" | custom-call | flops 256 | bytes 256 | tf_op jit(solution)/shard_map/pallas_call | solution.py:130
  9.1 0.5 %collective-permute-start.4 = (bf16[256,256]{1,0:T(8,128)(2,1)S(1)}, bf16[256,256]{1,0:T(8,128)(2,1)S(1)}, u32[]{:S(2)}, u32[]{:S(2)}) collective-permute-start(bf16[256,256]{1,0:T(8,128)(2,1)S(1)} %shard_map.48.refs_0_.refs_2_.refs_1_), channel_id=1, source_target_pairs={{0,8},{8,24},{16,0},{24,16},{1,9},{9,25},{17,1},{25,17},{2,10},{10... | collective-permute-start | bytes 393224 | tf_op jit(solution)/shard_map/ppermute | solution.py:397
  9.6 0.4 %shard_map.49.refs_0_.refs_3_.refs_1_ = bf16[128,256]{1,0:T(8,128)(2,1)S(1)} custom-call(s32[1]{0:T(128)} %bitcast.1.side_ref, f32[16,4,8,1024]{3,2,1,0:T(8,128)S(1)} %bitcast.8, f32[4,16,8,1024]{3,2,1,0:T(8,128)S(1)} %bitcast.13, bf16[512,256]{1,0:T(8,128)(2,1)S(1)} %copy-done.3, bf16[512,256]{1,0:T(8,128)(2,1)S(1)} %copy-done.2, ...), custom_call_target="tpu_custom_call" | custom-call | flops 128 | bytes 128 | tf_op jit(solution)/shard_map/pallas_call | solution.py:130
  10.0 0.5 %collective-permute-start.3 = (bf16[128,256]{1,0:T(8,128)(2,1)S(1)}, bf16[128,256]{1,0:T(8,128)(2,1)S(1)}, u32[]{:S(2)}, u32[]{:S(2)}) collective-permute-start(bf16[128,256]{1,0:T(8,128)(2,1)S(1)} %shard_map.49.refs_0_.refs_3_.refs_1_), channel_id=1, source_target_pairs={{0,8},{8,24},{16,0},{24,16},{1,9},{9,25},{17,1},{25,17},{2,10},{10... | collective-permute-start | bytes 196616 | tf_op jit(solution)/shard_map/ppermute | solution.py:397
  10.5 0.4 %shard_map.50.refs_4_.refs_5_.refs_3_ = bf16[128,256]{1,0:T(8,128)(2,1)S(1)} custom-call(s32[1]{0:T(128)} %bitcast.1.side_ref, f32[16,4,8,1024]{3,2,1,0:T(8,128)S(1)} %bitcast.9, f32[4,16,8,1024]{3,2,1,0:T(8,128)S(1)} %bitcast.14, bf16[512,256]{1,0:T(8,128)(2,1)S(1)} %copy-done.3, bf16[512,256]{1,0:T(8,128)(2,1)S(1)} %copy-done.2, ...), custom_call_target="tpu_custom_call" | custom-call | flops 128 | bytes 128 | tf_op jit(solution)/shard_map/pallas_call | solution.py:130
  10.9 1.7 %collective-permute-start.2 = (bf16[128,256]{1,0:T(8,128)(2,1)S(1)}, bf16[128,256]{1,0:T(8,128)(2,1)S(1)}, u32[]{:S(2)}, u32[]{:S(2)}) collective-permute-start(bf16[128,256]{1,0:T(8,128)(2,1)S(1)} %shard_map.50.refs_4_.refs_5_.refs_3_), channel_id=1, source_target_pairs={{0,8},{8,24},{16,0},{24,16},{1,9},{9,25},{17,1},{25,17},{2,10},{10... | collective-permute-start | bytes 196616 | tf_op jit(solution)/shard_map/ppermute | solution.py:397
  12.6 1.2 %shard_map.51.refs_2_.refs_0_ = f32[1,2,16,8,256]{4,3,2,1,0:T(8,128)S(1)} custom-call(s32[1]{0:T(128)} %bitcast.1.side_ref, bf16[256,256]{1,0:T(8,128)(2,1)S(1)} %shard_map.46.refs_0_, bf16[256,256]{1,0:T(8,128)(2,1)S(1)} %shard_map.47.refs_0_.refs_1_, bf16[256,256]{1,0:T(8,128)(2,1)S(1)} %shard_map.48.refs_0_.refs_2_.refs_1_, ...), custom_call_target="tpu_custom_call" | custom-call | flops 1 | bytes 1 | tf_op jit(solution)/shard_map/pallas_call | solution.py:275
  13.8 0.6 %shard_map.52.refs_2_ = f32[1,2,16,8,256]{4,3,2,1,0:T(8,128)S(1)} custom-call(s32[1]{0:T(128)} %bitcast.1.side_ref, bf16[256,256]{1,0:T(8,128)(2,1)S(1)} %shard_map.46.refs_0_, bf16[256,256]{1,0:T(8,128)(2,1)S(1)} %collective-permute-done.1.refs_1_.refs_2_, f32[1,2,16,8,256]{4,3,2,1,0:T(8,128)S(1)} %shard_map.51.refs_2_.refs_0_), custom_call_target="tpu_custom_call" | custom-call | flops 1 | bytes 1 | tf_op jit(solution)/shard_map/pallas_call | solution.py:275
  14.5 0.6 %shard_map.53.refs_3_.refs_4_.refs_1_.refs_6_ = f32[1,2,16,8,256]{4,3,2,1,0:T(8,128)S(1)} custom-call(s32[1]{0:T(128)} %bitcast.1.side_ref, bf16[256,256]{1,0:T(8,128)(2,1)S(1)} %shard_map.47.refs_0_.refs_1_, bf16[256,256]{1,0:T(8,128)(2,1)S(1)} %collective-permute-done.refs_1_.refs_2_.refs_4_, f32[1,2,16,8,256]{4,3,2,1,0:T(8,128)S(1)} %shard_map.52.refs_2_), custom_call_target="tpu_custom_call" | custom-call | flops 1 | bytes 1 | tf_op jit(solution)/shard_map/pallas_call | solution.py:275
  15.1 2.0 %collective-permute-done.4.refs_0_ = bf16[256,256]{1,0:T(8,128)(2,1)S(1)} collective-permute-done((bf16[256,256]{1,0:T(8,128)(2,1)S(1)}, bf16[256,256]{1,0:T(8,128)(2,1)S(1)}, u32[]{:S(2)}, u32[]{:S(2)}) %collective-permute-start.4) | collective-permute-done | bytes 131104 | tf_op jit(solution)/shard_map/ppermute | solution.py:397
  17.0 1.2 %shard_map.54.refs_3_ = f32[2,2,16,8,256]{4,3,2,1,0:T(8,128)S(1)} custom-call(s32[1]{0:T(128)} %bitcast.1.side_ref, bf16[256,256]{1,0:T(8,128)(2,1)S(1)} %collective-permute-done.4.refs_0_, bf16[256,256]{1,0:T(8,128)(2,1)S(1)} %shard_map.48.refs_0_.refs_2_.refs_1_, bf16[256,256]{1,0:T(8,128)(2,1)S(1)} %collective-permute-done.1.refs_1_.refs_2_, ...), custom_call_target="tpu_custom_call" | custom-call | flops 2 | bytes 2 | tf_op jit(solution)/shard_map/pallas_call | solution.py:275
  18.5 0.6 %shard_map.55.refs_5_ = f32[2,2,16,8,256]{4,3,2,1,0:T(8,128)S(1)} custom-call(s32[1]{0:T(128)} %bitcast.1.side_ref, bf16[128,256]{1,0:T(8,128)(2,1)S(1)} %collective-permute-done.3.refs_0_, bf16[128,256]{1,0:T(8,128)(2,1)S(1)} %shard_map.49.refs_0_.refs_3_.refs_1_, bf16[256,256]{1,0:T(8,128)(2,1)S(1)} %collective-permute-done.refs_1_.refs_2_.refs_4_, ...), custom_call_target="tpu_custom_call" | custom-call | flops 2 | bytes 2 | tf_op jit(solution)/shard_map/pallas_call | solution.py:275
  19.2 0.7 %shard_map.56 = (f32[2,2,16,8,256]{4,3,2,1,0:T(8,128)S(1)}, bf16[2,2,16,8,256]{4,3,2,1,0:T(8,128)(2,1)S(1)}) custom-call(s32[1]{0:T(128)} %bitcast.1.side_ref, s32[1]{0:T(128)} %bitcast.core_ref, s32[1]{0:T(128)} %bitcast.2.turn_ref, f32[1,2,16,8,256]{4,3,2,1,0:T(8,128)S(1)} %shard_map.51.refs_2_.refs_0_, ...), custom_call_target="tpu_custom_call" | custom-call | flops 2 | bytes 2 | tf_op jit(solution)/shard_map/pallas_call | solution.py:275
  20.0 1.5 %collective-permute-done.5.refs_3_ = bf16[2,2,16,8,256]{4,3,2,1,0:T(8,128)(2,1)S(1)} collective-permute-done((bf16[2,2,16,8,256]{4,3,2,1,0:T(8,128)(2,1)S(1)}, bf16[2,2,16,8,256]{4,3,2,1,0:T(8,128)(2,1)S(1)}, u32[]{:S(2)}, u32[]{:S(2)}) %collective-permute-start.5) | collective-permute-done | bytes 262176 | tf_op jit(solution)/shard_map/ppermute | solution.py:389
  21.6 0.8 %collective-permute-start.6 = (bf16[2,16,8,256]{3,2,1,0:T(8,128)(2,1)S(1)}, bf16[2,16,8,256]{3,2,1,0:T(8,128)(2,1)S(1)}, u32[]{:S(2)}, u32[]{:S(2)}) collective-permute-start(bf16[2,16,8,256]{3,2,1,0:T(8,128)(2,1)S(1)} %get-tuple-element.14), channel_id=1, source_target_pairs={{0,8},{1,5},{2,0},{3,13},{4,12},{5,1},{6,4},{7,9},{8,10},{9,7},{10... | collective-permute-start | bytes 393224 | tf_op jit(solution)/shard_map/ppermute | solution.py:409
  22.4 0.7 %collective-permute-start.8 = (bf16[16,8,256]{2,1,0:T(8,128)(2,1)S(1)}, bf16[16,8,256]{2,1,0:T(8,128)(2,1)S(1)}, u32[]{:S(2)}, u32[]{:S(2)}) collective-permute-start(bf16[16,8,256]{2,1,0:T(8,128)(2,1)S(1)} %get-tuple-element.17), channel_id=1, source_target_pairs={{0,0},{1,13},{2,8},{3,5},{4,4},{5,9},{6,12},{7,1},{8,2},{9,15},{10... | collective-permute-start | bytes 196616 | tf_op jit(solution)/shard_map/ppermute | solution.py:409
  23.0 4.0 %collective-permute-start.9 = (bf16[16,8,256]{2,1,0:T(8,128)(2,1)S(1)}, bf16[16,8,256]{2,1,0:T(8,128)(2,1)S(1)}, u32[]{:S(2)}, u32[]{:S(2)}) collective-permute-start(bf16[16,8,256]{2,1,0:T(8,128)(2,1)S(1)} %get-tuple-element.18), channel_id=1, source_target_pairs={{0,1},{1,12},{2,9},{3,4},{4,5},{5,8},{6,13},{7,0},{8,3},{9,14},{10... | collective-permute-start | bytes 196616 | tf_op jit(solution)/shard_map/ppermute | solution.py:409
  27.0 1.2 %collective-permute-start.7 = (bf16[16,8,256]{2,1,0:T(8,128)(2,1)S(1)}, bf16[16,8,256]{2,1,0:T(8,128)(2,1)S(1)}, u32[]{:S(2)}, u32[]{:S(2)}) collective-permute-start(bf16[16,8,256]{2,1,0:T(8,128)(2,1)S(1)} %get-tuple-element.16), channel_id=1, source_target_pairs={{0,1},{1,0},{2,3},{3,2},{4,5},{5,4},{6,7},{7,6},{8,9},{9,8},{10,11... | collective-permute-start | bytes 196616 | tf_op jit(solution)/shard_map/ppermute | solution.py:389
  28.2 1.6 %collective-permute-done.9 = bf16[16,8,256]{2,1,0:T(8,128)(2,1)S(1)} collective-permute-done((bf16[16,8,256]{2,1,0:T(8,128)(2,1)S(1)}, bf16[16,8,256]{2,1,0:T(8,128)(2,1)S(1)}, u32[]{:S(2)}, u32[]{:S(2)}) %collective-permute-start.9) | collective-permute-done | bytes 65568 | tf_op jit(solution)/shard_map/ppermute | solution.py:409
  29.8 0.7 %add_multiply_fusion = f32[16,8,256]{2,1,0:T(8,128)} fusion(bf16[16,8,256]{2,1,0:T(8,128)(2,1)S(1)} %collective-permute-done.9, bf16[16,8,256]{2,1,0:T(8,128)(2,1)S(1)} %collective-permute-done.8, bf16[16,8,256]{2,1,0:T(8,128)(2,1)S(1)} %collective-permute-done.7, bf16[16,8,256]{2,1,0:T(8,128)(2,1)S(1)} %get-tuple-element.15), kind=kLoop, calls=%fused_computation | loop fusion | flops 262144 | bytes 393216 | tf_op jit(solution)/shard_map/mul | solution.py:451
  (18 shorter events, 0.6 us)
Async XLA Ops:
  0.0 6.2 %copy-start = (f32[16,32,1024]{2,1,0:T(8,128)S(1)}, f32[16,32,1024]{2,1,0:T(8,128)}, u32[]{:S(2)}) copy-start(f32[16,32,1024]{2,1,0:T(8,128)} %param.4) | copy-start | bytes 6291460
  0.0 6.2 %copy-start.1 = (f32[32,16,1024]{2,1,0:T(8,128)S(1)}, f32[32,16,1024]{2,1,0:T(8,128)}, u32[]{:S(2)}) copy-start(f32[32,16,1024]{2,1,0:T(8,128)} %param.5) | copy-start | bytes 6291460
  0.0 6.2 %copy-start.2 = (bf16[512,256]{1,0:T(8,128)(2,1)S(1)}, bf16[512,256]{1,0:T(8,128)(2,1)}, u32[]{:S(2)}) copy-start(bf16[512,256]{1,0:T(8,128)(2,1)} %constant.51.clone.low_ref) | copy-start | bytes 786436
  0.0 6.2 %copy-start.3 = (bf16[512,256]{1,0:T(8,128)(2,1)S(1)}, bf16[512,256]{1,0:T(8,128)(2,1)}, u32[]{:S(2)}) copy-start(bf16[512,256]{1,0:T(8,128)(2,1)} %constant.50.clone.high_ref) | copy-start | bytes 786436
  2.1 11.7 %collective-permute-start.1 = (bf16[256,256]{1,0:T(8,128)(2,1)S(1)}, bf16[256,256]{1,0:T(8,128)(2,1)S(1)}, u32[]{:S(2)}, u32[]{:S(2)}) collective-permute-start(bf16[256,256]{1,0:T(8,128)(2,1)S(1)} %shard_map.46.refs_0_), channel_id=1, source_target_pairs={{0,16},{8,0},{16,24},{24,8},{1,17},{9,1},{17,25},{25,9},{2,18},{10... | collective-permute-start | bytes 393224 | tf_op jit(solution)/shard_map/ppermute | solution.py:397
  6.9 7.6 %collective-permute-start = (bf16[256,256]{1,0:T(8,128)(2,1)S(1)}, bf16[256,256]{1,0:T(8,128)(2,1)S(1)}, u32[]{:S(2)}, u32[]{:S(2)}) collective-permute-start(bf16[256,256]{1,0:T(8,128)(2,1)S(1)} %shard_map.47.refs_0_.refs_1_), channel_id=1, source_target_pairs={{0,16},{8,0},{16,24},{24,8},{1,17},{9,1},{17,25},{25,9},{2,18},{10... | collective-permute-start | bytes 393224 | tf_op jit(solution)/shard_map/ppermute | solution.py:397
  9.1 8.0 %collective-permute-start.4 = (bf16[256,256]{1,0:T(8,128)(2,1)S(1)}, bf16[256,256]{1,0:T(8,128)(2,1)S(1)}, u32[]{:S(2)}, u32[]{:S(2)}) collective-permute-start(bf16[256,256]{1,0:T(8,128)(2,1)S(1)} %shard_map.48.refs_0_.refs_2_.refs_1_), channel_id=1, source_target_pairs={{0,8},{8,24},{16,0},{24,16},{1,9},{9,25},{17,1},{25,17},{2,10},{10... | collective-permute-start | bytes 393224 | tf_op jit(solution)/shard_map/ppermute | solution.py:397
  10.0 8.5 %collective-permute-start.3 = (bf16[128,256]{1,0:T(8,128)(2,1)S(1)}, bf16[128,256]{1,0:T(8,128)(2,1)S(1)}, u32[]{:S(2)}, u32[]{:S(2)}) collective-permute-start(bf16[128,256]{1,0:T(8,128)(2,1)S(1)} %shard_map.49.refs_0_.refs_3_.refs_1_), channel_id=1, source_target_pairs={{0,8},{8,24},{16,0},{24,16},{1,9},{9,25},{17,1},{25,17},{2,10},{10... | collective-permute-start | bytes 196616 | tf_op jit(solution)/shard_map/ppermute | solution.py:397
  10.9 8.4 %collective-permute-start.2 = (bf16[128,256]{1,0:T(8,128)(2,1)S(1)}, bf16[128,256]{1,0:T(8,128)(2,1)S(1)}, u32[]{:S(2)}, u32[]{:S(2)}) collective-permute-start(bf16[128,256]{1,0:T(8,128)(2,1)S(1)} %shard_map.50.refs_4_.refs_5_.refs_3_), channel_id=1, source_target_pairs={{0,8},{8,24},{16,0},{24,16},{1,9},{9,25},{17,1},{25,17},{2,10},{10... | collective-permute-start | bytes 196616 | tf_op jit(solution)/shard_map/ppermute | solution.py:397
  19.9 1.6 %collective-permute-start.5 = (bf16[2,2,16,8,256]{4,3,2,1,0:T(8,128)(2,1)S(1)}, bf16[2,2,16,8,256]{4,3,2,1,0:T(8,128)(2,1)S(1)}, u32[]{:S(2)}, u32[]{:S(2)}) collective-permute-start(bf16[2,2,16,8,256]{4,3,2,1,0:T(8,128)(2,1)S(1)} %get-tuple-element.13), channel_id=1, source_target_pairs={{0,1},{1,0},{2,3},{3,2},{4,5},{5,4},{6,7},{7,6},{8,9},{9,8},{10,11... | collective-permute-start | bytes 786440 | tf_op jit(solution)/shard_map/ppermute | solution.py:389
  21.6 5.4 %collective-permute-start.6 = (bf16[2,16,8,256]{3,2,1,0:T(8,128)(2,1)S(1)}, bf16[2,16,8,256]{3,2,1,0:T(8,128)(2,1)S(1)}, u32[]{:S(2)}, u32[]{:S(2)}) collective-permute-start(bf16[2,16,8,256]{3,2,1,0:T(8,128)(2,1)S(1)} %get-tuple-element.14), channel_id=1, source_target_pairs={{0,8},{1,5},{2,0},{3,13},{4,12},{5,1},{6,4},{7,9},{8,10},{9,7},{10... | collective-permute-start | bytes 393224 | tf_op jit(solution)/shard_map/ppermute | solution.py:409
  22.4 5.9 %collective-permute-start.8 = (bf16[16,8,256]{2,1,0:T(8,128)(2,1)S(1)}, bf16[16,8,256]{2,1,0:T(8,128)(2,1)S(1)}, u32[]{:S(2)}, u32[]{:S(2)}) collective-permute-start(bf16[16,8,256]{2,1,0:T(8,128)(2,1)S(1)} %get-tuple-element.17), channel_id=1, source_target_pairs={{0,0},{1,13},{2,8},{3,5},{4,4},{5,9},{6,12},{7,1},{8,2},{9,15},{10... | collective-permute-start | bytes 196616 | tf_op jit(solution)/shard_map/ppermute | solution.py:409
  23.0 6.8 %collective-permute-start.9 = (bf16[16,8,256]{2,1,0:T(8,128)(2,1)S(1)}, bf16[16,8,256]{2,1,0:T(8,128)(2,1)S(1)}, u32[]{:S(2)}, u32[]{:S(2)}) collective-permute-start(bf16[16,8,256]{2,1,0:T(8,128)(2,1)S(1)} %get-tuple-element.18), channel_id=1, source_target_pairs={{0,1},{1,12},{2,9},{3,4},{4,5},{5,8},{6,13},{7,0},{8,3},{9,14},{10... | collective-permute-start | bytes 196616 | tf_op jit(solution)/shard_map/ppermute | solution.py:409
  27.0 2.8 %collective-permute-start.7 = (bf16[16,8,256]{2,1,0:T(8,128)(2,1)S(1)}, bf16[16,8,256]{2,1,0:T(8,128)(2,1)S(1)}, u32[]{:S(2)}, u32[]{:S(2)}) collective-permute-start(bf16[16,8,256]{2,1,0:T(8,128)(2,1)S(1)} %get-tuple-element.16), channel_id=1, source_target_pairs={{0,1},{1,0},{2,3},{3,2},{4,5},{5,4},{6,7},{7,6},{8,9},{9,8},{10,11... | collective-permute-start | bytes 196616 | tf_op jit(solution)/shard_map/ppermute | solution.py:389

commit v6 on v5

--- a/solution.py
+++ b/solution.py
@@ -17,6 +17,7 @@
 ROWS = 16 * POINTS
 ONES = ((0, 2), (2, 2))
 OTHERS = ((0, 2), (2, 1), (3, 1))
+TURNS = ((3, 2), (0, 1))
 
 
 def fourier_table(samples):
@@ -219,7 +220,7 @@
 
 def tile_at(place, core, op):
     side, _, turn = place
-    tile = turn ^ jnp.where(core == 0, 1 - op, 2 + op)
+    tile = turn ^ jnp.where(core == 0, *TURNS[op])
     middle = jnp.logical_or(tile == 1, tile == 2)
     return jnp.where(jnp.logical_and(middle, side == 1), 3 - tile, tile)
 
@@ -238,13 +239,13 @@
 
 def last_tiles_kernel(side_ref, core_ref, turn_ref, *refs, kept, **options):
     place = side_ref[0], core_ref[0], turn_ref[0]
-    earlier, send = refs[:kept], refs[-2]
-    refs = refs[kept:-2] + refs[-1:]
+    earlier, sends = refs[:kept], refs[-3:-1]
+    refs = refs[kept:-3] + refs[-1:]
     tiles_kernel(side_ref, *refs, **options)
-    for op in range(2):
-
-        def use(tile, op=op):
-            send[op] = tile[...].astype(send.dtype)
+    for op, send in enumerate(sends):
+
+        def use(tile, send=send):
+            send[...] = tile[...].astype(send.dtype)
 
         with_tile(tile_at(place, 1 - place[1], op), [*earlier, refs[-2]], use)
 
@@ -264,7 +265,7 @@
     count = len(others)
     out_shape = [jax.ShapeDtypeStruct((count, 2, 16, 8, 2 * F), jnp.float32)]
     if kept:
-        out_shape.append(jax.ShapeDtypeStruct((2, 2, 16, 8, 2 * F), jnp.bfloat16))
+        out_shape += [jax.ShapeDtypeStruct((2, 16, 8, 2 * F), jnp.bfloat16)] * 2
     operands = [*kept, *arrays] + ([] if before is None else [before])
     vmem = pl.BlockSpec(memory_space=pltpu.VMEM)
     options = dict(arrays=len(arrays), ones=ones, others=others, carried=before is not None, spare=len(after))
@@ -286,29 +287,34 @@
     return result if kept else result[0]
 
 
-def pairs_kernel(side_ref, core_ref, turn_ref, *refs, kept):
+def first_kernel_of_pair(side_ref, core_ref, turn_ref, *refs, kept):
     place = side_ref[0], core_ref[0], turn_ref[0]
-    came, first, second, third = refs[kept:]
-
-    def use_first(tile):
-        first[...] = (tile[...] + came[0].astype(jnp.float32)).astype(first.dtype)
-
-    def use_second(tile):
-        for out, half in ((second, place[1]), (third, 1 - place[1])):
-            out[...] = (tile[half] + came[1, half].astype(jnp.float32)).astype(out.dtype)
-
-    for op, use in enumerate((use_first, use_second)):
-        with_tile(tile_at(place, place[1], op), refs[:kept], use)
-
-
-def pairs_of(place, kept, came):
+    came, out = refs[kept:]
+
+    def use(tile):
+        out[...] = (tile[...] + came[...].astype(jnp.float32)).astype(out.dtype)
+
+    with_tile(tile_at(place, place[1], 0), refs[:kept], use)
+
+
+def second_kernel_of_pair(side_ref, core_ref, turn_ref, *refs, kept):
+    place = side_ref[0], core_ref[0], turn_ref[0]
+    came = refs[kept]
+
+    def use(tile):
+        for out, half in zip(refs[kept + 1 :], (place[1], 1 - place[1])):
+            out[...] = (tile[half] + came[half].astype(jnp.float32)).astype(out.dtype)
+
+    with_tile(tile_at(place, place[1], 1), refs[:kept], use)
+
+
+def pair_of(kernel, place, kept, came, shapes):
     vmem = pl.BlockSpec(memory_space=pltpu.VMEM)
-    shape = came.shape[1:]
-    return pl.pallas_call(
-        functools.partial(pairs_kernel, kept=len(kept)),
+    return pl.pallas_call(
+        functools.partial(kernel, kept=len(kept)),
         in_specs=[pl.BlockSpec(memory_space=pltpu.SMEM)] * 3 + [vmem] * (len(kept) + 1),
-        out_specs=(vmem,) * 3,
-        out_shape=[jax.ShapeDtypeStruct(one, jnp.bfloat16) for one in (shape, shape[1:], shape[1:])],
+        out_specs=[vmem] * len(shapes),
+        out_shape=[jax.ShapeDtypeStruct(one, jnp.bfloat16) for one in shapes],
         compiler_params=pltpu.CompilerParams(vmem_limit_bytes=VMEM),
     )(*place, *kept, came)
 
@@ -403,7 +409,7 @@
     for z in range(lax.axis_size("src")):
         for chip in range(members // 2):
             for core in range(2):
-                tile = z ^ chip ^ ((2 + op) if core else (1 - op))
+                tile = z ^ chip ^ TURNS[op][core]
                 target = (z ^ (tile & 1)) * members + (z ^ (tile & 2)) * 2 + (core ^ flip)
                 pairs.append((z * members + chip * 2 + core, target))
     return lax.ppermute(value, ("src", "xl"), pairs)
@@ -444,8 +450,11 @@
         here = slice(first, first + count)
         kept = early if first + count == blocks else ()
         sums = tiles_of(place, far_other[here], [other[here], far_one[here]], sums, (early[1],), kept)
-    sums, send = sums
-    first, second, third = pairs_of(place, [*early, sums], swap(send, "xl", 1))
+    kept = [*early, sums[0]]
+    came = [swap(send, "xl", 1) for send in sums[1:]]
+    shape = came[0].shape
+    (first,) = pair_of(first_kernel_of_pair, place, kept, came[0], [shape])
+    second, third = pair_of(second_kernel_of_pair, place, kept, came[1], [shape[1:]] * 2)
     keep, send = halves_of(place, deliver(first, 0, 0))
     parts = [keep, swap(send, "xl", 1), deliver(second, 1, 0), deliver(third, 1, 1)]
     return sum(part.astype(jnp.float32) for part in parts) * weight

time: 30.6 us -> 30.2 us (0.987); the launches traced: 30.5 us -> 29.6 us
  waiting for transfers between devices: 5.48 us -> 4.47 us
    ppermute x3, waiting for transfers between devices: 1.56 us -> 1.02 us  [deliver(): return lax.ppermute(value, ('src', 'xl'), pairs)]
    ppermute x2 -> x3, waiting for transfers between devices: 1.52 us -> 1.06 us  [swap(): return lax.ppermute(value, axis, [(i, i ^ flip) for i in range(count)])]
    ppermute x2 -> x3, starting transfers between devices: 1.27 us -> 1.34 us  [swap(): return lax.ppermute(value, axis, [(i, i ^ flip) for i in range(count)])]
  transfers between devices with their start and end apart: 10 -> 11, of which waited for: 5 -> 7; matrix products, arithmetic and copies ran while one was open for 0% -> 0% of each run, Pallas kernels for 20% -> 21%
where the time goes in v6:
time: 30.2 us; the launch traced here: 29.6 us
  starting transfers between devices  15.3 us (51%)
  Pallas kernels  8.98 us (30%)
  waiting for transfers between devices  4.47 us (15%)
  other arithmetic  0.69 us (2%)
    ppermute x5, starting transfers between devices, cross(): lax.ppermute(value, 'src', [(z, z ^ (1 if side_of(z) ^ other else 2)) for...  8.46 us
    ppermute x3, starting transfers between devices, deliver(): return lax.ppermute(value, ('src', 'xl'), pairs)  5.51 us
    pallas_call x6, Pallas kernels, tiles_of(): pl.pallas_call(kernel, in_specs=[pl.BlockSpec(memory_space=pltpu.SMEM)] *...  4.83 us
    ppermute x5, waiting for transfers between devices, cross(): lax.ppermute(value, 'src', [(z, z ^ (1 if side_of(z) ^ other else 2)) for...  2.39 us
    pallas_call x1, Pallas kernels, first_spectra(): pl.pallas_call(functools.partial(first_kernel, blocks=blocks), in_specs=[...  2.11 us
    pallas_call x4, Pallas kernels, either_spectra(): pl.pallas_call(functools.partial(either_kernel, other=other, first=first,...  1.96 us
    ppermute x3, starting transfers between devices, swap(): return lax.ppermute(value, axis, [(i, i ^ flip) for i in range(count)])  1.34 us
    ppermute x3, waiting for transfers between devices, swap(): return lax.ppermute(value, axis, [(i, i ^ flip) for i in range(count)])  1.06 us
  transfers between devices with their start and end apart: 11, of which 7 were waited for; matrix products, arithmetic and copies ran while one was open for 0% of the time, Pallas kernels for 21%

profile of v6, /device:TPU:0, one launch (start us, length us, event | category | flops | bytes accessed | tf_op | source)
XLA Modules:
  0.0 29.6 jit_solution(12710866561071651080)
XLA Ops:
  0.0 2.1 %shard_map.46.refs_0_ = bf16[256,256]{1,0:T(8,128)(2,1)S(1)} custom-call(s32[1]{0:T(128)} %bitcast.1.side_ref, f32[16,4,8,1024]{3,2,1,0:T(8,128)} %bitcast.5, f32[4,16,8,1024]{3,2,1,0:T(8,128)} %bitcast.10, bf16[512,256]{1,0:T(8,128)(2,1)} %constant.50.clone.high_ref, bf16[512,256]{1,0:T(8,128)(2,1)} %constant.51.clone.low_ref), custom_call_target="tpu_custom_call" | custom-call | tf_op jit(solution)/shard_map/pallas_call | solution.py:100
  2.1 4.1 %collective-permute-start.1 = (bf16[256,256]{1,0:T(8,128)(2,1)S(1)}, bf16[256,256]{1,0:T(8,128)(2,1)S(1)}, u32[]{:S(2)}, u32[]{:S(2)}) collective-permute-start(bf16[256,256]{1,0:T(8,128)(2,1)S(1)} %shard_map.46.refs_0_), channel_id=1, source_target_pairs={{0,16},{8,0},{16,24},{24,8},{1,17},{9,1},{17,25},{25,9},{2,18},{10... | collective-permute-start | bytes 393224 | tf_op jit(solution)/shard_map/ppermute | solution.py:403
  6.3 0.6 %shard_map.47.refs_0_.refs_1_ = bf16[256,256]{1,0:T(8,128)(2,1)S(1)} custom-call(s32[1]{0:T(128)} %bitcast.1.side_ref, f32[16,4,8,1024]{3,2,1,0:T(8,128)S(1)} %bitcast.6, f32[4,16,8,1024]{3,2,1,0:T(8,128)S(1)} %bitcast.11, bf16[512,256]{1,0:T(8,128)(2,1)S(1)} %copy-done.3, bf16[512,256]{1,0:T(8,128)(2,1)S(1)} %copy-done.2, ...), custom_call_target="tpu_custom_call" | custom-call | flops 256 | bytes 256 | tf_op jit(solution)/shard_map/pallas_call | solution.py:131
  6.9 1.6 %collective-permute-start = (bf16[256,256]{1,0:T(8,128)(2,1)S(1)}, bf16[256,256]{1,0:T(8,128)(2,1)S(1)}, u32[]{:S(2)}, u32[]{:S(2)}) collective-permute-start(bf16[256,256]{1,0:T(8,128)(2,1)S(1)} %shard_map.47.refs_0_.refs_1_), channel_id=1, source_target_pairs={{0,16},{8,0},{16,24},{24,8},{1,17},{9,1},{17,25},{25,9},{2,18},{10... | collective-permute-start | bytes 393224 | tf_op jit(solution)/shard_map/ppermute | solution.py:403
  8.5 0.6 %shard_map.48.refs_0_.refs_2_.refs_1_ = bf16[256,256]{1,0:T(8,128)(2,1)S(1)} custom-call(s32[1]{0:T(128)} %bitcast.1.side_ref, f32[16,4,8,1024]{3,2,1,0:T(8,128)S(1)} %bitcast.7, f32[4,16,8,1024]{3,2,1,0:T(8,128)S(1)} %bitcast.12, bf16[512,256]{1,0:T(8,128)(2,1)S(1)} %copy-done.3, bf16[512,256]{1,0:T(8,128)(2,1)S(1)} %copy-done.2, ...), custom_call_target="tpu_custom_call" | custom-call | flops 256 | bytes 256 | tf_op jit(solution)/shard_map/pallas_call | solution.py:131
  9.1 0.5 %collective-permute-start.4 = (bf16[256,256]{1,0:T(8,128)(2,1)S(1)}, bf16[256,256]{1,0:T(8,128)(2,1)S(1)}, u32[]{:S(2)}, u32[]{:S(2)}) collective-permute-start(bf16[256,256]{1,0:T(8,128)(2,1)S(1)} %shard_map.48.refs_0_.refs_2_.refs_1_), channel_id=1, source_target_pairs={{0,8},{8,24},{16,0},{24,16},{1,9},{9,25},{17,1},{25,17},{2,10},{10... | collective-permute-start | bytes 393224 | tf_op jit(solution)/shard_map/ppermute | solution.py:403
  10.0 0.5 %collective-permute-start.3 = (bf16[128,256]{1,0:T(8,128)(2,1)S(1)}, bf16[128,256]{1,0:T(8,128)(2,1)S(1)}, u32[]{:S(2)}, u32[]{:S(2)}) collective-permute-start(bf16[128,256]{1,0:T(8,128)(2,1)S(1)} %shard_map.49.refs_0_.refs_3_.refs_1_), channel_id=1, source_target_pairs={{0,8},{8,24},{16,0},{24,16},{1,9},{9,25},{17,1},{25,17},{2,10},{10... | collective-permute-start | bytes 196616 | tf_op jit(solution)/shard_map/ppermute | solution.py:403
  10.5 0.4 %shard_map.50.refs_4_.refs_5_.refs_3_ = bf16[128,256]{1,0:T(8,128)(2,1)S(1)} custom-call(s32[1]{0:T(128)} %bitcast.1.side_ref, f32[16,4,8,1024]{3,2,1,0:T(8,128)S(1)} %bitcast.9, f32[4,16,8,1024]{3,2,1,0:T(8,128)S(1)} %bitcast.14, bf16[512,256]{1,0:T(8,128)(2,1)S(1)} %copy-done.3, bf16[512,256]{1,0:T(8,128)(2,1)S(1)} %copy-done.2, ...), custom_call_target="tpu_custom_call" | custom-call | flops 128 | bytes 128 | tf_op jit(solution)/shard_map/pallas_call | solution.py:131
  10.9 1.7 %collective-permute-start.2 = (bf16[128,256]{1,0:T(8,128)(2,1)S(1)}, bf16[128,256]{1,0:T(8,128)(2,1)S(1)}, u32[]{:S(2)}, u32[]{:S(2)}) collective-permute-start(bf16[128,256]{1,0:T(8,128)(2,1)S(1)} %shard_map.50.refs_4_.refs_5_.refs_3_), channel_id=1, source_target_pairs={{0,8},{8,24},{16,0},{24,16},{1,9},{9,25},{17,1},{25,17},{2,10},{10... | collective-permute-start | bytes 196616 | tf_op jit(solution)/shard_map/ppermute | solution.py:403
  12.6 1.2 %shard_map.51.refs_2_.refs_0_ = f32[1,2,16,8,256]{4,3,2,1,0:T(8,128)S(1)} custom-call(s32[1]{0:T(128)} %bitcast.1.side_ref, bf16[256,256]{1,0:T(8,128)(2,1)S(1)} %shard_map.46.refs_0_, bf16[256,256]{1,0:T(8,128)(2,1)S(1)} %shard_map.47.refs_0_.refs_1_, bf16[256,256]{1,0:T(8,128)(2,1)S(1)} %shard_map.48.refs_0_.refs_2_.refs_1_, ...), custom_call_target="tpu_custom_call" | custom-call | flops 1 | bytes 1 | tf_op jit(solution)/shard_map/pallas_call | solution.py:276
  13.8 0.6 %shard_map.52.refs_2_ = f32[1,2,16,8,256]{4,3,2,1,0:T(8,128)S(1)} custom-call(s32[1]{0:T(128)} %bitcast.1.side_ref, bf16[256,256]{1,0:T(8,128)(2,1)S(1)} %shard_map.46.refs_0_, bf16[256,256]{1,0:T(8,128)(2,1)S(1)} %collective-permute-done.1.refs_1_.refs_2_, f32[1,2,16,8,256]{4,3,2,1,0:T(8,128)S(1)} %shard_map.51.refs_2_.refs_0_), custom_call_target="tpu_custom_call" | custom-call | flops 1 | bytes 1 | tf_op jit(solution)/shard_map/pallas_call | solution.py:276
  14.5 0.6 %shard_map.53.refs_3_.refs_4_.refs_1_.refs_6_ = f32[1,2,16,8,256]{4,3,2,1,0:T(8,128)S(1)} custom-call(s32[1]{0:T(128)} %bitcast.1.side_ref, bf16[256,256]{1,0:T(8,128)(2,1)S(1)} %shard_map.47.refs_0_.refs_1_, bf16[256,256]{1,0:T(8,128)(2,1)S(1)} %collective-permute-done.refs_1_.refs_2_.refs_4_, f32[1,2,16,8,256]{4,3,2,1,0:T(8,128)S(1)} %shard_map.52.refs_2_), custom_call_target="tpu_custom_call" | custom-call | flops 1 | bytes 1 | tf_op jit(solution)/shard_map/pallas_call | solution.py:276
  15.1 2.0 %collective-permute-done.4.refs_0_ = bf16[256,256]{1,0:T(8,128)(2,1)S(1)} collective-permute-done((bf16[256,256]{1,0:T(8,128)(2,1)S(1)}, bf16[256,256]{1,0:T(8,128)(2,1)S(1)}, u32[]{:S(2)}, u32[]{:S(2)}) %collective-permute-start.4) | collective-permute-done | bytes 131104 | tf_op jit(solution)/shard_map/ppermute | solution.py:403
  17.0 1.2 %shard_map.54.refs_3_ = f32[2,2,16,8,256]{4,3,2,1,0:T(8,128)S(1)} custom-call(s32[1]{0:T(128)} %bitcast.1.side_ref, bf16[256,256]{1,0:T(8,128)(2,1)S(1)} %collective-permute-done.4.refs_0_, bf16[256,256]{1,0:T(8,128)(2,1)S(1)} %shard_map.48.refs_0_.refs_2_.refs_1_, bf16[256,256]{1,0:T(8,128)(2,1)S(1)} %collective-permute-done.1.refs_1_.refs_2_, ...), custom_call_target="tpu_custom_call" | custom-call | flops 2 | bytes 2 | tf_op jit(solution)/shard_map/pallas_call | solution.py:276
  18.5 0.6 %shard_map.55.refs_5_ = f32[2,2,16,8,256]{4,3,2,1,0:T(8,128)S(1)} custom-call(s32[1]{0:T(128)} %bitcast.1.side_ref, bf16[128,256]{1,0:T(8,128)(2,1)S(1)} %collective-permute-done.3.refs_0_, bf16[128,256]{1,0:T(8,128)(2,1)S(1)} %shard_map.49.refs_0_.refs_3_.refs_1_, bf16[256,256]{1,0:T(8,128)(2,1)S(1)} %collective-permute-done.refs_1_.refs_2_.refs_4_, ...), custom_call_target="tpu_custom_call" | custom-call | flops 2 | bytes 2 | tf_op jit(solution)/shard_map/pallas_call | solution.py:276
  19.2 0.7 %shard_map.56 = (f32[2,2,16,8,256]{4,3,2,1,0:T(8,128)S(1)}, bf16[2,16,8,256]{3,2,1,0:T(8,128)(2,1)S(1)}, bf16[2,16,8,256]{3,2,1,0:T(8,128)(2,1)S(1)}) custom-call(s32[1]{0:T(128)} %bitcast.1.side_ref, s32[1]{0:T(128)} %bitcast.core_ref, s32[1]{0:T(128)} %bitcast.2.turn_ref, f32[1,2,16,8,256]{4,3,2,1,0:T(8,128)S(1)} %shard_map.51.refs_2_.refs_0_, ...), custom_call_target="tpu_custom_call" | custom-call | flops 2 | bytes 2 | tf_op jit(solution)/shard_map/pallas_call | solution.py:276
  20.0 0.5 %collective-permute-start.8 = (bf16[2,16,8,256]{3,2,1,0:T(8,128)(2,1)S(1)}, bf16[2,16,8,256]{3,2,1,0:T(8,128)(2,1)S(1)}, u32[]{:S(2)}, u32[]{:S(2)}) collective-permute-start(bf16[2,16,8,256]{3,2,1,0:T(8,128)(2,1)S(1)} %get-tuple-element.16), channel_id=1, source_target_pairs={{0,1},{1,0},{2,3},{3,2},{4,5},{5,4},{6,7},{7,6},{8,9},{9,8},{10,11... | collective-permute-start | bytes 393224 | tf_op jit(solution)/shard_map/ppermute | solution.py:395
  20.5 0.8 %collective-permute-done.5.refs_3_ = bf16[2,16,8,256]{3,2,1,0:T(8,128)(2,1)S(1)} collective-permute-done((bf16[2,16,8,256]{3,2,1,0:T(8,128)(2,1)S(1)}, bf16[2,16,8,256]{3,2,1,0:T(8,128)(2,1)S(1)}, u32[]{:S(2)}, u32[]{:S(2)}) %collective-permute-start.5) | collective-permute-done | bytes 131104 | tf_op jit(solution)/shard_map/ppermute | solution.py:395
  21.3 1.7 %collective-permute-start.6 = (bf16[2,16,8,256]{3,2,1,0:T(8,128)(2,1)S(1)}, bf16[2,16,8,256]{3,2,1,0:T(8,128)(2,1)S(1)}, u32[]{:S(2)}, u32[]{:S(2)}) collective-permute-start(bf16[2,16,8,256]{3,2,1,0:T(8,128)(2,1)S(1)} %shard_map.57), channel_id=1, source_target_pairs={{0,12},{1,5},{2,4},{3,13},{4,8},{5,1},{6,0},{7,9},{8,14},{9,7},{10... | collective-permute-start | bytes 393224 | tf_op jit(solution)/shard_map/ppermute | solution.py:415
  23.1 0.7 %collective-permute-start.9 = (bf16[16,8,256]{2,1,0:T(8,128)(2,1)S(1)}, bf16[16,8,256]{2,1,0:T(8,128)(2,1)S(1)}, u32[]{:S(2)}, u32[]{:S(2)}) collective-permute-start(bf16[16,8,256]{2,1,0:T(8,128)(2,1)S(1)} %get-tuple-element.17), channel_id=1, source_target_pairs={{0,0},{1,9},{2,8},{3,1},{4,4},{5,13},{6,12},{7,5},{8,2},{9,11},{10... | collective-permute-start | bytes 196616 | tf_op jit(solution)/shard_map/ppermute | solution.py:415
  23.8 3.1 %collective-permute-start.10 = (bf16[16,8,256]{2,1,0:T(8,128)(2,1)S(1)}, bf16[16,8,256]{2,1,0:T(8,128)(2,1)S(1)}, u32[]{:S(2)}, u32[]{:S(2)}) collective-permute-start(bf16[16,8,256]{2,1,0:T(8,128)(2,1)S(1)} %get-tuple-element.18), channel_id=1, source_target_pairs={{0,1},{1,8},{2,9},{3,0},{4,5},{5,12},{6,13},{7,4},{8,3},{9,10},{10... | collective-permute-start | bytes 196616 | tf_op jit(solution)/shard_map/ppermute | solution.py:415
  27.3 0.8 %collective-permute-start.7 = (bf16[16,8,256]{2,1,0:T(8,128)(2,1)S(1)}, bf16[16,8,256]{2,1,0:T(8,128)(2,1)S(1)}, u32[]{:S(2)}, u32[]{:S(2)}) collective-permute-start(bf16[16,8,256]{2,1,0:T(8,128)(2,1)S(1)} %get-tuple-element.15), channel_id=1, source_target_pairs={{0,1},{1,0},{2,3},{3,2},{4,5},{5,4},{6,7},{7,6},{8,9},{9,8},{10,11... | collective-permute-start | bytes 196616 | tf_op jit(solution)/shard_map/ppermute | solution.py:395
  28.0 0.7 %collective-permute-done.10 = bf16[16,8,256]{2,1,0:T(8,128)(2,1)S(1)} collective-permute-done((bf16[16,8,256]{2,1,0:T(8,128)(2,1)S(1)}, bf16[16,8,256]{2,1,0:T(8,128)(2,1)S(1)}, u32[]{:S(2)}, u32[]{:S(2)}) %collective-permute-start.10) | collective-permute-done | bytes 65568 | tf_op jit(solution)/shard_map/ppermute | solution.py:415
  28.9 0.7 %add_multiply_fusion = f32[16,8,256]{2,1,0:T(8,128)} fusion(bf16[16,8,256]{2,1,0:T(8,128)(2,1)S(1)} %collective-permute-done.10, bf16[16,8,256]{2,1,0:T(8,128)(2,1)S(1)} %collective-permute-done.9, bf16[16,8,256]{2,1,0:T(8,128)(2,1)S(1)} %collective-permute-done.7, bf16[16,8,256]{2,1,0:T(8,128)(2,1)S(1)} %get-tuple-element.14), kind=kLoop, calls=%fused_computation | loop fusion | flops 262144 | bytes 393216 | tf_op jit(solution)/shard_map/mul | solution.py:460
  (21 shorter events, 1.5 us)
Async XLA Ops:
  0.0 6.2 %copy-start = (f32[16,32,1024]{2,1,0:T(8,128)S(1)}, f32[16,32,1024]{2,1,0:T(8,128)}, u32[]{:S(2)}) copy-start(f32[16,32,1024]{2,1,0:T(8,128)} %param.4) | copy-start | bytes 6291460
  0.0 6.2 %copy-start.1 = (f32[32,16,1024]{2,1,0:T(8,128)S(1)}, f32[32,16,1024]{2,1,0:T(8,128)}, u32[]{:S(2)}) copy-start(f32[32,16,1024]{2,1,0:T(8,128)} %param.5) | copy-start | bytes 6291460
  0.0 6.2 %copy-start.2 = (bf16[512,256]{1,0:T(8,128)(2,1)S(1)}, bf16[512,256]{1,0:T(8,128)(2,1)}, u32[]{:S(2)}) copy-start(bf16[512,256]{1,0:T(8,128)(2,1)} %constant.51.clone.low_ref) | copy-start | bytes 786436
  0.0 6.2 %copy-start.3 = (bf16[512,256]{1,0:T(8,128)(2,1)S(1)}, bf16[512,256]{1,0:T(8,128)(2,1)}, u32[]{:S(2)}) copy-start(bf16[512,256]{1,0:T(8,128)(2,1)} %constant.50.clone.high_ref) | copy-start | bytes 786436
  2.1 11.7 %collective-permute-start.1 = (bf16[256,256]{1,0:T(8,128)(2,1)S(1)}, bf16[256,256]{1,0:T(8,128)(2,1)S(1)}, u32[]{:S(2)}, u32[]{:S(2)}) collective-permute-start(bf16[256,256]{1,0:T(8,128)(2,1)S(1)} %shard_map.46.refs_0_), channel_id=1, source_target_pairs={{0,16},{8,0},{16,24},{24,8},{1,17},{9,1},{17,25},{25,9},{2,18},{10... | collective-permute-start | bytes 393224 | tf_op jit(solution)/shard_map/ppermute | solution.py:403
  6.9 7.6 %collective-permute-start = (bf16[256,256]{1,0:T(8,128)(2,1)S(1)}, bf16[256,256]{1,0:T(8,128)(2,1)S(1)}, u32[]{:S(2)}, u32[]{:S(2)}) collective-permute-start(bf16[256,256]{1,0:T(8,128)(2,1)S(1)} %shard_map.47.refs_0_.refs_1_), channel_id=1, source_target_pairs={{0,16},{8,0},{16,24},{24,8},{1,17},{9,1},{17,25},{25,9},{2,18},{10... | collective-permute-start | bytes 393224 | tf_op jit(solution)/shard_map/ppermute | solution.py:403
  9.1 8.0 %collective-permute-start.4 = (bf16[256,256]{1,0:T(8,128)(2,1)S(1)}, bf16[256,256]{1,0:T(8,128)(2,1)S(1)}, u32[]{:S(2)}, u32[]{:S(2)}) collective-permute-start(bf16[256,256]{1,0:T(8,128)(2,1)S(1)} %shard_map.48.refs_0_.refs_2_.refs_1_), channel_id=1, source_target_pairs={{0,8},{8,24},{16,0},{24,16},{1,9},{9,25},{17,1},{25,17},{2,10},{10... | collective-permute-start | bytes 393224 | tf_op jit(solution)/shard_map/ppermute | solution.py:403
  10.0 8.5 %collective-permute-start.3 = (bf16[128,256]{1,0:T(8,128)(2,1)S(1)}, bf16[128,256]{1,0:T(8,128)(2,1)S(1)}, u32[]{:S(2)}, u32[]{:S(2)}) collective-permute-start(bf16[128,256]{1,0:T(8,128)(2,1)S(1)} %shard_map.49.refs_0_.refs_3_.refs_1_), channel_id=1, source_target_pairs={{0,8},{8,24},{16,0},{24,16},{1,9},{9,25},{17,1},{25,17},{2,10},{10... | collective-permute-start | bytes 196616 | tf_op jit(solution)/shard_map/ppermute | solution.py:403
  10.9 8.4 %collective-permute-start.2 = (bf16[128,256]{1,0:T(8,128)(2,1)S(1)}, bf16[128,256]{1,0:T(8,128)(2,1)S(1)}, u32[]{:S(2)}, u32[]{:S(2)}) collective-permute-start(bf16[128,256]{1,0:T(8,128)(2,1)S(1)} %shard_map.50.refs_4_.refs_5_.refs_3_), channel_id=1, source_target_pairs={{0,8},{8,24},{16,0},{24,16},{1,9},{9,25},{17,1},{25,17},{2,10},{10... | collective-permute-start | bytes 196616 | tf_op jit(solution)/shard_map/ppermute | solution.py:403
  19.9 1.4 %collective-permute-start.5 = (bf16[2,16,8,256]{3,2,1,0:T(8,128)(2,1)S(1)}, bf16[2,16,8,256]{3,2,1,0:T(8,128)(2,1)S(1)}, u32[]{:S(2)}, u32[]{:S(2)}) collective-permute-start(bf16[2,16,8,256]{3,2,1,0:T(8,128)(2,1)S(1)} %get-tuple-element.13), channel_id=1, source_target_pairs={{0,1},{1,0},{2,3},{3,2},{4,5},{5,4},{6,7},{7,6},{8,9},{9,8},{10,11... | collective-permute-start | bytes 393224 | tf_op jit(solution)/shard_map/ppermute | solution.py:395
  20.0 3.1 %collective-permute-start.8 = (bf16[2,16,8,256]{3,2,1,0:T(8,128)(2,1)S(1)}, bf16[2,16,8,256]{3,2,1,0:T(8,128)(2,1)S(1)}, u32[]{:S(2)}, u32[]{:S(2)}) collective-permute-start(bf16[2,16,8,256]{3,2,1,0:T(8,128)(2,1)S(1)} %get-tuple-element.16), channel_id=1, source_target_pairs={{0,1},{1,0},{2,3},{3,2},{4,5},{5,4},{6,7},{7,6},{8,9},{9,8},{10,11... | collective-permute-start | bytes 393224 | tf_op jit(solution)/shard_map/ppermute | solution.py:395
  21.3 5.9 %collective-permute-start.6 = (bf16[2,16,8,256]{3,2,1,0:T(8,128)(2,1)S(1)}, bf16[2,16,8,256]{3,2,1,0:T(8,128)(2,1)S(1)}, u32[]{:S(2)}, u32[]{:S(2)}) collective-permute-start(bf16[2,16,8,256]{3,2,1,0:T(8,128)(2,1)S(1)} %shard_map.57), channel_id=1, source_target_pairs={{0,12},{1,5},{2,4},{3,13},{4,8},{5,1},{6,0},{7,9},{8,14},{9,7},{10... | collective-permute-start | bytes 393224 | tf_op jit(solution)/shard_map/ppermute | solution.py:415
  23.1 4.9 %collective-permute-start.9 = (bf16[16,8,256]{2,1,0:T(8,128)(2,1)S(1)}, bf16[16,8,256]{2,1,0:T(8,128)(2,1)S(1)}, u32[]{:S(2)}, u32[]{:S(2)}) collective-permute-start(bf16[16,8,256]{2,1,0:T(8,128)(2,1)S(1)} %get-tuple-element.17), channel_id=1, source_target_pairs={{0,0},{1,9},{2,8},{3,1},{4,4},{5,13},{6,12},{7,5},{8,2},{9,11},{10... | collective-permute-start | bytes 196616 | tf_op jit(solution)/shard_map/ppermute | solution.py:415
  23.8 4.9 %collective-permute-start.10 = (bf16[16,8,256]{2,1,0:T(8,128)(2,1)S(1)}, bf16[16,8,256]{2,1,0:T(8,128)(2,1)S(1)}, u32[]{:S(2)}, u32[]{:S(2)}) collective-permute-start(bf16[16,8,256]{2,1,0:T(8,128)(2,1)S(1)} %get-tuple-element.18), channel_id=1, source_target_pairs={{0,1},{1,8},{2,9},{3,0},{4,5},{5,12},{6,13},{7,4},{8,3},{9,10},{10... | collective-permute-start | bytes 196616 | tf_op jit(solution)/shard_map/ppermute | solution.py:415
  27.3 1.7 %collective-permute-start.7 = (bf16[16,8,256]{2,1,0:T(8,128)(2,1)S(1)}, bf16[16,8,256]{2,1,0:T(8,128)(2,1)S(1)}, u32[]{:S(2)}, u32[]{:S(2)}) collective-permute-start(bf16[16,8,256]{2,1,0:T(8,128)(2,1)S(1)} %get-tuple-element.15), channel_id=1, source_target_pairs={{0,1},{1,0},{2,3},{3,2},{4,5},{5,4},{6,7},{7,6},{8,9},{9,8},{10,11... | collective-permute-start | bytes 196616 | tf_op jit(solution)/shard_map/ppermute | solution.py:395

commit v7 on v6

--- a/solution.py
+++ b/solution.py
@@ -438,18 +438,17 @@
         far = cross(token, 1)
         other += [(token, i) for i in range(count)]
         far_other += [(far, i) for i in range(count)]
-    early = [tiles_of(place, one, [other], after=(token,))]
-    sums, after = None, (early[0],)
+    sums, after = None, (token,)
     for first, count in ONES:
         here = slice(first, first + count)
         sums = tiles_of(place, one[here], [far_one[here]], sums, after)
         after = ()
-    early.append(sums)
+    early = [tiles_of(place, one, [other], after=(sums,)), sums]
     sums = None
     for first, count in OTHERS:
         here = slice(first, first + count)
         kept = early if first + count == blocks else ()
-        sums = tiles_of(place, far_other[here], [other[here], far_one[here]], sums, (early[1],), kept)
+        sums = tiles_of(place, far_other[here], [other[here], far_one[here]], sums, (early[0],), kept)
     kept = [*early, sums[0]]
     came = [swap(send, "xl", 1) for send in sums[1:]]
     shape = came[0].shape

time: 30.2 us -> 30.2 us (level)
  no operation moved by 1% of the time
where the time goes in v7:
time: 30.2 us; the launch traced here: 29.6 us
  starting transfers between devices  15.3 us (51%)
  Pallas kernels  8.97 us (30%)
  waiting for transfers between devices  4.5 us (15%)
  other arithmetic  0.69 us (2%)
    ppermute x5, starting transfers between devices, cross(): lax.ppermute(value, 'src', [(z, z ^ (1 if side_of(z) ^ other else 2)) for...  8.46 us
    ppermute x3, starting transfers between devices, deliver(): return lax.ppermute(value, ('src', 'xl'), pairs)  5.52 us
    pallas_call x6, Pallas kernels, tiles_of(): pl.pallas_call(kernel, in_specs=[pl.BlockSpec(memory_space=pltpu.SMEM)] *...  4.83 us
    ppermute x5, waiting for transfers between devices, cross(): lax.ppermute(value, 'src', [(z, z ^ (1 if side_of(z) ^ other else 2)) for...  2.41 us
    pallas_call x1, Pallas kernels, first_spectra(): pl.pallas_call(functools.partial(first_kernel, blocks=blocks), in_specs=[...  2.11 us
    pallas_call x4, Pallas kernels, either_spectra(): pl.pallas_call(functools.partial(either_kernel, other=other, first=first,...  1.96 us
    ppermute x3, starting transfers between devices, swap(): return lax.ppermute(value, axis, [(i, i ^ flip) for i in range(count)])  1.35 us
    ppermute x3, waiting for transfers between devices, swap(): return lax.ppermute(value, axis, [(i, i ^ flip) for i in range(count)])  1.07 us
  transfers between devices with their start and end apart: 11, of which 7 were waited for; matrix products, arithmetic and copies ran while one was open for 0% of the time, Pallas kernels for 21%

profile of v7, /device:TPU:0, one launch (start us, length us, event | category | flops | bytes accessed | tf_op | source)
XLA Modules:
  0.0 29.6 jit_solution(10139790281725300891)
XLA Ops:
  0.0 2.1 %shard_map.46.refs_0_ = bf16[256,256]{1,0:T(8,128)(2,1)S(1)} custom-call(s32[1]{0:T(128)} %bitcast.1.side_ref, f32[16,4,8,1024]{3,2,1,0:T(8,128)} %bitcast.5, f32[4,16,8,1024]{3,2,1,0:T(8,128)} %bitcast.10, bf16[512,256]{1,0:T(8,128)(2,1)} %constant.50.clone.high_ref, bf16[512,256]{1,0:T(8,128)(2,1)} %constant.51.clone.low_ref), custom_call_target="tpu_custom_call" | custom-call | tf_op jit(solution)/shard_map/pallas_call | solution.py:100
  2.1 4.1 %collective-permute-start.1 = (bf16[256,256]{1,0:T(8,128)(2,1)S(1)}, bf16[256,256]{1,0:T(8,128)(2,1)S(1)}, u32[]{:S(2)}, u32[]{:S(2)}) collective-permute-start(bf16[256,256]{1,0:T(8,128)(2,1)S(1)} %shard_map.46.refs_0_), channel_id=1, source_target_pairs={{0,16},{8,0},{16,24},{24,8},{1,17},{9,1},{17,25},{25,9},{2,18},{10... | collective-permute-start | bytes 393224 | tf_op jit(solution)/shard_map/ppermute | solution.py:403
  6.3 0.6 %shard_map.47.refs_0_.refs_1_ = bf16[256,256]{1,0:T(8,128)(2,1)S(1)} custom-call(s32[1]{0:T(128)} %bitcast.1.side_ref, f32[16,4,8,1024]{3,2,1,0:T(8,128)S(1)} %bitcast.6, f32[4,16,8,1024]{3,2,1,0:T(8,128)S(1)} %bitcast.11, bf16[512,256]{1,0:T(8,128)(2,1)S(1)} %copy-done.3, bf16[512,256]{1,0:T(8,128)(2,1)S(1)} %copy-done.2, ...), custom_call_target="tpu_custom_call" | custom-call | flops 256 | bytes 256 | tf_op jit(solution)/shard_map/pallas_call | solution.py:131
  6.9 1.6 %collective-permute-start = (bf16[256,256]{1,0:T(8,128)(2,1)S(1)}, bf16[256,256]{1,0:T(8,128)(2,1)S(1)}, u32[]{:S(2)}, u32[]{:S(2)}) collective-permute-start(bf16[256,256]{1,0:T(8,128)(2,1)S(1)} %shard_map.47.refs_0_.refs_1_), channel_id=1, source_target_pairs={{0,16},{8,0},{16,24},{24,8},{1,17},{9,1},{17,25},{25,9},{2,18},{10... | collective-permute-start | bytes 393224 | tf_op jit(solution)/shard_map/ppermute | solution.py:403
  8.5 0.6 %shard_map.48.refs_0_.refs_2_.refs_1_ = bf16[256,256]{1,0:T(8,128)(2,1)S(1)} custom-call(s32[1]{0:T(128)} %bitcast.1.side_ref, f32[16,4,8,1024]{3,2,1,0:T(8,128)S(1)} %bitcast.7, f32[4,16,8,1024]{3,2,1,0:T(8,128)S(1)} %bitcast.12, bf16[512,256]{1,0:T(8,128)(2,1)S(1)} %copy-done.3, bf16[512,256]{1,0:T(8,128)(2,1)S(1)} %copy-done.2, ...), custom_call_target="tpu_custom_call" | custom-call | flops 256 | bytes 256 | tf_op jit(solution)/shard_map/pallas_call | solution.py:131
  9.1 0.5 %collective-permute-start.4 = (bf16[256,256]{1,0:T(8,128)(2,1)S(1)}, bf16[256,256]{1,0:T(8,128)(2,1)S(1)}, u32[]{:S(2)}, u32[]{:S(2)}) collective-permute-start(bf16[256,256]{1,0:T(8,128)(2,1)S(1)} %shard_map.48.refs_0_.refs_2_.refs_1_), channel_id=1, source_target_pairs={{0,8},{8,24},{16,0},{24,16},{1,9},{9,25},{17,1},{25,17},{2,10},{10... | collective-permute-start | bytes 393224 | tf_op jit(solution)/shard_map/ppermute | solution.py:403
  10.0 0.5 %collective-permute-start.3 = (bf16[128,256]{1,0:T(8,128)(2,1)S(1)}, bf16[128,256]{1,0:T(8,128)(2,1)S(1)}, u32[]{:S(2)}, u32[]{:S(2)}) collective-permute-start(bf16[128,256]{1,0:T(8,128)(2,1)S(1)} %shard_map.49.refs_0_.refs_3_.refs_1_), channel_id=1, source_target_pairs={{0,8},{8,24},{16,0},{24,16},{1,9},{9,25},{17,1},{25,17},{2,10},{10... | collective-permute-start | bytes 196616 | tf_op jit(solution)/shard_map/ppermute | solution.py:403
  10.5 0.4 %shard_map.50.refs_2_.refs_4_.refs_3_ = bf16[128,256]{1,0:T(8,128)(2,1)S(1)} custom-call(s32[1]{0:T(128)} %bitcast.1.side_ref, f32[16,4,8,1024]{3,2,1,0:T(8,128)S(1)} %bitcast.9, f32[4,16,8,1024]{3,2,1,0:T(8,128)S(1)} %bitcast.14, bf16[512,256]{1,0:T(8,128)(2,1)S(1)} %copy-done.3, bf16[512,256]{1,0:T(8,128)(2,1)S(1)} %copy-done.2, ...), custom_call_target="tpu_custom_call" | custom-call | flops 128 | bytes 128 | tf_op jit(solution)/shard_map/pallas_call | solution.py:131
  10.9 1.7 %collective-permute-start.2 = (bf16[128,256]{1,0:T(8,128)(2,1)S(1)}, bf16[128,256]{1,0:T(8,128)(2,1)S(1)}, u32[]{:S(2)}, u32[]{:S(2)}) collective-permute-start(bf16[128,256]{1,0:T(8,128)(2,1)S(1)} %shard_map.50.refs_2_.refs_4_.refs_3_), channel_id=1, source_target_pairs={{0,8},{8,24},{16,0},{24,16},{1,9},{9,25},{17,1},{25,17},{2,10},{10... | collective-permute-start | bytes 196616 | tf_op jit(solution)/shard_map/ppermute | solution.py:403
  12.6 0.6 %shard_map.51.refs_2_ = f32[1,2,16,8,256]{4,3,2,1,0:T(8,128)S(1)} custom-call(s32[1]{0:T(128)} %bitcast.1.side_ref, bf16[256,256]{1,0:T(8,128)(2,1)S(1)} %shard_map.46.refs_0_, bf16[256,256]{1,0:T(8,128)(2,1)S(1)} %collective-permute-done.1.refs_1_.refs_2_, bf16[128,256]{1,0:T(8,128)(2,1)S(1)} %shard_map.50.refs_2_.refs_4_.refs_3_), custom_call_target="tpu_custom_call" | custom-call | flops 1 | bytes 1 | tf_op jit(solution)/shard_map/pallas_call | solution.py:276
  13.2 0.6 %shard_map.52.refs_5_.refs_1_ = f32[1,2,16,8,256]{4,3,2,1,0:T(8,128)S(1)} custom-call(s32[1]{0:T(128)} %bitcast.1.side_ref, bf16[256,256]{1,0:T(8,128)(2,1)S(1)} %shard_map.47.refs_0_.refs_1_, bf16[256,256]{1,0:T(8,128)(2,1)S(1)} %collective-permute-done.refs_1_.refs_2_.refs_4_, f32[1,2,16,8,256]{4,3,2,1,0:T(8,128)S(1)} %shard_map.51.refs_2_), custom_call_target="tpu_custom_call" | custom-call | flops 1 | bytes 1 | tf_op jit(solution)/shard_map/pallas_call | solution.py:276
  13.8 1.2 %shard_map.53.refs_3_.refs_4_.refs_0_.refs_6_ = f32[1,2,16,8,256]{4,3,2,1,0:T(8,128)S(1)} custom-call(s32[1]{0:T(128)} %bitcast.1.side_ref, bf16[256,256]{1,0:T(8,128)(2,1)S(1)} %shard_map.46.refs_0_, bf16[256,256]{1,0:T(8,128)(2,1)S(1)} %shard_map.47.refs_0_.refs_1_, bf16[256,256]{1,0:T(8,128)(2,1)S(1)} %shard_map.48.refs_0_.refs_2_.refs_1_, ...), custom_call_target="tpu_custom_call" | custom-call | flops 1 | bytes 1 | tf_op jit(solution)/shard_map/pallas_call | solution.py:276
  15.1 2.0 %collective-permute-done.4.refs_0_ = bf16[256,256]{1,0:T(8,128)(2,1)S(1)} collective-permute-done((bf16[256,256]{1,0:T(8,128)(2,1)S(1)}, bf16[256,256]{1,0:T(8,128)(2,1)S(1)}, u32[]{:S(2)}, u32[]{:S(2)}) %collective-permute-start.4) | collective-permute-done | bytes 131104 | tf_op jit(solution)/shard_map/ppermute | solution.py:403
  17.0 1.2 %shard_map.54.refs_3_ = f32[2,2,16,8,256]{4,3,2,1,0:T(8,128)S(1)} custom-call(s32[1]{0:T(128)} %bitcast.1.side_ref, bf16[256,256]{1,0:T(8,128)(2,1)S(1)} %collective-permute-done.4.refs_0_, bf16[256,256]{1,0:T(8,128)(2,1)S(1)} %shard_map.48.refs_0_.refs_2_.refs_1_, bf16[256,256]{1,0:T(8,128)(2,1)S(1)} %collective-permute-done.1.refs_1_.refs_2_, ...), custom_call_target="tpu_custom_call" | custom-call | flops 2 | bytes 2 | tf_op jit(solution)/shard_map/pallas_call | solution.py:276
  18.5 0.6 %shard_map.55.refs_5_ = f32[2,2,16,8,256]{4,3,2,1,0:T(8,128)S(1)} custom-call(s32[1]{0:T(128)} %bitcast.1.side_ref, bf16[128,256]{1,0:T(8,128)(2,1)S(1)} %collective-permute-done.3.refs_0_, bf16[128,256]{1,0:T(8,128)(2,1)S(1)} %shard_map.49.refs_0_.refs_3_.refs_1_, bf16[256,256]{1,0:T(8,128)(2,1)S(1)} %collective-permute-done.refs_1_.refs_2_.refs_4_, ...), custom_call_target="tpu_custom_call" | custom-call | flops 2 | bytes 2 | tf_op jit(solution)/shard_map/pallas_call | solution.py:276
  19.2 0.7 %shard_map.56 = (f32[2,2,16,8,256]{4,3,2,1,0:T(8,128)S(1)}, bf16[2,16,8,256]{3,2,1,0:T(8,128)(2,1)S(1)}, bf16[2,16,8,256]{3,2,1,0:T(8,128)(2,1)S(1)}) custom-call(s32[1]{0:T(128)} %bitcast.1.side_ref, s32[1]{0:T(128)} %bitcast.core_ref, s32[1]{0:T(128)} %bitcast.2.turn_ref, f32[1,2,16,8,256]{4,3,2,1,0:T(8,128)S(1)} %shard_map.53.refs_3_.refs_4_.refs_0_.refs_6_, ...), custom_call_target="tpu_custom_call" | custom-call | flops 2 | bytes 2 | tf_op jit(solution)/shard_map/pallas_call | solution.py:276
  20.0 0.5 %collective-permute-start.8 = (bf16[2,16,8,256]{3,2,1,0:T(8,128)(2,1)S(1)}, bf16[2,16,8,256]{3,2,1,0:T(8,128)(2,1)S(1)}, u32[]{:S(2)}, u32[]{:S(2)}) collective-permute-start(bf16[2,16,8,256]{3,2,1,0:T(8,128)(2,1)S(1)} %get-tuple-element.16), channel_id=1, source_target_pairs={{0,1},{1,0},{2,3},{3,2},{4,5},{5,4},{6,7},{7,6},{8,9},{9,8},{10,11... | collective-permute-start | bytes 393224 | tf_op jit(solution)/shard_map/ppermute | solution.py:395
  20.5 0.8 %collective-permute-done.5.refs_3_ = bf16[2,16,8,256]{3,2,1,0:T(8,128)(2,1)S(1)} collective-permute-done((bf16[2,16,8,256]{3,2,1,0:T(8,128)(2,1)S(1)}, bf16[2,16,8,256]{3,2,1,0:T(8,128)(2,1)S(1)}, u32[]{:S(2)}, u32[]{:S(2)}) %collective-permute-start.5) | collective-permute-done | bytes 131104 | tf_op jit(solution)/shard_map/ppermute | solution.py:395
  21.3 1.7 %collective-permute-start.6 = (bf16[2,16,8,256]{3,2,1,0:T(8,128)(2,1)S(1)}, bf16[2,16,8,256]{3,2,1,0:T(8,128)(2,1)S(1)}, u32[]{:S(2)}, u32[]{:S(2)}) collective-permute-start(bf16[2,16,8,256]{3,2,1,0:T(8,128)(2,1)S(1)} %shard_map.57), channel_id=1, source_target_pairs={{0,12},{1,5},{2,4},{3,13},{4,8},{5,1},{6,0},{7,9},{8,14},{9,7},{10... | collective-permute-start | bytes 393224 | tf_op jit(solution)/shard_map/ppermute | solution.py:415
  23.1 0.7 %collective-permute-start.9 = (bf16[16,8,256]{2,1,0:T(8,128)(2,1)S(1)}, bf16[16,8,256]{2,1,0:T(8,128)(2,1)S(1)}, u32[]{:S(2)}, u32[]{:S(2)}) collective-permute-start(bf16[16,8,256]{2,1,0:T(8,128)(2,1)S(1)} %get-tuple-element.17), channel_id=1, source_target_pairs={{0,0},{1,9},{2,8},{3,1},{4,4},{5,13},{6,12},{7,5},{8,2},{9,11},{10... | collective-permute-start | bytes 196616 | tf_op jit(solution)/shard_map/ppermute | solution.py:415
  23.8 3.1 %collective-permute-start.10 = (bf16[16,8,256]{2,1,0:T(8,128)(2,1)S(1)}, bf16[16,8,256]{2,1,0:T(8,128)(2,1)S(1)}, u32[]{:S(2)}, u32[]{:S(2)}) collective-permute-start(bf16[16,8,256]{2,1,0:T(8,128)(2,1)S(1)} %get-tuple-element.18), channel_id=1, source_target_pairs={{0,1},{1,8},{2,9},{3,0},{4,5},{5,12},{6,13},{7,4},{8,3},{9,10},{10... | collective-permute-start | bytes 196616 | tf_op jit(solution)/shard_map/ppermute | solution.py:415
  27.3 0.8 %collective-permute-start.7 = (bf16[16,8,256]{2,1,0:T(8,128)(2,1)S(1)}, bf16[16,8,256]{2,1,0:T(8,128)(2,1)S(1)}, u32[]{:S(2)}, u32[]{:S(2)}) collective-permute-start(bf16[16,8,256]{2,1,0:T(8,128)(2,1)S(1)} %get-tuple-element.15), channel_id=1, source_target_pairs={{0,1},{1,0},{2,3},{3,2},{4,5},{5,4},{6,7},{7,6},{8,9},{9,8},{10,11... | collective-permute-start | bytes 196616 | tf_op jit(solution)/shard_map/ppermute | solution.py:395
  28.1 0.7 %collective-permute-done.10 = bf16[16,8,256]{2,1,0:T(8,128)(2,1)S(1)} collective-permute-done((bf16[16,8,256]{2,1,0:T(8,128)(2,1)S(1)}, bf16[16,8,256]{2,1,0:T(8,128)(2,1)S(1)}, u32[]{:S(2)}, u32[]{:S(2)}) %collective-permute-start.10) | collective-permute-done | bytes 65568 | tf_op jit(solution)/shard_map/ppermute | solution.py:415
  29.0 0.7 %add_multiply_fusion = f32[16,8,256]{2,1,0:T(8,128)} fusion(bf16[16,8,256]{2,1,0:T(8,128)(2,1)S(1)} %collective-permute-done.10, bf16[16,8,256]{2,1,0:T(8,128)(2,1)S(1)} %collective-permute-done.9, bf16[16,8,256]{2,1,0:T(8,128)(2,1)S(1)} %collective-permute-done.7, bf16[16,8,256]{2,1,0:T(8,128)(2,1)S(1)} %get-tuple-element.14), kind=kLoop, calls=%fused_computation | loop fusion | flops 262144 | bytes 393216 | tf_op jit(solution)/shard_map/mul | solution.py:459
  (21 shorter events, 1.5 us)
Async XLA Ops:
  0.0 6.2 %copy-start = (f32[16,32,1024]{2,1,0:T(8,128)S(1)}, f32[16,32,1024]{2,1,0:T(8,128)}, u32[]{:S(2)}) copy-start(f32[16,32,1024]{2,1,0:T(8,128)} %param.4) | copy-start | bytes 6291460
  0.0 6.2 %copy-start.1 = (f32[32,16,1024]{2,1,0:T(8,128)S(1)}, f32[32,16,1024]{2,1,0:T(8,128)}, u32[]{:S(2)}) copy-start(f32[32,16,1024]{2,1,0:T(8,128)} %param.5) | copy-start | bytes 6291460
  0.0 6.2 %copy-start.2 = (bf16[512,256]{1,0:T(8,128)(2,1)S(1)}, bf16[512,256]{1,0:T(8,128)(2,1)}, u32[]{:S(2)}) copy-start(bf16[512,256]{1,0:T(8,128)(2,1)} %constant.51.clone.low_ref) | copy-start | bytes 786436
  0.0 6.2 %copy-start.3 = (bf16[512,256]{1,0:T(8,128)(2,1)S(1)}, bf16[512,256]{1,0:T(8,128)(2,1)}, u32[]{:S(2)}) copy-start(bf16[512,256]{1,0:T(8,128)(2,1)} %constant.50.clone.high_ref) | copy-start | bytes 786436
  2.1 10.5 %collective-permute-start.1 = (bf16[256,256]{1,0:T(8,128)(2,1)S(1)}, bf16[256,256]{1,0:T(8,128)(2,1)S(1)}, u32[]{:S(2)}, u32[]{:S(2)}) collective-permute-start(bf16[256,256]{1,0:T(8,128)(2,1)S(1)} %shard_map.46.refs_0_), channel_id=1, source_target_pairs={{0,16},{8,0},{16,24},{24,8},{1,17},{9,1},{17,25},{25,9},{2,18},{10... | collective-permute-start | bytes 393224 | tf_op jit(solution)/shard_map/ppermute | solution.py:403
  6.9 6.3 %collective-permute-start = (bf16[256,256]{1,0:T(8,128)(2,1)S(1)}, bf16[256,256]{1,0:T(8,128)(2,1)S(1)}, u32[]{:S(2)}, u32[]{:S(2)}) collective-permute-start(bf16[256,256]{1,0:T(8,128)(2,1)S(1)} %shard_map.47.refs_0_.refs_1_), channel_id=1, source_target_pairs={{0,16},{8,0},{16,24},{24,8},{1,17},{9,1},{17,25},{25,9},{2,18},{10... | collective-permute-start | bytes 393224 | tf_op jit(solution)/shard_map/ppermute | solution.py:403
  9.1 8.0 %collective-permute-start.4 = (bf16[256,256]{1,0:T(8,128)(2,1)S(1)}, bf16[256,256]{1,0:T(8,128)(2,1)S(1)}, u32[]{:S(2)}, u32[]{:S(2)}) collective-permute-start(bf16[256,256]{1,0:T(8,128)(2,1)S(1)} %shard_map.48.refs_0_.refs_2_.refs_1_), channel_id=1, source_target_pairs={{0,8},{8,24},{16,0},{24,16},{1,9},{9,25},{17,1},{25,17},{2,10},{10... | collective-permute-start | bytes 393224 | tf_op jit(solution)/shard_map/ppermute | solution.py:403
  10.0 8.5 %collective-permute-start.3 = (bf16[128,256]{1,0:T(8,128)(2,1)S(1)}, bf16[128,256]{1,0:T(8,128)(2,1)S(1)}, u32[]{:S(2)}, u32[]{:S(2)}) collective-permute-start(bf16[128,256]{1,0:T(8,128)(2,1)S(1)} %shard_map.49.refs_0_.refs_3_.refs_1_), channel_id=1, source_target_pairs={{0,8},{8,24},{16,0},{24,16},{1,9},{9,25},{17,1},{25,17},{2,10},{10... | collective-permute-start | bytes 196616 | tf_op jit(solution)/shard_map/ppermute | solution.py:403
  10.9 8.4 %collective-permute-start.2 = (bf16[128,256]{1,0:T(8,128)(2,1)S(1)}, bf16[128,256]{1,0:T(8,128)(2,1)S(1)}, u32[]{:S(2)}, u32[]{:S(2)}) collective-permute-start(bf16[128,256]{1,0:T(8,128)(2,1)S(1)} %shard_map.50.refs_2_.refs_4_.refs_3_), channel_id=1, source_target_pairs={{0,8},{8,24},{16,0},{24,16},{1,9},{9,25},{17,1},{25,17},{2,10},{10... | collective-permute-start | bytes 196616 | tf_op jit(solution)/shard_map/ppermute | solution.py:403
  19.9 1.4 %collective-permute-start.5 = (bf16[2,16,8,256]{3,2,1,0:T(8,128)(2,1)S(1)}, bf16[2,16,8,256]{3,2,1,0:T(8,128)(2,1)S(1)}, u32[]{:S(2)}, u32[]{:S(2)}) collective-permute-start(bf16[2,16,8,256]{3,2,1,0:T(8,128)(2,1)S(1)} %get-tuple-element.13), channel_id=1, source_target_pairs={{0,1},{1,0},{2,3},{3,2},{4,5},{5,4},{6,7},{7,6},{8,9},{9,8},{10,11... | collective-permute-start | bytes 393224 | tf_op jit(solution)/shard_map/ppermute | solution.py:395
  20.0 3.1 %collective-permute-start.8 = (bf16[2,16,8,256]{3,2,1,0:T(8,128)(2,1)S(1)}, bf16[2,16,8,256]{3,2,1,0:T(8,128)(2,1)S(1)}, u32[]{:S(2)}, u32[]{:S(2)}) collective-permute-start(bf16[2,16,8,256]{3,2,1,0:T(8,128)(2,1)S(1)} %get-tuple-element.16), channel_id=1, source_target_pairs={{0,1},{1,0},{2,3},{3,2},{4,5},{5,4},{6,7},{7,6},{8,9},{9,8},{10,11... | collective-permute-start | bytes 393224 | tf_op jit(solution)/shard_map/ppermute | solution.py:395
  21.3 5.9 %collective-permute-start.6 = (bf16[2,16,8,256]{3,2,1,0:T(8,128)(2,1)S(1)}, bf16[2,16,8,256]{3,2,1,0:T(8,128)(2,1)S(1)}, u32[]{:S(2)}, u32[]{:S(2)}) collective-permute-start(bf16[2,16,8,256]{3,2,1,0:T(8,128)(2,1)S(1)} %shard_map.57), channel_id=1, source_target_pairs={{0,12},{1,5},{2,4},{3,13},{4,8},{5,1},{6,0},{7,9},{8,14},{9,7},{10... | collective-permute-start | bytes 393224 | tf_op jit(solution)/shard_map/ppermute | solution.py:415
  23.1 4.9 %collective-permute-start.9 = (bf16[16,8,256]{2,1,0:T(8,128)(2,1)S(1)}, bf16[16,8,256]{2,1,0:T(8,128)(2,1)S(1)}, u32[]{:S(2)}, u32[]{:S(2)}) collective-permute-start(bf16[16,8,256]{2,1,0:T(8,128)(2,1)S(1)} %get-tuple-element.17), channel_id=1, source_target_pairs={{0,0},{1,9},{2,8},{3,1},{4,4},{5,13},{6,12},{7,5},{8,2},{9,11},{10... | collective-permute-start | bytes 196616 | tf_op jit(solution)/shard_map/ppermute | solution.py:415
  23.8 4.9 %collective-permute-start.10 = (bf16[16,8,256]{2,1,0:T(8,128)(2,1)S(1)}, bf16[16,8,256]{2,1,0:T(8,128)(2,1)S(1)}, u32[]{:S(2)}, u32[]{:S(2)}) collective-permute-start(bf16[16,8,256]{2,1,0:T(8,128)(2,1)S(1)} %get-tuple-element.18), channel_id=1, source_target_pairs={{0,1},{1,8},{2,9},{3,0},{4,5},{5,12},{6,13},{7,4},{8,3},{9,10},{10... | collective-permute-start | bytes 196616 | tf_op jit(solution)/shard_map/ppermute | solution.py:415
  27.3 1.7 %collective-permute-start.7 = (bf16[16,8,256]{2,1,0:T(8,128)(2,1)S(1)}, bf16[16,8,256]{2,1,0:T(8,128)(2,1)S(1)}, u32[]{:S(2)}, u32[]{:S(2)}) collective-permute-start(bf16[16,8,256]{2,1,0:T(8,128)(2,1)S(1)} %get-tuple-element.15), channel_id=1, source_target_pairs={{0,1},{1,0},{2,3},{3,2},{4,5},{5,4},{6,7},{7,6},{8,9},{9,8},{10,11... | collective-permute-start | bytes 196616 | tf_op jit(solution)/shard_map/ppermute | solution.py:395
